TPU v7x, 32 devices: a whole 2x2x4 slice. The times are simulated.
32 devices in a mesh: rep: 2 (over y), blk: 4 (over z), mpo: 4 (over x, core).
Axes of the slice: x: 2, y: 2, z: 4, core: 2. Of those that a mesh axis runs over, the one named last changes fastest.
Arguments:
- wavefunction: bfloat16 [1024, 4096], P('rep', 'blk'), parts along dimension 0, may hold values from -6 to 6
- left_blocks: bfloat16 [32, 4, 128, 128], P(('rep', 'mpo'), 'blk'), parts along dimension 0, may hold values from -0.125 to 0.125
- right_blocks: bfloat16 [32, 2, 128, 128], P(('rep', 'mpo')), parts along dimension 0, may hold values from -0.5 to 0.5
- site_terms: bfloat16 [32, 16, 16], P(('rep', 'mpo')), parts along dimension 0, may hold values from -1.5 to 1.5
- left_source: int32 [32, 4], P(('rep', 'mpo')), parts along dimension 0, may hold values from 0 to 3
- right_source: int32 [32, 2], P(('rep', 'mpo')), parts along dimension 0, may hold values from 0 to 1
- live_pairs: int32 [8, 2], P('rep'), parts along dimension 0, may hold values 0 or 1
Outputs:
- sigma_vector: bfloat16 [1024, 4096], P(('rep', 'blk'), 'mpo'), parts along dimension 0
There are 2 independent parts, one for each index of `rep`. A program takes and returns all parts, laid end to end along the dimension named above; each array names one. Nothing has to cross between parts.
Inputs may be any that keep to these rules, and one draw needn't show every extreme that they name: left_source[w, a] is the left block of the wavefunction that term w carries into left block a. right_source[w, b] is the right block that term w carries into right block b. `live_pairs`: 1 where the pair of blocks is allowed by the quantum numbers.
All inputs are finite; a program needn't handle non-finite values.
Results may differ from a plain program's by a relative error of at most 0.0057.
Values may be sent and summed in bfloat16 or wider, within the bound.
No kernel may reach another device: no remote copies, remote signals or barrier semaphores. Data moves between devices by JAX's collectives and lax.ppermute only.
A program may use at most 64 MiB of HBM per device.

v0:
```python
import jax
import jax.numpy as jnp
from jax import lax
from jax.sharding import PartitionSpec as P


def carry_left(blocks, sources, pieces):
    picked = jnp.take(blocks, sources, axis=0)
    return jnp.einsum(
        "...aij,...ajc->...aic", pieces, picked, preferred_element_type=jnp.float32
    ).astype(jnp.bfloat16)


def apply_right(received, site_one, source_one, right_one, physical, right_count, block_rows):
    shaped = received.reshape(received.shape[0], physical, right_count, block_rows)
    turned = jnp.einsum(
        "st,itrj->isrj", site_one, shaped, preferred_element_type=jnp.float32
    ).astype(jnp.bfloat16)
    picked = jnp.take(turned, source_one, axis=2)
    return jnp.einsum("isbj,bkj->isbk", picked, right_one, preferred_element_type=jnp.float32)


def on_device(
    wavefunction, left_blocks, right_blocks, site_terms, left_source, right_source, live_pairs
):
    all_rows, columns = wavefunction.shape
    term_count = left_blocks.shape[0]
    own_sectors = left_blocks.shape[1]
    block_rows = left_blocks.shape[2]
    physical = site_terms.shape[1]
    right_count = right_blocks.shape[1]
    own_rows = own_sectors * block_rows
    blocks = wavefunction.reshape(all_rows // block_rows, block_rows, columns)
    accumulated = jnp.zeros((own_rows, physical, right_count, block_rows), jnp.float32)
    for member in range(term_count):
        sources = left_source[member]

        def carry_one(pieces, offset, sources=sources):
            return carry_left(blocks, sources, pieces)

        carried = carry_one(
            lax.all_gather(left_blocks[member], "blk", axis=0, tiled=True), jnp.int32(0)
        )
        received = lax.all_to_all(
            carried.reshape(all_rows, columns), "blk", split_axis=0, concat_axis=1, tiled=True
        )
        accumulated = accumulated + apply_right(
            received,
            site_terms[member],
            right_source[member],
            right_blocks[member],
            physical,
            right_count,
            block_rows,
        )
    position = lax.axis_index("blk")
    live_rows = lax.dynamic_slice_in_dim(live_pairs, position * own_sectors, own_sectors, 0)
    row_mask = jnp.repeat(live_rows.astype(jnp.float32), block_rows, axis=0)
    accumulated = accumulated * row_mask[:, None, :, None]
    flattened = accumulated.reshape(own_rows, physical * right_count * block_rows)
    summed = lax.psum_scatter(flattened, "mpo", scatter_dimension=1, tiled=True)
    return summed.astype(jnp.bfloat16)


def solution(mesh):
    return jax.shard_map(
        on_device,
        mesh=mesh,
        in_specs=(
            P("rep", "blk"),
            P(("rep", "mpo"), "blk", None, None),
            P(("rep", "mpo"), None, None, None),
            P(("rep", "mpo"), None, None),
            P(("rep", "mpo"), None),
            P(("rep", "mpo"), None),
            P("rep", None),
        ),
        out_specs=P(("rep", "blk"), "mpo"),
        check_vma=False,
    )
```

profile of v0, /device:TPU:0, one launch (start us, length us, event | category | flops | bytes accessed | tf_op | source)
XLA Modules:
  0.0 224.4 jit_solution(6710559288287700722)
XLA Ops:
  6.5 0.0 copy-start
  6.5 0.8 compare_and_fusion.1
  7.4 0.8 fusion.51
  8.2 15.1 %all-gather.2 = bf16[4,1,128,128]{3,2,1,0:T(8,128)(2,1)S(1)} all-gather(bf16[1,1,128,128]{3,2,1,0:T(8,128)(2,1)S(1)} %get-tuple-element.22), channel_id=4, replica_groups=mesh['rep'=2,'blk'=4,'mpo'=4] {'blk'}, dimensions={0}, use_global_device_ids=true | all-gather | bytes 163840 | tf_op jit(solution)/shard_map/all_gather | solution.py:42
  23.3 0.0 copy-done
  23.3 0.6 gather_fusion.4
  23.9 1.6 fusion.2
  25.5 5.0 %all-to-all-start.2 = ((bf16[4,128,1024]{1,2,0:T(8,128)(2,1)}), bf16[4,128,1024]{1,2,0:T(8,128)(2,1)S(1)}, u32[]{:S(2)}, u32[]{:S(2)}) async-start(bf16[4,128,1024]{1,2,0:T(8,128)(2,1)} %fusion.2), calls=%async_computation.2 | async-start | bytes 2097152 | tf_op jit(solution)/shard_map/all_to_all | solution.py:44
  30.5 0.6 gather_fusion
  31.1 28.3 %all-gather = bf16[4,1,128,128]{3,2,1,0:T(8,128)(2,1)S(1)} all-gather(bf16[1,1,128,128]{3,2,1,0:T(8,128)(2,1)S(1)} %get-tuple-element.21), channel_id=2, replica_groups=mesh['rep'=2,'blk'=4,'mpo'=4] {'blk'}, dimensions={0}, use_global_device_ids=true | all-gather | bytes 163840 | tf_op jit(solution)/shard_map/all_gather | solution.py:42
  59.5 1.6 fusion
  61.1 0.0 all-to-all-done.2
  61.1 4.3 %all-to-all-start = ((bf16[4,128,1024]{1,2,0:T(8,128)(2,1)}), bf16[4,128,1024]{1,2,0:T(8,128)(2,1)}, u32[]{:S(2)}, u32[]{:S(2)}) async-start(bf16[4,128,1024]{1,2,0:T(8,128)(2,1)} %fusion), calls=%async_computation | async-start | bytes 2097152 | tf_op jit(solution)/shard_map/all_to_all | solution.py:44
  65.3 0.6 gather_fusion.2
  66.0 28.8 %all-gather.1 = bf16[4,1,128,128]{3,2,1,0:T(8,128)(2,1)S(1)} all-gather(bf16[1,1,128,128]{3,2,1,0:T(8,128)(2,1)S(1)} %get-tuple-element.20), channel_id=3, replica_groups=mesh['rep'=2,'blk'=4,'mpo'=4] {'blk'}, dimensions={0}, use_global_device_ids=true | all-gather | bytes 163840 | tf_op jit(solution)/shard_map/all_gather | solution.py:42
  94.7 1.6 fusion.1
  96.3 0.0 copy-start.9
  96.3 0.0 copy-start.8
  96.3 0.0 all-to-all-done
  96.3 4.4 %all-to-all-start.1 = ((bf16[4,128,1024]{1,2,0:T(8,128)(2,1)}), bf16[4,128,1024]{1,2,0:T(8,128)(2,1)}, u32[]{:S(2)}, u32[]{:S(2)}) async-start(bf16[4,128,1024]{1,2,0:T(8,128)(2,1)} %fusion.1), calls=%async_computation.1 | async-start | bytes 2097152 | tf_op jit(solution)/shard_map/all_to_all | solution.py:44
  100.7 0.6 gather_fusion.6
  101.4 0.0 copy-done.9
  101.4 0.2 convert_reduce_fusion
  101.6 28.6 %all-gather.3 = bf16[4,1,128,128]{3,2,1,0:T(8,128)(2,1)S(1)} all-gather(bf16[1,1,128,128]{3,2,1,0:T(8,128)(2,1)S(1)} %get-tuple-element.19), channel_id=5, replica_groups=mesh['rep'=2,'blk'=4,'mpo'=4] {'blk'}, dimensions={0}, use_global_device_ids=true | all-gather | bytes 163840 | tf_op jit(solution)/shard_map/all_gather | solution.py:42
  130.1 0.0 copy-done.8
  130.1 0.2 slice_reduce_fusion
  130.4 1.6 fusion.3
  132.0 0.0 all-to-all-done.1
  132.0 3.9 %all-to-all-start.3 = ((bf16[4,128,1024]{1,2,0:T(8,128)(2,1)}), bf16[4,128,1024]{1,2,0:T(8,128)(2,1)S(1)}, u32[]{:S(2)}, u32[]{:S(2)}) async-start(bf16[4,128,1024]{1,2,0:T(8,128)(2,1)} %fusion.3), calls=%async_computation.3 | async-start | bytes 2097152 | tf_op jit(solution)/shard_map/all_to_all | solution.py:44
  135.9 0.0 reduce-scatter.2.cloned.1.call-start
  135.9 1.7 copy.33
  137.7 2.7 %copy.27 = bf16[128,16,2,128]{3,1,2,0:T(8,128)(2,1)} copy(bf16[128,16,2,128]{0,3,2,1:T(8,128)(2,1)} %bitcast.5) | data formatting | bytes 2097152 | tf_op jit(solution)/shard_map/reshape | solution.py:15
  140.4 2.7 %copy.30 = bf16[128,16,2,128]{3,1,2,0:T(8,128)(2,1)} copy(bf16[128,16,2,128]{0,3,2,1:T(8,128)(2,1)} %bitcast.18) | data formatting | bytes 2097152 | tf_op jit(solution)/shard_map/reshape | solution.py:15
  143.1 0.0 copy-done.3
  143.1 0.0 copy-done.7
  143.1 0.0 copy-start.5
  143.1 1.4 fusion.6
  144.5 0.0 copy-done.4
  144.5 1.4 fusion.4
  145.9 0.0 copy-done.5
  145.9 0.4 fusion.5
  146.3 12.6 %all-to-all-done.3 = bf16[4,128,1024]{1,2,0:T(8,128)(2,1)S(1)} async-done(((bf16[4,128,1024]{1,2,0:T(8,128)(2,1)}), bf16[4,128,1024]{1,2,0:T(8,128)(2,1)S(1)}, u32[]{:S(2)}, u32[]{:S(2)}) %all-to-all-start.3) | async-done | bytes 1048608 | tf_op jit(solution)/shard_map/all_to_all | solution.py:44
  158.9 1.7 copy.36
  160.6 2.6 %fusion.7 = bf16[128,16,2,128]{3,1,2,0:T(8,128)(2,1)} fusion(bf16[128,16,2,128]{3,1,2,0:T(8,128)(2,1)} %copy.36, bf16[4,16,16]{2,1,0:T(8,128)(2,1)S(1)} %copy-done.7), kind=kOutput, calls=%fused_computation.24 | convolution fusion | flops 17301504 | bytes 2101248 | tf_op jit(solution)/shard_map/st,itrj->isrj/dot_general | solution.py:16
  163.2 2.0 gather_fusion.1
  165.2 1.1 select_bitcast_fusion.3
  166.3 0.7 gather_fusion.3
  167.1 0.2 select_bitcast_fusion.2
  167.3 0.0 copy-done.6
  167.3 0.4 fusion.11
  167.7 0.8 copy-done.2
  168.5 1.8 fusion.13
  170.3 2.9 %gather_fusion.5 = bf16[2,128,16,128]{3,2,1,0:T(8,128)(2,1)} fusion(bf16[128,16,2,128]{3,1,2,0:T(8,128)(2,1)} %fusion.6, s32[1024]{0:T(1024)S(1)} %pad_clamp_fusion.2), kind=kCustom, calls=%fused_computation.6.clone | custom fusion | bytes 2097160 | tf_op jit(solution)/shard_map/jit(_take)/gather | solution.py:19
  173.2 1.4 select_bitcast_fusion.1
  174.6 1.8 fusion.9
  176.3 2.9 %gather_fusion.7 = bf16[2,128,16,128]{3,2,1,0:T(8,128)(2,1)} fusion(bf16[128,16,2,128]{3,1,2,0:T(8,128)(2,1)} %fusion.7, s32[1024]{0:T(1024)S(1)} %pad_clamp_fusion), kind=kCustom, calls=%fused_computation.7.clone | custom fusion | bytes 2097160 | tf_op jit(solution)/shard_map/jit(_take)/gather | solution.py:19
  179.2 1.5 select_bitcast_fusion
  180.8 0.4 copy-done.1
  181.1 2.2 %multiply_bitcast_fusion = f32[128,16,2,128]{0,3,1,2:T(8,128)S(1)} fusion(f32[2,128,16,128]{1,3,2,0:T(8,128)} %fusion.9, f32[2,128,16,128]{1,3,2,0:T(8,128)S(1)} %copy-done.1, f32[2,128,16,128]{1,3,2,0:T(8,128)S(1)} %fusion.11, bf16[128,16,2,128]{3,1,0,2:T(8,128)(2,1)S(1)} %select_bitcast_fusion, f32[2]{0:T(128)S(1)} %convert_reduce_fusion, ...), kind=kOutput, calls=%fused_computation.8 | convolution fusion | flops 136314880 | bytes 9503232 | tf_op jit(solution)/shard_map/isbj,bkj->isbk/dot_general | solution.py:20
  183.4 1.5 copy.38
  184.9 0.0 reduce-scatter.2.cloned.1.call-update
  184.9 30.7 %reduce-scatter.2.cloned.1.call-done = f32[128,1024]{0,1:T(8,128)} async-done(((f32[128,4096]{0,1:T(8,128)}), f32[128,1024]{0,1:T(8,128)}) %reduce-scatter.2.cloned.1.call-update) | async-done | bytes 524304 | tf_op jit(solution)/shard_map/reduce_scatter | solution.py:61
  215.6 1.1 convert_element_type.74
  216.7 0.9 copy.39
  (20 shorter events, 0.1 us)
Async XLA Ops:
  6.5 16.7 %copy-start = (bf16[512,1024]{1,0:T(8,128)(2,1)S(1)}, bf16[512,1024]{1,0:T(8,128)(2,1)}, u32[]{:S(2)}) copy-start(bf16[512,1024]{1,0:T(8,128)(2,1)} %param.11) | copy-start | bytes 3145732
  25.5 35.5 %all-to-all-start.2 = ((bf16[4,128,1024]{1,2,0:T(8,128)(2,1)}), bf16[4,128,1024]{1,2,0:T(8,128)(2,1)S(1)}, u32[]{:S(2)}, u32[]{:S(2)}) async-start(bf16[4,128,1024]{1,2,0:T(8,128)(2,1)} %fusion.2), calls=%async_computation.2 | async-start | bytes 2097152 | tf_op jit(solution)/shard_map/all_to_all | solution.py:44
  61.1 35.3 %all-to-all-start = ((bf16[4,128,1024]{1,2,0:T(8,128)(2,1)}), bf16[4,128,1024]{1,2,0:T(8,128)(2,1)}, u32[]{:S(2)}, u32[]{:S(2)}) async-start(bf16[4,128,1024]{1,2,0:T(8,128)(2,1)} %fusion), calls=%async_computation | async-start | bytes 2097152 | tf_op jit(solution)/shard_map/all_to_all | solution.py:44
  96.3 5.0 %copy-start.9 = (s32[4,2]{0,1:T(2,128)S(1)}, s32[4,2]{0,1:T(2,128)}, u32[]{:S(2)}) copy-start(s32[4,2]{0,1:T(2,128)} %param.17) | copy-start | bytes 100
  96.3 33.8 %copy-start.8 = (s32[4,2]{0,1:T(2,128)S(1)}, s32[4,2]{0,1:T(2,128)}, u32[]{:S(2)}) copy-start(s32[4,2]{0,1:T(2,128)} %param.16) | copy-start | bytes 100
  96.3 35.7 %all-to-all-start.1 = ((bf16[4,128,1024]{1,2,0:T(8,128)(2,1)}), bf16[4,128,1024]{1,2,0:T(8,128)(2,1)}, u32[]{:S(2)}, u32[]{:S(2)}) async-start(bf16[4,128,1024]{1,2,0:T(8,128)(2,1)} %fusion.1), calls=%async_computation.1 | async-start | bytes 2097152 | tf_op jit(solution)/shard_map/all_to_all | solution.py:44
  132.0 26.9 %all-to-all-start.3 = ((bf16[4,128,1024]{1,2,0:T(8,128)(2,1)}), bf16[4,128,1024]{1,2,0:T(8,128)(2,1)S(1)}, u32[]{:S(2)}, u32[]{:S(2)}) async-start(bf16[4,128,1024]{1,2,0:T(8,128)(2,1)} %fusion.3), calls=%async_computation.3 | async-start | bytes 2097152 | tf_op jit(solution)/shard_map/all_to_all | solution.py:44
  135.9 79.7 %reduce-scatter.2.cloned.1.call-start = ((), (), s32[]{:S(2)}) async-start(), calls=%async_computation.5 | async-start | bytes 2621440 | tf_op jit(solution)/shard_map/reduce_scatter | solution.py:61
  137.7 5.4 %copy-start.3 = (bf16[128,16,2,128]{3,1,2,0:T(8,128)(2,1)S(1)}, bf16[128,16,2,128]{3,1,2,0:T(8,128)(2,1)}, u32[]{:S(2)}) copy-start(bf16[128,16,2,128]{3,1,2,0:T(8,128)(2,1)} %copy.33) | copy-start | bytes 3145732
  137.7 5.4 %copy-start.7 = (bf16[4,16,16]{2,1,0:T(8,128)(2,1)S(1)}, bf16[4,16,16]{2,1,0:T(8,128)(2,1)}, u32[]{:S(2)}) copy-start(bf16[4,16,16]{2,1,0:T(8,128)(2,1)} %param.14) | copy-start | bytes 6148
  143.1 1.4 copy-start.4
  143.1 2.8 %copy-start.5 = (bf16[128,16,2,128]{3,1,2,0:T(8,128)(2,1)S(1)}, bf16[128,16,2,128]{3,1,2,0:T(8,128)(2,1)}, u32[]{:S(2)}) copy-start(bf16[128,16,2,128]{3,1,2,0:T(8,128)(2,1)} %copy.30) | copy-start | bytes 3145732
  166.3 0.9 copy-start.6
  167.3 1.2 copy-start.2
  179.2 1.9 copy-start.1
Sparse Core Ops, SparseCore 0:
  185.0 30.5 reduce-scatter.1
where the time goes:
time: 225 us; the launch traced here: 224 us
  blocking collectives  101 us (45%)
  waiting for transfers between devices  43.3 us (19%)
  local copies, waits for them, and re-layouts  24.4 us (11%)
  matrix products  18.4 us (8%)
  starting transfers between devices  17.5 us (8%)
  between operations  13.6 us (6%)
  other arithmetic  6.41 us (3%)
    all_gather x4, blocking collectives, on_device(): lax.all_gather(left_blocks[member], 'blk', axis=0, tiled=True)  101 us
    reduce_scatter x1, waiting for transfers between devices, on_device(): summed = lax.psum_scatter(flattened, 'mpo', scatter_dimension=1, tiled=True)  30.7 us
    all_to_all x4, starting transfers between devices, on_device(): lax.all_to_all(carried.reshape(all_rows, columns), 'blk', split_axis=0, c...  17.5 us
    all_to_all x4, waiting for transfers between devices, on_device(): lax.all_to_all(carried.reshape(all_rows, columns), 'blk', split_axis=0, c...  12.6 us
    reshape x4, local copies, waits for them, and re-layouts, apply_right(): received.reshape(received.shape[0], physical, right_count, block_rows)  8.85 us
    gather x4, local copies, waits for them, and re-layouts, apply_right(): picked = jnp.take(turned, source_one, axis=2)  8.51 us
    dot_general x4, matrix products, carry_left(): jnp.einsum('...aij,...ajc->...aic', pieces, picked, preferred_element_typ...  6.39 us
    dot_general x4, matrix products, apply_right(): jnp.einsum('isbj,bkj->isbk', picked, right_one, preferred_element_type=jn...  6.23 us
  transfers between devices with their start and end apart: 5, of which 2 were waited for; matrix products, arithmetic and copies ran while one was open for 8% of the time, Pallas kernels for 0%

commit v1 on v0

v1 whole, which is shorter than its diff:
```python
import functools

import jax
import jax.numpy as jnp
from jax import lax
from jax.experimental import pallas as pl
from jax.experimental.pallas import tpu as pltpu
from jax.sharding import PartitionSpec as P

F32 = jnp.float32
BF16 = jnp.bfloat16
VMEM_BYTES = 32 * 1024 * 1024
NEAR = ((0, 1), (1, 0), (2, 3), (3, 2))
FAR = ((0, 2), (2, 0), (1, 3), (3, 1))
MIDDLE = ((1, 2), (2, 1))
OUTWARD = ((1, 0), (2, 3))
CORE = ((0, 1), (1, 0), (2, 3), (3, 2))
ACROSS = ((0, 2), (2, 0), (1, 3), (3, 1))
SUB = 16


def carry_left(blocks, sources, pieces):
    picked = jnp.take(blocks, sources, axis=0)
    return jnp.einsum(
        "...aij,...ajc->...aic", pieces, picked, preferred_element_type=F32
    ).astype(BF16)


def apply_right(received, site_one, source_one, right_one, physical, right_count, block_rows):
    shaped = received.reshape(received.shape[0], physical, right_count, block_rows)
    turned = jnp.einsum(
        "st,itrj->isrj", site_one, shaped, preferred_element_type=F32
    ).astype(BF16)
    picked = jnp.take(turned, source_one, axis=2)
    return jnp.einsum("isbj,bkj->isbk", picked, right_one, preferred_element_type=F32)


def by_terms(
    wavefunction, left_blocks, right_blocks, site_terms, left_source, right_source, live_pairs
):
    all_rows, columns = wavefunction.shape
    term_count, own_sectors, block_rows = left_blocks.shape[:3]
    physical = site_terms.shape[1]
    right_count = right_blocks.shape[1]
    own_rows = own_sectors * block_rows
    blocks = wavefunction.reshape(all_rows // block_rows, block_rows, columns)
    accumulated = jnp.zeros((own_rows, physical, right_count, block_rows), F32)
    for member in range(term_count):
        pieces = lax.all_gather(left_blocks[member], "blk", axis=0, tiled=True)
        carried = carry_left(blocks, left_source[member], pieces)
        received = lax.all_to_all(
            carried.reshape(all_rows, columns), "blk", split_axis=0, concat_axis=1, tiled=True
        )
        accumulated = accumulated + apply_right(
            received,
            site_terms[member],
            right_source[member],
            right_blocks[member],
            physical,
            right_count,
            block_rows,
        )
    position = lax.axis_index("blk")
    live_rows = lax.dynamic_slice_in_dim(live_pairs, position * own_sectors, own_sectors, 0)
    row_mask = jnp.repeat(live_rows.astype(F32), block_rows, axis=0)
    accumulated = accumulated * row_mask[:, None, :, None]
    flattened = accumulated.reshape(own_rows, physical * right_count * block_rows)
    summed = lax.psum_scatter(flattened, "mpo", scatter_dimension=1, tiled=True)
    return summed.astype(BF16)


def matmul(a, b):
    return jnp.dot(a, b, preferred_element_type=F32)


def pack_body(terms, rights, phys, place_ref, left_ref, right_ref, site_ref, sources_ref, rsource_ref, out_ref):
    block = left_ref.shape[-1]
    base = 0
    for w in range(terms):
        out_ref[base : base + block, :] = left_ref[w, 0]
        base += block
    for w in range(terms):
        for b in range(rights):
            out_ref[base : base + block, :] = right_ref[w, b]
            base += block
    lane = lax.broadcasted_iota(jnp.int32, (phys, block), 1)
    row = lax.broadcasted_iota(jnp.int32, (phys, block), 0)
    site = jnp.zeros((phys, block), F32)
    for w in range(terms):
        spot = jnp.where(lane == row + w * phys, 1.0, 0.0).astype(BF16)
        site = site + matmul(site_ref[w], spot)
    out_ref[base : base + phys, :] = site.astype(BF16)
    base += phys
    lane = lax.broadcasted_iota(jnp.int32, (SUB, block), 1)
    numbers = jnp.zeros((SUB, block), F32)
    for w in range(terms):
        numbers = jnp.where(lane == w, sources_ref[w, place_ref[1]].astype(F32), numbers)
        for b in range(rights):
            numbers = jnp.where(
                lane == terms + w * rights + b, rsource_ref[w, b].astype(F32), numbers
            )
    out_ref[base : base + SUB, :] = numbers.astype(BF16)


def operators(terms, rights, phys, place_ref, index_ref, live_ref, packs, w_ref, kron_ref):
    block = packs[0].shape[-1]
    per_term = 1 + rights
    me, own_blk = place_ref[0], place_ref[1]
    slots = len(packs)
    width = w_ref.shape[-1]
    for k in range(slots):
        for w in range(terms):
            for b in range(rights):
                start = (terms + w * rights + b) * block
                turned = packs[k][start : start + block, :].astype(F32).T.astype(BF16)
                source = index_ref[k, terms + w * rights + b]
                alive = live_ref[own_blk, b]
                for r in range(rights):
                    keep = jnp.logical_and(source == r, alive != 0)
                    w_ref[k * terms + w, r * block : (r + 1) * block, b * block : (b + 1) * block] = (
                        jnp.where(keep, turned, jnp.zeros_like(turned))
                    )
    site_at = per_term * terms * block
    site = jnp.concatenate([p[site_at : site_at + phys, :] for p in packs], axis=1)
    rows, depth = kron_ref.shape[1:]
    quarter = phys // slots
    srow = lax.broadcasted_iota(jnp.int32, (rows, phys), 0) // SUB
    owner = jnp.where(srow < quarter, lax.bitwise_xor(me, 2), me)
    swant = owner * quarter + lax.rem(srow, quarter)
    pick_s = jnp.where(
        lax.broadcasted_iota(jnp.int32, (rows, phys), 1) == swant, 1.0, 0.0
    ).astype(BF16)
    here = slots * block
    source_row = lax.broadcasted_iota(jnp.int32, (here, depth), 0)
    column = lax.broadcasted_iota(jnp.int32, (here, depth), 1)
    want_term = column // (2 * SUB)
    which = lax.rem(column // SUB, 2)
    diagonal = lax.rem(lax.broadcasted_iota(jnp.int32, (rows, depth), 0), SUB) == lax.rem(
        lax.broadcasted_iota(jnp.int32, (rows, depth), 1), SUB
    )
    per_blk = slots
    for q in range(slots):
        state = lax.bitwise_xor(own_blk, q) * per_blk + lax.bitwise_xor(me, which)
        want = (want_term // terms) * block + lax.rem(want_term, terms) * phys + state
        pick_t = jnp.where(source_row == want, 1.0, 0.0).astype(BF16)
        spread = matmul(pick_s, matmul(site, pick_t).astype(BF16))
        kron_ref[q] = jnp.where(diagonal, spread, 0.0).astype(BF16)


def add_shard(terms, index_ref, packs, w_ref, kron, halves, y_ref):
    block = packs[0].shape[-1]
    tiles = y_ref.shape[0]
    for k in range(len(packs)):
        for w in range(terms):
            row = pl.multiple_of(index_ref[k, w] * block, block)
            left = packs[k][w * block : (w + 1) * block, :]
            carried = jnp.concatenate(
                [matmul(left, h[pl.ds(row, block), :]).astype(BF16) for h in halves], axis=0
            )
            y = matmul(carried, w_ref[k * terms + w]).astype(BF16)
            at = (k * terms + w) * 2 * SUB
            for t in range(2):
                y_ref[:, at + t * SUB : at + (t + 1) * SUB, :] = y[
                    t * block : (t + 1) * block, :
                ].reshape(tiles, SUB, y.shape[-1])
    return [matmul(kron, y_ref[i]) for i in range(tiles)]


def own_body(terms, rights, phys, place_ref, index_ref, live_ref, *refs):
    packs, (mine, other), (w_ref, kron_ref, acc_ref), (y_ref,) = (
        refs[:4], refs[4:6], refs[6:9], refs[9:])
    operators(terms, rights, phys, place_ref, index_ref, live_ref, packs, w_ref, kron_ref)
    sums = add_shard(terms, index_ref, packs, w_ref, kron_ref[0], (mine, other), y_ref)
    for i, s in enumerate(sums):
        acc_ref[i] = s


def middle_body(terms, index_ref, *refs):
    packs, w_ref, kron_ref, acc_in, near, far = refs[:4], refs[4], refs[5], refs[6], refs[7:9], refs[9:11]
    acc_ref, y_ref = refs[11], refs[12]
    for q, halves in ((1, near), (2, far)):
        sums = add_shard(terms, index_ref, packs, w_ref, kron_ref[q], halves, y_ref)
        for i, s in enumerate(sums):
            acc_ref[i] = s + (acc_in[i] if q == 1 else acc_ref[i])


def last_body(terms, place_ref, index_ref, *refs):
    packs, w_ref, kron_ref, acc_in = refs[:4], refs[4], refs[5], refs[6]
    inner, outer = refs[7:9], refs[9:11]
    give_ref, keep_ref, y_ref, half_ref = refs[11:]
    at_end = jnp.logical_or(place_ref[1] == 0, place_ref[1] == 3)
    for h in range(2):
        half_ref[h] = jnp.where(at_end, outer[h][...], inner[h][...])
    sums = add_shard(
        terms, index_ref, packs, w_ref, kron_ref[3], (half_ref.at[0], half_ref.at[1]), y_ref
    )
    width = w_ref.shape[-1]
    for i, s in enumerate(sums):
        total = s + acc_in[i]
        count = total.shape[0] // SUB // 2
        for n in range(count):
            rows, cols = slice(i * SUB, (i + 1) * SUB), slice(n * width, (n + 1) * width)
            give_ref[rows, cols] = total[n * SUB : (n + 1) * SUB, :].astype(BF16)
            keep_ref[rows, cols] = total[(count + n) * SUB : (count + n + 1) * SUB, :]


def call(body, out_shape, in_specs, scratch=(), flops=0, nbytes=0, name=None):
    return pl.pallas_call(
        body,
        out_shape=out_shape,
        in_specs=in_specs,
        scratch_shapes=scratch,
        compiler_params=pltpu.CompilerParams(vmem_limit_bytes=VMEM_BYTES),
        cost_estimate=pl.CostEstimate(flops=flops, bytes_accessed=nbytes, transcendentals=0),
        name=name,
    )


def by_states(
    wavefunction, left_blocks, right_blocks, site_terms, left_source, right_source, live_pairs
):
    all_rows, columns = wavefunction.shape
    terms, _, block, _ = left_blocks.shape
    rights = right_blocks.shape[1]
    phys = site_terms.shape[1]
    width = rights * block
    slots = 4
    depth = slots * terms * 2 * SUB
    rows = phys // 2 * SUB
    tiles = block // SUB
    me, own_blk = lax.axis_index("mpo"), lax.axis_index("blk")
    place = jnp.stack([me, own_blk]).astype(jnp.int32)
    smem = pl.BlockSpec(memory_space=pltpu.SMEM)
    vmem = pl.BlockSpec(memory_space=pltpu.VMEM)

    mine = lax.dynamic_slice_in_dim(wavefunction, me * width, width, 1)
    far = lax.ppermute(mine, "blk", FAR)
    near = lax.ppermute(mine, "blk", NEAR)
    inner = lax.ppermute(mine, "blk", MIDDLE)
    outer = lax.ppermute(far, "blk", OUTWARD)

    pack_rows = terms * (1 + rights) * block + phys + SUB
    pack = call(
        functools.partial(pack_body, terms, rights, phys),
        jax.ShapeDtypeStruct((pack_rows, block), BF16),
        [smem, vmem, vmem, vmem, smem, smem],
        name="pack_operators",
    )(place, left_blocks, right_blocks, site_terms, left_source, right_source)
    pack_x = lax.ppermute(pack, "mpo", ACROSS)
    pack_c = lax.ppermute(pack, "mpo", CORE)
    pack_xc = lax.ppermute(pack_x, "mpo", CORE)
    packs = (pack, pack_x, pack_c, pack_xc)
    numbers = terms * (1 + rights)
    index = jnp.stack([p[pack_rows - SUB, :numbers] for p in packs]).astype(jnp.int32)

    def swap(x):
        return lax.ppermute(x, "mpo", CORE)

    other = lax.dynamic_slice_in_dim(wavefunction, lax.bitwise_xor(me, 1) * width, width, 1)
    shard_flops = 2 * slots * terms * (2 * block * width * (block + width)) + 2 * tiles * rows * depth * width
    y_scratch = pltpu.VMEM((tiles, depth, width), BF16)
    acc_shape = jax.ShapeDtypeStruct((tiles, rows, width), F32)
    w_all, kron, acc = call(
        functools.partial(own_body, terms, rights, phys),
        (
            jax.ShapeDtypeStruct((slots * terms, width, width), BF16),
            jax.ShapeDtypeStruct((slots, rows, depth), BF16),
            acc_shape,
        ),
        [smem, smem, smem] + [vmem] * 6,
        [y_scratch],
        flops=shard_flops,
        nbytes=8 << 20,
        name="own_shard",
    )(place, index, live_pairs, *packs, mine, other)
    acc = call(
        functools.partial(middle_body, terms),
        acc_shape,
        [smem] + [vmem] * 11,
        [y_scratch],
        flops=2 * shard_flops,
        nbytes=8 << 20,
        name="middle_shards",
    )(index, *packs, w_all, kron, acc, near, swap(near), far, swap(far))
    give, keep = call(
        functools.partial(last_body, terms),
        (
            jax.ShapeDtypeStruct((block, phys // slots * width), BF16),
            jax.ShapeDtypeStruct((block, phys // slots * width), F32),
        ),
        [smem, smem] + [vmem] * 11,
        [y_scratch, pltpu.VMEM((2, all_rows, width), BF16)],
        flops=shard_flops,
        nbytes=8 << 20,
        name="last_shard",
    )(place, index, *packs, w_all, kron, acc, inner, swap(inner), outer, swap(outer))
    taken = lax.ppermute(give, "mpo", ACROSS)
    return (keep + taken.astype(F32)).astype(BF16)


def solution(mesh):
    sizes = dict(mesh.shape)

    def on_device(
        wavefunction, left_blocks, right_blocks, site_terms, left_source, right_source, live_pairs
    ):
        columns = wavefunction.shape[1]
        terms, sectors, block, _ = left_blocks.shape
        phys, rights = site_terms.shape[1], right_blocks.shape[1]
        square = sizes["blk"] == 4 and sizes["mpo"] == 4 and sectors == 1 and rights == 2
        fits = columns == 4 * rights * block and phys == 16 and block == 128 and terms == 4
        step = by_states if square and fits else by_terms
        return step(
            wavefunction, left_blocks, right_blocks, site_terms, left_source, right_source, live_pairs
        )

    return jax.shard_map(
        on_device,
        mesh=mesh,
        in_specs=(
            P("rep", "blk"),
            P(("rep", "mpo"), "blk", None, None),
            P(("rep", "mpo"), None, None, None),
            P(("rep", "mpo"), None, None),
            P(("rep", "mpo"), None),
            P(("rep", "mpo"), None),
            P("rep", None),
        ),
        out_specs=P(("rep", "blk"), "mpo"),
        check_vma=False,
    )
```

time: 225 us -> 54.5 us (0.24)
  blocking collectives: 101 us -> 0 us
  local copies, waits for them, and re-layouts: 24.4 us -> 5.85 us
  matrix products: 18.4 us -> 0 us
  waiting for transfers between devices: 43.3 us -> 25.9 us
  between operations: 13.6 us -> 0.09 us
  Pallas kernels: 0 us -> 10.8 us
  starting transfers between devices: 17.5 us -> 10.6 us
  other arithmetic: 6.41 us -> 0.85 us
    all_gather x4 -> x0, blocking collectives: 101 us -> none  [on_device(): lax.all_gather(left_blocks[member], 'blk', axis=0, tiled=True)]
    reduce_scatter x1 -> x0, waiting for transfers between devices: 30.7 us -> none  [on_device(): summed = lax.psum_scatter(flattened, 'mpo', scatter_dimension=1, tiled=True)]
    ppermute x0 -> x12, waiting for transfers between devices: none -> 25.9 us  [the longest x1 8.18 us: by_states(): taken = lax.ppermute(give, 'mpo', ACROSS)]
    dot_general x12 -> x0, matrix products: 18.4 us -> none  [the longest x4 6.39 us: carry_left(): jnp.einsum('...aij,...ajc->...aic', pieces, picked, preferred_element_typ...]
    all_to_all x4 -> x0, starting transfers between devices: 17.5 us -> none  [on_device(): lax.all_to_all(carried.reshape(all_rows, columns), 'blk', split_axis=0, c...]
    all_to_all x4 -> x0, waiting for transfers between devices: 12.6 us -> none  [on_device(): lax.all_to_all(carried.reshape(all_rows, columns), 'blk', split_axis=0, c...]
    gather x8 -> x0, local copies, waits for them, and re-layouts: 11 us -> none  [the longest x4 8.51 us: apply_right(): picked = jnp.take(turned, source_one, axis=2)]
    pallas_call x0 -> x4, Pallas kernels: none -> 10.8 us  [the longest x1 4.43 us: by_states(): call(functools.partial(middle_body, terms), acc_shape, [smem] + [vmem] *...]
  transfers between devices with their start and end apart: 5 -> 12, of which waited for: 2 -> 5; matrix products, arithmetic and copies ran while one was open for 8% -> 3% of each run, Pallas kernels for 0% -> 14%
where the time goes in v1:
time: 54.5 us; the launch traced here: 54.1 us
  waiting for transfers between devices  25.9 us (48%)
  Pallas kernels  10.8 us (20%)
  starting transfers between devices  10.6 us (19%)
  local copies, waits for them, and re-layouts  5.85 us (11%)
  other arithmetic  0.85 us (2%)
    ppermute x1, waiting for transfers between devices, by_states(): taken = lax.ppermute(give, 'mpo', ACROSS)  8.18 us
    ppermute x1, waiting for transfers between devices, by_states(): pack_x = lax.ppermute(pack, 'mpo', ACROSS)  5.56 us
    unnamed x10, local copies, waits for them, and re-layouts  4.78 us
    pallas_call x1, Pallas kernels, by_states(): call(functools.partial(middle_body, terms), acc_shape, [smem] + [vmem] *...  4.43 us
    ppermute x1, waiting for transfers between devices, by_states(): near = lax.ppermute(mine, 'blk', NEAR)  4.25 us
    ppermute x1, waiting for transfers between devices, by_states(): outer = lax.ppermute(far, 'blk', OUTWARD)  4.21 us
    ppermute x1, waiting for transfers between devices, by_states(): far = lax.ppermute(mine, 'blk', FAR)  3.73 us
    pallas_call x1, Pallas kernels, by_states(): call(functools.partial(own_body, terms, rights, phys), (jax.ShapeDtypeStr...  3.12 us
  transfers between devices with their start and end apart: 12, of which 5 were waited for; matrix products, arithmetic and copies ran while one was open for 3% of the time, Pallas kernels for 14%

profile of v1, /device:TPU:0, one launch (start us, length us, event | category | flops | bytes accessed | tf_op | source)
XLA Modules:
  0.0 54.1 jit_solution(15232290043519046945)
XLA Ops:
  0.0 0.8 %copy.8.rsource_ref = s32[4,2]{1,0:T(4,128)S(1)} copy(s32[4,2]{0,1:T(2,128)} %param.12) | data formatting | bytes 64 | tf_op args[5]
  0.8 0.1 pad_add_fusion.place_ref
  0.8 0.0 copy-start
  0.8 0.9 %copy-done = bf16[4,2,128,128]{3,2,1,0:T(8,128)(2,1)S(1)} copy-done((bf16[4,2,128,128]{3,2,1,0:T(8,128)(2,1)S(1)}, bf16[4,2,128,128]{3,2,1,0:T(8,128)(2,1)}, u32[]{:S(2)}) %copy-start) | copy-done | bytes 262168
  1.8 0.0 copy-start.1
  1.8 0.9 %copy-done.1 = bf16[4,1,128,128]{3,2,1,0:T(8,128)(2,1)S(1)} copy-done((bf16[4,1,128,128]{3,2,1,0:T(8,128)(2,1)S(1)}, bf16[4,1,128,128]{3,2,1,0:T(8,128)(2,1)}, u32[]{:S(2)}) %copy-start.1) | copy-done | bytes 131096
  2.7 0.0 copy-start.2
  2.7 0.7 %copy-done.2 = bf16[4,16,16]{2,1,0:T(8,128)(2,1)S(1)} copy-done((bf16[4,16,16]{2,1,0:T(8,128)(2,1)S(1)}, bf16[4,16,16]{2,1,0:T(8,128)(2,1)}, u32[]{:S(2)}) %copy-start.2) | copy-done | bytes 2072
  3.4 0.0 copy-start.3
  3.4 0.7 %copy-done.3 = s32[4,4]{1,0:T(4,128)S(1)} copy-done((s32[4,4]{1,0:T(4,128)S(1)}, s32[4,4]{1,0:T(4,128)}, u32[]{:S(2)}) %copy-start.3) | copy-done | bytes 88
  4.1 0.7 %pack_operators.1.refs_0_ = bf16[1568,128]{1,0:T(8,128)(2,1)S(1)} custom-call(s32[2]{0:T(128)S(1)} %pad_add_fusion.place_ref, bf16[4,1,128,128]{3,2,1,0:T(8,128)(2,1)S(1)} %copy-done.1, bf16[4,2,128,128]{3,2,1,0:T(8,128)(2,1)S(1)} %copy-done, bf16[4,16,16]{2,1,0:T(8,128)(2,1)S(1)} %copy-done.2, s32[4,4]{1,0:T(4,128)S(1)} %copy-done.3, ...), custom_call_target="tpu_custom_call" | custom-call | tf_op jit(solution)/shard_map/pack_operators/pallas_call | solution.py:243
  4.8 2.9 %collective-permute-start = (bf16[1568,128]{1,0:T(8,128)(2,1)S(1)}, bf16[1568,128]{1,0:T(8,128)(2,1)S(1)}, u32[]{:S(2)}, u32[]{:S(2)}) collective-permute-start(bf16[1568,128]{1,0:T(8,128)(2,1)S(1)} %pack_operators.1.refs_0_), channel_id=1, source_target_pairs={{0,2},{2,0},{1,3},{3,1},{4,6},{6,4},{5,7},{7,5},{8,10},{10,8},{9,1... | collective-permute-start | bytes 1204232 | tf_op jit(solution)/shard_map/ppermute | solution.py:249
  7.8 1.1 %constant_dynamic-slice_fusion = (bf16[512,256]{1,0:T(8,128)(2,1)S(1)}, bf16[512,256]{1,0:T(8,128)(2,1)S(1)}) fusion(bf16[512,1024]{1,0:T(8,128)(2,1)} %param.7, s32[]{:T(128)S(6)} %select_n.7, s32[]{:T(128)S(6)} %select_n.6), kind=kLoop, calls=%fused_computation.3 | loop fusion | bytes 1048584 | tf_op jit(solution)/shard_map/dynamic_slice | solution.py:259
  8.9 2.7 %collective-permute-start.5 = (bf16[512,256]{1,0:T(8,128)(2,1)S(1)}, bf16[512,256]{1,0:T(8,128)(2,1)S(1)}, u32[]{:S(2)}, u32[]{:S(2)}) collective-permute-start(bf16[512,256]{1,0:T(8,128)(2,1)S(1)} %get-tuple-element.16.refs_4_), channel_id=1, source_target_pairs={{0,8},{8,0},{4,12},{12,4},{1,9},{9,1},{5,13},{13,5},{2,10},{10,2},... | collective-permute-start | bytes 786440 | tf_op jit(solution)/shard_map/ppermute | solution.py:237
  11.5 0.0 collective-permute-start.1
  11.5 5.6 %collective-permute-done.refs_1_ = bf16[1568,128]{1,0:T(8,128)(2,1)S(1)} collective-permute-done((bf16[1568,128]{1,0:T(8,128)(2,1)S(1)}, bf16[1568,128]{1,0:T(8,128)(2,1)S(1)}, u32[]{:S(2)}, u32[]{:S(2)}) %collective-permute-start) | collective-permute-done | bytes 401440 | tf_op jit(solution)/shard_map/ppermute | solution.py:249
  17.1 0.0 collective-permute-start.2
  17.1 1.8 %collective-permute-start.3 = (bf16[512,256]{1,0:T(8,128)(2,1)S(1)}, bf16[512,256]{1,0:T(8,128)(2,1)S(1)}, u32[]{:S(2)}, u32[]{:S(2)}) collective-permute-start(bf16[512,256]{1,0:T(8,128)(2,1)S(1)} %get-tuple-element.16.refs_4_), channel_id=1, source_target_pairs={{0,4},{4,0},{8,12},{12,8},{1,5},{5,1},{9,13},{13,9},{2,6},{6,2},{1... | collective-permute-start | bytes 786440 | tf_op jit(solution)/shard_map/ppermute | solution.py:238
  18.9 0.7 %collective-permute-start.7 = (bf16[512,256]{1,0:T(8,128)(2,1)S(1)}, bf16[512,256]{1,0:T(8,128)(2,1)S(1)}, u32[]{:S(2)}, u32[]{:S(2)}) collective-permute-start(bf16[512,256]{1,0:T(8,128)(2,1)S(1)} %get-tuple-element.16.refs_4_), channel_id=1, source_target_pairs={{4,8},{8,4},{5,9},{9,5},{6,10},{10,6},{7,11},{11,7},{20,24},{24,20... | collective-permute-start | bytes 786440 | tf_op jit(solution)/shard_map/ppermute | solution.py:239
  19.6 3.7 %collective-permute-done.5.refs_9_ = bf16[512,256]{1,0:T(8,128)(2,1)S(1)} collective-permute-done((bf16[512,256]{1,0:T(8,128)(2,1)S(1)}, bf16[512,256]{1,0:T(8,128)(2,1)S(1)}, u32[]{:S(2)}, u32[]{:S(2)}) %collective-permute-start.5) | collective-permute-done | bytes 262176 | tf_op jit(solution)/shard_map/ppermute | solution.py:237
  23.3 1.3 %collective-permute-start.9 = (bf16[512,256]{1,0:T(8,128)(2,1)S(1)}, bf16[512,256]{1,0:T(8,128)(2,1)S(1)}, u32[]{:S(2)}, u32[]{:S(2)}) collective-permute-start(bf16[512,256]{1,0:T(8,128)(2,1)S(1)} %collective-permute-done.5.refs_9_), channel_id=1, source_target_pairs={{4,0},{8,12},{5,1},{9,13},{6,2},{10,14},{7,3},{11,15},{20,16},{24,... | collective-permute-start | bytes 786440 | tf_op jit(solution)/shard_map/ppermute | solution.py:240
  24.6 4.3 %collective-permute-done.3.refs_7_ = bf16[512,256]{1,0:T(8,128)(2,1)S(1)} collective-permute-done((bf16[512,256]{1,0:T(8,128)(2,1)S(1)}, bf16[512,256]{1,0:T(8,128)(2,1)S(1)}, u32[]{:S(2)}, u32[]{:S(2)}) %collective-permute-start.3) | collective-permute-done | bytes 262176 | tf_op jit(solution)/shard_map/ppermute | solution.py:238
  28.9 0.1 collective-permute-start.6
  28.9 0.0 collective-permute-done.7.refs_7_
  28.9 0.5 collective-permute-start.4
  29.4 0.8 %copy.9.live_ref = s32[4,2]{1,0:T(4,128)S(1)} copy(s32[4,2]{0,1:T(2,128)} %param.13) | data formatting | bytes 64 | tf_op args[6]
  30.1 0.0 collective-permute-done.1.refs_2_
  30.1 0.1 collective-permute-start.8
  30.2 4.2 %collective-permute-done.9.refs_9_ = bf16[512,256]{1,0:T(8,128)(2,1)S(1)} collective-permute-done((bf16[512,256]{1,0:T(8,128)(2,1)S(1)}, bf16[512,256]{1,0:T(8,128)(2,1)S(1)}, u32[]{:S(2)}, u32[]{:S(2)}) %collective-permute-start.9) | collective-permute-done | bytes 262176 | tf_op jit(solution)/shard_map/ppermute | solution.py:240
  34.4 0.1 collective-permute-start.10
  34.5 0.0 collective-permute-done.2.refs_3_
  34.5 3.1 %own_shard.1 = (bf16[16,256,256]{2,1,0:T(8,128)(2,1)S(1)}, bf16[4,128,512]{2,1,0:T(8,128)(2,1)S(1)}, f32[8,128,256]{2,1,0:T(8,128)S(1)}) custom-call(s32[2]{0:T(128)S(1)} %pad_add_fusion.place_ref, s32[4,12]{1,0:T(4,128)S(1)} %maximum_convert_fusion.index_ref, s32[4,2]{1,0:T(4,128)S(1)} %copy.9.live_ref, bf16[1568,128]{1,0:T(8,128)(2,1)S(1)} %pack_operators.1.refs_0_, ...), custom_call_target="tpu_custom_call" | custom-call | flops 1073741824 | bytes 8388608 | tf_op jit(solution)/shard_map/own_shard/pallas_call | solution.py:263
  37.7 0.0 collective-permute-done.6.refs_10_
  37.7 0.0 collective-permute-done.4.refs_8_
  37.7 4.4 %middle_shards.1.refs_6_ = f32[8,128,256]{2,1,0:T(8,128)S(1)} custom-call(s32[4,12]{1,0:T(4,128)S(1)} %maximum_convert_fusion.index_ref, bf16[1568,128]{1,0:T(8,128)(2,1)S(1)} %pack_operators.1.refs_0_, bf16[1568,128]{1,0:T(8,128)(2,1)S(1)} %collective-permute-done.refs_1_, bf16[1568,128]{1,0:T(8,128)(2,1)S(1)} %collective-permute-done.1.refs_2_, ...), custom_call_target="tpu_custom_call" | custom-call | flops 2147483648 | bytes 8388608 | tf_op jit(solution)/shard_map/middle_shards/pallas_call | solution.py:276
  42.1 0.0 collective-permute-done.8.refs_8_
  42.1 0.0 collective-permute-done.10.refs_10_
  42.2 2.5 %last_shard.1 = (bf16[128,1024]{1,0:T(8,128)(2,1)S(1)}, f32[128,1024]{1,0:T(8,128)S(1)}) custom-call(s32[2]{0:T(128)S(1)} %pad_add_fusion.place_ref, s32[4,12]{1,0:T(4,128)S(1)} %maximum_convert_fusion.index_ref, bf16[1568,128]{1,0:T(8,128)(2,1)S(1)} %pack_operators.1.refs_0_, bf16[1568,128]{1,0:T(8,128)(2,1)S(1)} %collective-permute-done.refs_1_, ...), custom_call_target="tpu_custom_call" | custom-call | flops 1073741824 | bytes 8388608 | tf_op jit(solution)/shard_map/last_shard/pallas_call | solution.py:285
  44.6 0.5 %collective-permute-start.11 = (bf16[128,1024]{1,0:T(8,128)(2,1)S(1)}, bf16[128,1024]{1,0:T(8,128)(2,1)S(1)}, u32[]{:S(2)}, u32[]{:S(2)}) collective-permute-start(bf16[128,1024]{1,0:T(8,128)(2,1)S(1)} %get-tuple-element.14), channel_id=1, source_target_pairs={{0,2},{2,0},{1,3},{3,1},{4,6},{6,4},{5,7},{7,5},{8,10},{10,8},{9,1... | collective-permute-start | bytes 786440 | tf_op jit(solution)/shard_map/ppermute | solution.py:297
  45.2 8.2 %collective-permute-done.11 = bf16[128,1024]{1,0:T(8,128)(2,1)S(1)} collective-permute-done((bf16[128,1024]{1,0:T(8,128)(2,1)S(1)}, bf16[128,1024]{1,0:T(8,128)(2,1)S(1)}, u32[]{:S(2)}, u32[]{:S(2)}) %collective-permute-start.11) | collective-permute-done | bytes 262176 | tf_op jit(solution)/shard_map/ppermute | solution.py:297
  53.4 0.8 %add_convert_fusion = bf16[128,1024]{1,0:T(8,128)(2,1)} fusion(f32[128,1024]{1,0:T(8,128)S(1)} %get-tuple-element.13, bf16[128,1024]{1,0:T(8,128)(2,1)S(1)} %collective-permute-done.11), kind=kLoop, calls=%fused_computation | loop fusion | flops 393216 | bytes 1048576 | tf_op jit(solution)/shard_map/convert_element_type | solution.py:298
  (5 shorter events, 0.0 us)
Async XLA Ops:
  0.8 0.9 %copy-start = (bf16[4,2,128,128]{3,2,1,0:T(8,128)(2,1)S(1)}, bf16[4,2,128,128]{3,2,1,0:T(8,128)(2,1)}, u32[]{:S(2)}) copy-start(bf16[4,2,128,128]{3,2,1,0:T(8,128)(2,1)} %right_ref.1) | copy-start | bytes 786436
  1.8 0.9 %copy-start.1 = (bf16[4,1,128,128]{3,2,1,0:T(8,128)(2,1)S(1)}, bf16[4,1,128,128]{3,2,1,0:T(8,128)(2,1)}, u32[]{:S(2)}) copy-start(bf16[4,1,128,128]{3,2,1,0:T(8,128)(2,1)} %left_ref.1) | copy-start | bytes 393220
  2.7 0.7 %copy-start.2 = (bf16[4,16,16]{2,1,0:T(8,128)(2,1)S(1)}, bf16[4,16,16]{2,1,0:T(8,128)(2,1)}, u32[]{:S(2)}) copy-start(bf16[4,16,16]{2,1,0:T(8,128)(2,1)} %site_ref.1) | copy-start | bytes 6148
  3.4 0.7 %copy-start.3 = (s32[4,4]{1,0:T(4,128)S(1)}, s32[4,4]{1,0:T(4,128)}, u32[]{:S(2)}) copy-start(s32[4,4]{1,0:T(4,128)} %sources_ref.1) | copy-start | bytes 196
  4.8 12.2 %collective-permute-start = (bf16[1568,128]{1,0:T(8,128)(2,1)S(1)}, bf16[1568,128]{1,0:T(8,128)(2,1)S(1)}, u32[]{:S(2)}, u32[]{:S(2)}) collective-permute-start(bf16[1568,128]{1,0:T(8,128)(2,1)S(1)} %pack_operators.1.refs_0_), channel_id=1, source_target_pairs={{0,2},{2,0},{1,3},{3,1},{4,6},{6,4},{5,7},{7,5},{8,10},{10,8},{9,1... | collective-permute-start | bytes 1204232 | tf_op jit(solution)/shard_map/ppermute | solution.py:249
  8.9 14.5 %collective-permute-start.5 = (bf16[512,256]{1,0:T(8,128)(2,1)S(1)}, bf16[512,256]{1,0:T(8,128)(2,1)S(1)}, u32[]{:S(2)}, u32[]{:S(2)}) collective-permute-start(bf16[512,256]{1,0:T(8,128)(2,1)S(1)} %get-tuple-element.16.refs_4_), channel_id=1, source_target_pairs={{0,8},{8,0},{4,12},{12,4},{1,9},{9,1},{5,13},{13,5},{2,10},{10,2},... | collective-permute-start | bytes 786440 | tf_op jit(solution)/shard_map/ppermute | solution.py:237
  11.5 18.6 %collective-permute-start.1 = (bf16[1568,128]{1,0:T(8,128)(2,1)S(1)}, bf16[1568,128]{1,0:T(8,128)(2,1)S(1)}, u32[]{:S(2)}, u32[]{:S(2)}) collective-permute-start(bf16[1568,128]{1,0:T(8,128)(2,1)S(1)} %pack_operators.1.refs_0_), channel_id=1, source_target_pairs={{0,1},{1,0},{2,3},{3,2},{4,5},{5,4},{6,7},{7,6},{8,9},{9,8},{10,11... | collective-permute-start | bytes 1204232 | tf_op jit(solution)/shard_map/ppermute | solution.py:250
  17.1 17.5 %collective-permute-start.2 = (bf16[1568,128]{1,0:T(8,128)(2,1)S(1)}, bf16[1568,128]{1,0:T(8,128)(2,1)S(1)}, u32[]{:S(2)}, u32[]{:S(2)}) collective-permute-start(bf16[1568,128]{1,0:T(8,128)(2,1)S(1)} %collective-permute-done.refs_1_), channel_id=1, source_target_pairs={{0,1},{1,0},{2,3},{3,2},{4,5},{5,4},{6,7},{7,6},{8,9},{9,8},{10,11... | collective-permute-start | bytes 1204232 | tf_op jit(solution)/shard_map/ppermute | solution.py:251
  17.1 11.8 %collective-permute-start.3 = (bf16[512,256]{1,0:T(8,128)(2,1)S(1)}, bf16[512,256]{1,0:T(8,128)(2,1)S(1)}, u32[]{:S(2)}, u32[]{:S(2)}) collective-permute-start(bf16[512,256]{1,0:T(8,128)(2,1)S(1)} %get-tuple-element.16.refs_4_), channel_id=1, source_target_pairs={{0,4},{4,0},{8,12},{12,8},{1,5},{5,1},{9,13},{13,9},{2,6},{6,2},{1... | collective-permute-start | bytes 786440 | tf_op jit(solution)/shard_map/ppermute | solution.py:238
  18.9 10.0 %collective-permute-start.7 = (bf16[512,256]{1,0:T(8,128)(2,1)S(1)}, bf16[512,256]{1,0:T(8,128)(2,1)S(1)}, u32[]{:S(2)}, u32[]{:S(2)}) collective-permute-start(bf16[512,256]{1,0:T(8,128)(2,1)S(1)} %get-tuple-element.16.refs_4_), channel_id=1, source_target_pairs={{4,8},{8,4},{5,9},{9,5},{6,10},{10,6},{7,11},{11,7},{20,24},{24,20... | collective-permute-start | bytes 786440 | tf_op jit(solution)/shard_map/ppermute | solution.py:239
  23.3 11.1 %collective-permute-start.9 = (bf16[512,256]{1,0:T(8,128)(2,1)S(1)}, bf16[512,256]{1,0:T(8,128)(2,1)S(1)}, u32[]{:S(2)}, u32[]{:S(2)}) collective-permute-start(bf16[512,256]{1,0:T(8,128)(2,1)S(1)} %collective-permute-done.5.refs_9_), channel_id=1, source_target_pairs={{4,0},{8,12},{5,1},{9,13},{6,2},{10,14},{7,3},{11,15},{20,16},{24,... | collective-permute-start | bytes 786440 | tf_op jit(solution)/shard_map/ppermute | solution.py:240
  28.9 8.8 %collective-permute-start.6 = (bf16[512,256]{1,0:T(8,128)(2,1)S(1)}, bf16[512,256]{1,0:T(8,128)(2,1)S(1)}, u32[]{:S(2)}, u32[]{:S(2)}) collective-permute-start(bf16[512,256]{1,0:T(8,128)(2,1)S(1)} %collective-permute-done.5.refs_9_), channel_id=1, source_target_pairs={{0,1},{1,0},{2,3},{3,2},{4,5},{5,4},{6,7},{7,6},{8,9},{9,8},{10,11... | collective-permute-start | bytes 786440 | tf_op jit(solution)/shard_map/ppermute | solution.py:257
  28.9 8.8 %collective-permute-start.4 = (bf16[512,256]{1,0:T(8,128)(2,1)S(1)}, bf16[512,256]{1,0:T(8,128)(2,1)}, u32[]{:S(2)}, u32[]{:S(2)}) collective-permute-start(bf16[512,256]{1,0:T(8,128)(2,1)S(1)} %collective-permute-done.3.refs_7_), channel_id=1, source_target_pairs={{0,1},{1,0},{2,3},{3,2},{4,5},{5,4},{6,7},{7,6},{8,9},{9,8},{10,11... | collective-permute-start | bytes 786440 | tf_op jit(solution)/shard_map/ppermute | solution.py:257
  30.1 12.0 %collective-permute-start.8 = (bf16[512,256]{1,0:T(8,128)(2,1)S(1)}, bf16[512,256]{1,0:T(8,128)(2,1)S(1)}, u32[]{:S(2)}, u32[]{:S(2)}) collective-permute-start(bf16[512,256]{1,0:T(8,128)(2,1)S(1)} %collective-permute-done.7.refs_7_), channel_id=1, source_target_pairs={{0,1},{1,0},{2,3},{3,2},{4,5},{5,4},{6,7},{7,6},{8,9},{9,8},{10,11... | collective-permute-start | bytes 786440 | tf_op jit(solution)/shard_map/ppermute | solution.py:257
  34.4 7.7 %collective-permute-start.10 = (bf16[512,256]{1,0:T(8,128)(2,1)S(1)}, bf16[512,256]{1,0:T(8,128)(2,1)S(1)}, u32[]{:S(2)}, u32[]{:S(2)}) collective-permute-start(bf16[512,256]{1,0:T(8,128)(2,1)S(1)} %collective-permute-done.9.refs_9_), channel_id=1, source_target_pairs={{0,1},{1,0},{2,3},{3,2},{4,5},{5,4},{6,7},{7,6},{8,9},{9,8},{10,11... | collective-permute-start | bytes 786440 | tf_op jit(solution)/shard_map/ppermute | solution.py:257
  44.6 8.7 %collective-permute-start.11 = (bf16[128,1024]{1,0:T(8,128)(2,1)S(1)}, bf16[128,1024]{1,0:T(8,128)(2,1)S(1)}, u32[]{:S(2)}, u32[]{:S(2)}) collective-permute-start(bf16[128,1024]{1,0:T(8,128)(2,1)S(1)} %get-tuple-element.14), channel_id=1, source_target_pairs={{0,2},{2,0},{1,3},{3,1},{4,6},{6,4},{5,7},{7,5},{8,10},{10,8},{9,1... | collective-permute-start | bytes 786440 | tf_op jit(solution)/shard_map/ppermute | solution.py:297

commit v2 on v0

v2 whole, which is shorter than its diff:
```python
import functools

import jax
import jax.numpy as jnp
from jax import lax
from jax.experimental import pallas as pl
from jax.experimental.pallas import tpu as pltpu
from jax.sharding import PartitionSpec as P

F32 = jnp.float32
BF16 = jnp.bfloat16
VMEM_BYTES = 32 * 1024 * 1024
SLICE_BYTES = 53 * 1024 * 1024
PACK_BYTES = 53 * 1024 * 1024
CHIP_FLOPS = int(8e9)
CORE_FLOPS = int(3e9)
NEAR = ((0, 1), (1, 0), (2, 3), (3, 2))
FAR = ((0, 2), (2, 0), (1, 3), (3, 1))
MIDDLE = ((1, 2), (2, 1))
OUTWARD = ((1, 0), (2, 3))
CORE = ((0, 1), (1, 0), (2, 3), (3, 2))
ACROSS = ((0, 2), (2, 0), (1, 3), (3, 1))
SUB = 16


def carry_left(blocks, sources, pieces):
    picked = jnp.take(blocks, sources, axis=0)
    return jnp.einsum(
        "...aij,...ajc->...aic", pieces, picked, preferred_element_type=F32
    ).astype(BF16)


def apply_right(received, site_one, source_one, right_one, physical, right_count, block_rows):
    shaped = received.reshape(received.shape[0], physical, right_count, block_rows)
    turned = jnp.einsum(
        "st,itrj->isrj", site_one, shaped, preferred_element_type=F32
    ).astype(BF16)
    picked = jnp.take(turned, source_one, axis=2)
    return jnp.einsum("isbj,bkj->isbk", picked, right_one, preferred_element_type=F32)


def by_terms(
    wavefunction, left_blocks, right_blocks, site_terms, left_source, right_source, live_pairs
):
    all_rows, columns = wavefunction.shape
    term_count, own_sectors, block_rows = left_blocks.shape[:3]
    physical = site_terms.shape[1]
    right_count = right_blocks.shape[1]
    own_rows = own_sectors * block_rows
    blocks = wavefunction.reshape(all_rows // block_rows, block_rows, columns)
    accumulated = jnp.zeros((own_rows, physical, right_count, block_rows), F32)
    for member in range(term_count):
        pieces = lax.all_gather(left_blocks[member], "blk", axis=0, tiled=True)
        carried = carry_left(blocks, left_source[member], pieces)
        received = lax.all_to_all(
            carried.reshape(all_rows, columns), "blk", split_axis=0, concat_axis=1, tiled=True
        )
        accumulated = accumulated + apply_right(
            received,
            site_terms[member],
            right_source[member],
            right_blocks[member],
            physical,
            right_count,
            block_rows,
        )
    position = lax.axis_index("blk")
    live_rows = lax.dynamic_slice_in_dim(live_pairs, position * own_sectors, own_sectors, 0)
    row_mask = jnp.repeat(live_rows.astype(F32), block_rows, axis=0)
    accumulated = accumulated * row_mask[:, None, :, None]
    flattened = accumulated.reshape(own_rows, physical * right_count * block_rows)
    summed = lax.psum_scatter(flattened, "mpo", scatter_dimension=1, tiled=True)
    return summed.astype(BF16)


def matmul(a, b):
    return jnp.dot(a, b, preferred_element_type=F32)


def slice_body(wave_ref, own_ref, sem):
    width = own_ref.shape[1]
    start = pl.multiple_of(lax.axis_index("mpo") * width, width)
    copy = pltpu.make_async_copy(wave_ref.at[:, pl.ds(start, width)], own_ref, sem)
    copy.start()
    copy.wait()


def pack_body(
    terms, rights, phys, left_hbm, right_hbm, site_hbm, sources_hbm, rsource_hbm, live_hbm,
    pack_ref, right_ref, site_ref, sources_ref, rsource_ref, live_ref, sems,
):
    block = right_ref.shape[-1]
    own_blk = lax.axis_index("blk")
    inputs = [
        (right_hbm, right_ref),
        (site_hbm, site_ref),
        (sources_hbm, sources_ref),
        (rsource_hbm, rsource_ref),
        (live_hbm, live_ref),
    ]
    for w in range(terms):
        inputs.append((left_hbm.at[w, 0], pack_ref.at[pl.ds(w * block, block), :]))
    copies = [
        pltpu.make_async_copy(source, target, sems.at[n])
        for n, (source, target) in enumerate(inputs)
    ]
    for copy in copies:
        copy.start()
    for copy in copies[1:5]:
        copy.wait()
    base = terms * (1 + rights) * block
    lane = lax.broadcasted_iota(jnp.int32, (phys, block), 1)
    row = lax.broadcasted_iota(jnp.int32, (phys, block), 0)
    site = jnp.zeros((phys, block), F32)
    for w in range(terms):
        spot = jnp.where(lane == row + w * phys, 1.0, 0.0).astype(BF16)
        site = site + matmul(site_ref[w], spot)
    pack_ref[base : base + phys, :] = site.astype(BF16)
    numbers = jnp.zeros((SUB, block), F32)
    lane = lax.broadcasted_iota(jnp.int32, (SUB, block), 1)
    for w in range(terms):
        numbers = jnp.where(lane == w, sources_ref[w, own_blk].astype(F32), numbers)
        for b in range(rights):
            at = terms + w * rights + b
            numbers = jnp.where(lane == at, rsource_ref[b, w].astype(F32), numbers)
    for b in range(rights):
        at = terms * (1 + rights) + b
        numbers = jnp.where(lane == at, live_ref[b, own_blk].astype(F32), numbers)
    pack_ref[base + phys : base + phys + SUB, :] = numbers.astype(BF16)
    copies[0].wait()
    for w in range(terms):
        for b in range(rights):
            at = (terms + w * rights + b) * block
            pack_ref[at : at + block, :] = right_ref[w, b].astype(F32).T.astype(BF16)
    for copy in copies[5:]:
        copy.wait()


def right_matrices(terms, rights, numbers, alive, packs, w_ref):
    block = packs[0].shape[-1]
    for k in range(len(packs)):
        for w in range(terms):
            for b in range(rights):
                start = (terms + w * rights + b) * block
                turned = packs[k][start : start + block, :]
                source = numbers[k, terms + w * rights + b]
                for r in range(rights):
                    keep = jnp.logical_and(source == r, alive[b] != 0)
                    w_ref[k * terms + w, r * block : (r + 1) * block, b * block : (b + 1) * block] = (
                        jnp.where(keep, turned, jnp.zeros_like(turned))
                    )


def spread_site(terms, rights, phys, packs, first, kron_ref):
    block = packs[0].shape[-1]
    me, own_blk = lax.axis_index("mpo"), lax.axis_index("blk")
    site_at = (1 + rights) * terms * block
    site = jnp.concatenate([p[site_at : site_at + phys, :] for p in packs], axis=1)
    rows, depth = kron_ref.shape
    quarter, here = phys // 4, len(packs) * block
    srow = lax.broadcasted_iota(jnp.int32, (rows, phys), 0) >> 4
    turn = srow >> 2
    owner = lax.bitwise_xor(me, jnp.where(turn == 0, 3, jnp.where(turn == 3, 0, turn)))
    swant = owner * quarter + (srow & 3)
    pick_s = jnp.where(
        lax.broadcasted_iota(jnp.int32, (rows, phys), 1) == swant, 1.0, 0.0
    ).astype(BF16)
    column = lax.broadcasted_iota(jnp.int32, (here, depth), 1)
    slot = column >> 4
    shard, pack, term = slot // (terms * len(packs)), (slot // terms) % len(packs), slot % terms
    state = lax.bitwise_xor(own_blk, shard + first) * quarter + me
    pick_t = jnp.where(
        lax.broadcasted_iota(jnp.int32, (here, depth), 0) == pack * block + term * phys + state,
        1.0,
        0.0,
    ).astype(BF16)
    spread = matmul(pick_s, matmul(site, pick_t).astype(BF16))
    diagonal = (lax.broadcasted_iota(jnp.int32, (rows, depth), 0) & 15) == (
        lax.broadcasted_iota(jnp.int32, (rows, depth), 1) & 15
    )
    kron_ref[...] = jnp.where(diagonal, spread, 0.0).astype(BF16)


def turn_shard(terms, numbers, packs, w_ref, shard, y_ref, at):
    block = packs[0].shape[-1]
    tiles = y_ref.shape[0]
    for k in range(len(packs)):
        for w in range(terms):
            row = pl.multiple_of(numbers[k, w] * block, block)
            left = packs[k][w * block : (w + 1) * block, :]
            carried = matmul(left, shard[pl.ds(row, block), :]).astype(BF16)
            y = matmul(carried, w_ref[k * terms + w]).astype(BF16)
            y_ref[:, at : at + SUB, :] = y.reshape(tiles, SUB, y.shape[-1])
            at += SUB
    return at


class Numbers:
    def __init__(self, refs):
        self.refs = refs

    def __getitem__(self, at):
        return self.refs[at[0]][0, at[1]]


def terms_body(terms, rights, phys, plan, live_ref, *refs):
    packs_n, shards_n, first, make, before, all_n = plan
    number_refs, refs = refs[:packs_n], refs[packs_n:]
    packs, refs = refs[:packs_n], refs[packs_n:]
    others, refs = refs[:all_n], refs[all_n:]
    shards, refs = refs[:shards_n], refs[shards_n:]
    if not make:
        w_ref, refs = refs[0], refs[1:]
    acc_in, refs = (refs[0], refs[1:]) if before else (None, refs)
    numbers = Numbers(number_refs)
    if make:
        w_ref, refs = refs[0], refs[1:]
        alive = [live_ref[0, terms * (1 + rights) + b] for b in range(rights)]
        right_matrices(terms, rights, numbers, alive, packs, w_ref)
    if all_n:
        spread_site(terms, rights, phys, others, 3, refs[0])
        refs = refs[1:]
    acc_ref, kron_ref, y_ref = refs
    spread_site(terms, rights, phys, packs, first, kron_ref)
    at = 0
    for shard in shards:
        at = turn_shard(terms, numbers, packs, w_ref, shard, y_ref, at)
    for i in range(y_ref.shape[0]):
        total = matmul(kron_ref[...], y_ref[i])
        acc_ref[i] = total if acc_in is None else total + acc_in[i]


def last_body(terms, *refs):
    number_refs, packs, (w_own, w_core, w_far, kron_ref, acc_in) = refs[:4], refs[4:8], refs[8:13]
    inner, outer = refs[13:15]
    quarters, (y_ref, shard_ref) = refs[15:19], refs[19:]
    own_blk = lax.axis_index("blk")
    at_end = jnp.logical_or(own_blk == 0, own_blk == 3)
    shard_ref[...] = jnp.where(at_end, outer[...], inner[...])
    at = 0
    for here, w_ref in (((0,), w_own), ((1,), w_core), ((2, 3), w_far)):
        numbers = Numbers([number_refs[k] for k in here])
        at = turn_shard(terms, numbers, [packs[k] for k in here], w_ref, shard_ref, y_ref, at)
    width = w_own.shape[-1]
    for i in range(y_ref.shape[0]):
        total = matmul(kron_ref[...], y_ref[i]) + acc_in[i]
        count = total.shape[0] // SUB // 4
        for n, target in enumerate(quarters):
            for m in range(count):
                start = (n * count + m) * SUB
                target[i * SUB : (i + 1) * SUB, m * width : (m + 1) * width] = total[
                    start : start + SUB, :
                ].astype(target.dtype)


def call(body, out_shape, in_specs, scratch=(), out_specs=None, name=None, vmem=VMEM_BYTES, flops=1000):
    extra = {} if out_specs is None else {"out_specs": out_specs}
    return pl.pallas_call(
        body,
        out_shape=out_shape,
        in_specs=in_specs,
        scratch_shapes=scratch,
        compiler_params=pltpu.CompilerParams(vmem_limit_bytes=vmem),
        cost_estimate=pl.CostEstimate(flops=flops, bytes_accessed=1000, transcendentals=0),
        name=name,
        **extra,
    )


def by_states(
    wavefunction, left_blocks, right_blocks, site_terms, left_source, right_source, live_pairs
):
    all_rows = wavefunction.shape[0]
    terms, _, block, _ = left_blocks.shape
    rights = right_blocks.shape[1]
    phys = site_terms.shape[1]
    width = rights * block
    slots = 4
    rows = phys * SUB
    tiles = block // SUB
    smem = pl.BlockSpec(memory_space=pltpu.SMEM)
    vmem = pl.BlockSpec(memory_space=pltpu.VMEM)
    hbm = pl.BlockSpec(memory_space=pltpu.HBM)

    pack_rows = terms * (1 + rights) * block + phys + SUB
    mine = call(
        slice_body,
        jax.ShapeDtypeStruct((all_rows, width), BF16),
        [hbm],
        [pltpu.SemaphoreType.DMA],
        out_specs=vmem,
        name="own_states",
        vmem=SLICE_BYTES,
    )(wavefunction)

    def swap(x):
        return lax.ppermute(x, "mpo", CORE)

    pack = call(
        functools.partial(pack_body, terms, rights, phys),
        jax.ShapeDtypeStruct((pack_rows, block), BF16),
        [hbm] * 6,
        [
            pltpu.VMEM(right_blocks.shape, BF16),
            pltpu.VMEM(site_terms.shape, BF16),
            pltpu.SMEM(left_source.shape, jnp.int32),
            pltpu.SMEM(right_source.T.shape, jnp.int32),
            pltpu.SMEM(live_pairs.T.shape, jnp.int32),
            pltpu.SemaphoreType.DMA((terms + 5,)),
        ],
        out_specs=vmem,
        name="pack_operators",
        vmem=PACK_BYTES,
    )(left_blocks, right_blocks, site_terms, left_source, right_source.T, live_pairs.T)

    def numbers_of(p):
        return p[pack_rows - SUB : pack_rows - SUB + 1, :].astype(jnp.int32)

    far = lax.ppermute(mine, "blk", FAR)
    near = lax.ppermute(mine, "blk", NEAR)
    pack_x = lax.ppermute(pack, "mpo", ACROSS)
    acc_shape = jax.ShapeDtypeStruct((tiles, rows, width), F32)
    one_pack = terms * SUB

    def run(name, packs, numbers, shards, first, acc, w=None, every=(), flops=1000):
        plan = (len(packs), len(shards), first, w is None, acc is not None, len(every))
        depth = len(packs) * len(shards) * one_pack
        shapes = [acc_shape]
        if every:
            shapes.insert(0, jax.ShapeDtypeStruct((rows, len(every) * one_pack), BF16))
        if w is None:
            shapes.insert(0, jax.ShapeDtypeStruct((len(packs) * terms, width, width), BF16))
        arrays = [*packs, *every, *shards]
        arrays += [a for a in (w, acc) if a is not None]
        return call(
            functools.partial(terms_body, terms, rights, phys, plan),
            tuple(shapes),
            [smem] * (1 + len(numbers)) + [vmem] * len(arrays),
            [pltpu.VMEM((rows, depth), BF16), pltpu.VMEM((tiles, depth, width), BF16)],
            name=name,
            flops=flops,
        )(own_number, *numbers, *arrays)

    own_number = numbers_of(pack)
    w_own, acc = run("own_terms_own", (pack,), (own_number,), (mine,), 0, None)
    far, acc = lax.optimization_barrier((far, acc))
    outer = lax.ppermute(far, "blk", OUTWARD)
    far, later, pack_own = lax.optimization_barrier((far, mine, pack))
    inner = lax.ppermute(later, "blk", MIDDLE)
    pack_c = swap(pack_own)
    (acc,) = run(
        "own_terms", (pack_own,), (own_number,), (near, far), 1, acc, w=w_own, flops=CHIP_FLOPS
    )
    acc, pack_x, pack_c = lax.optimization_barrier((acc, pack_x, pack_c))
    core_number = numbers_of(pack_c)
    x_packs = (pack_x, swap(pack_x))
    x_numbers = [numbers_of(p) for p in x_packs]
    w_core, acc = run(
        "core_terms", (pack_c,), (core_number,), (later, near, far), 0, acc, flops=CORE_FLOPS
    )
    packs = (pack_own, pack_c, *x_packs)
    w_far, kron, acc = run(
        "beside_terms", x_packs, x_numbers, (later, near, far), 0, acc, every=packs
    )
    outer, acc = lax.optimization_barrier((outer, acc))
    quarter = (block, phys // slots * width)
    give_far, give_core, keep_x, keep = call(
        functools.partial(last_body, terms),
        tuple(jax.ShapeDtypeStruct(quarter, t) for t in (BF16, BF16, F32, F32)),
        [smem] * 4 + [vmem] * 11,
        [pltpu.VMEM((tiles, slots * one_pack, width), BF16), pltpu.VMEM((all_rows, width), BF16)],
        name="last_shard",
    )(
        own_number, core_number, *x_numbers, *packs, w_own, w_core, w_far, kron, acc, inner, outer
    )
    give = (keep_x + swap(give_far).astype(F32)).astype(BF16)
    taken = lax.ppermute(give, "mpo", ACROSS)
    return (keep + swap(give_core).astype(F32) + taken.astype(F32)).astype(BF16)


def solution(mesh):
    sizes = dict(mesh.shape)

    def on_device(
        wavefunction, left_blocks, right_blocks, site_terms, left_source, right_source, live_pairs
    ):
        columns = wavefunction.shape[1]
        terms, sectors, block, _ = left_blocks.shape
        phys, rights = site_terms.shape[1], right_blocks.shape[1]
        square = sizes["blk"] == 4 and sizes["mpo"] == 4 and sectors == 1 and rights == 2
        fits = columns == 4 * rights * block and phys == 16 and block == 128 and terms == 4
        step = by_states if square and fits else by_terms
        return step(
            wavefunction, left_blocks, right_blocks, site_terms, left_source, right_source, live_pairs
        )

    return jax.shard_map(
        on_device,
        mesh=mesh,
        in_specs=(
            P("rep", "blk"),
            P(("rep", "mpo"), "blk", None, None),
            P(("rep", "mpo"), None, None, None),
            P(("rep", "mpo"), None, None),
            P(("rep", "mpo"), None),
            P(("rep", "mpo"), None),
            P("rep", None),
        ),
        out_specs=P(("rep", "blk"), "mpo"),
        check_vma=False,
    )
```

time: 225 us -> 42.6 us (0.19)
  the two profiles are of different devices: /device:TPU:0 before, /device:TPU:18 now
where the time goes in v2:
time: 42.6 us; the launch traced here: 42.3 us
  waiting for transfers between devices  12.9 us (30%)
  starting transfers between devices  12.7 us (30%)
  Pallas kernels  11.1 us (26%)
  local copies, waits for them, and re-layouts  4.61 us (11%)
  other arithmetic  0.88 us (2%)
    ppermute x1, waiting for transfers between devices, by_states(): taken = lax.ppermute(give, 'mpo', ACROSS)  7.81 us
    pallas_call x4, Pallas kernels, run(): call(functools.partial(terms_body, terms, rights, phys, plan), tuple(shap...  7.41 us
    ppermute x1, starting transfers between devices, by_states(): outer = lax.ppermute(far, 'blk', OUTWARD)  6.37 us
    unnamed x12, local copies, waits for them, and re-layouts  4.61 us
    ppermute x1, waiting for transfers between devices, by_states(): far = lax.ppermute(mine, 'blk', FAR)  2.06 us
    ppermute x1, waiting for transfers between devices, by_states(): inner = lax.ppermute(later, 'blk', MIDDLE)  1.97 us
    ppermute x1, starting transfers between devices, by_states(): inner = lax.ppermute(later, 'blk', MIDDLE)  1.92 us
    pallas_call x1, Pallas kernels, by_states(): call(functools.partial(last_body, terms), tuple((jax.ShapeDtypeStruct(qua...  1.79 us
  transfers between devices with their start and end apart: 10, of which 4 were waited for; matrix products, arithmetic and copies ran while one was open for 0% of the time, Pallas kernels for 20%

profile of v2, /device:TPU:18, one launch (start us, length us, event | category | flops | bytes accessed | tf_op | source)
XLA Modules:
  0.0 42.3 jit_solution(11552038469261126761)
XLA Ops:
  0.0 1.0 %own_states.1.refs_2_.refs_8_ = bf16[512,256]{1,0:T(8,128)(2,1)S(1)} custom-call(bf16[512,1024]{1,0:T(8,128)(2,1)} %wave_ref.1), custom_call_target="tpu_custom_call" | custom-call | flops 1000 | bytes 1000 | tf_op jit(solution)/shard_map/own_states/pallas_call | solution.py:286
  1.0 0.4 collective-permute-start
  1.4 1.6 %collective-permute-start.1 = (bf16[512,256]{1,0:T(8,128)(2,1)S(1)}, bf16[512,256]{1,0:T(8,128)(2,1)S(1)}, u32[]{:S(2)}, u32[]{:S(2)}) collective-permute-start(bf16[512,256]{1,0:T(8,128)(2,1)S(1)} %own_states.1.refs_2_.refs_8_), channel_id=1, source_target_pairs={{0,4},{4,0},{8,12},{12,8},{1,5},{5,1},{9,13},{13,9},{2,6},{6,2},{1... | collective-permute-start | bytes 786440 | tf_op jit(solution)/shard_map/ppermute | solution.py:320
  2.9 0.0 copy-start
  2.9 0.9 %copy-done = bf16[4,2,128,128]{3,2,1,0:T(8,128)(2,1)S(1)} copy-done((bf16[4,2,128,128]{3,2,1,0:T(8,128)(2,1)S(1)}, bf16[4,2,128,128]{3,2,1,0:T(8,128)(2,1)}, u32[]{:S(2)}) %copy-start) | copy-done | bytes 262168
  3.9 0.0 copy-start.1
  3.9 0.9 %copy-done.1 = bf16[4,1,128,128]{3,2,1,0:T(8,128)(2,1)S(1)} copy-done((bf16[4,1,128,128]{3,2,1,0:T(8,128)(2,1)S(1)}, bf16[4,1,128,128]{3,2,1,0:T(8,128)(2,1)}, u32[]{:S(2)}) %copy-start.1) | copy-done | bytes 131096
  4.8 0.0 copy-start.2
  4.8 0.7 %copy-done.2 = bf16[4,16,16]{2,1,0:T(8,128)(2,1)S(1)} copy-done((bf16[4,16,16]{2,1,0:T(8,128)(2,1)S(1)}, bf16[4,16,16]{2,1,0:T(8,128)(2,1)}, u32[]{:S(2)}) %copy-start.2) | copy-done | bytes 2072
  5.5 0.0 copy-start.3
  5.5 0.7 %copy-done.3 = s32[4,4]{1,0:T(4,128)S(1)} copy-done((s32[4,4]{1,0:T(4,128)S(1)}, s32[4,4]{1,0:T(4,128)}, u32[]{:S(2)}) %copy-start.3) | copy-done | bytes 88
  6.2 0.0 copy-start.4
  6.2 0.7 %copy-done.4 = s32[4,2]{0,1:T(2,128)S(1)} copy-done((s32[4,2]{0,1:T(2,128)S(1)}, s32[4,2]{0,1:T(2,128)}, u32[]{:S(2)}) %copy-start.4) | copy-done | bytes 56
  6.9 0.0 copy-start.5
  6.9 0.7 %copy-done.5 = s32[4,2]{0,1:T(2,128)S(1)} copy-done((s32[4,2]{0,1:T(2,128)S(1)}, s32[4,2]{0,1:T(2,128)}, u32[]{:S(2)}) %copy-start.5) | copy-done | bytes 56
  7.6 1.0 %pack_operators.1.refs_1_.refs_4_ = bf16[1568,128]{1,0:T(8,128)(2,1)S(1)} custom-call(bf16[4,1,128,128]{3,2,1,0:T(8,128)(2,1)S(1)} %copy-done.1, bf16[4,2,128,128]{3,2,1,0:T(8,128)(2,1)S(1)} %copy-done, bf16[4,16,16]{2,1,0:T(8,128)(2,1)S(1)} %copy-done.2, s32[4,4]{1,0:T(4,128)S(1)} %copy-done.3, s32[2,4]{1,0:T(2,128)S(1)} %bitcast.2, s32[2,4]{1,0:T(2,128)S(1)} %bitcast.3), custom_call_target="tpu_custom_call" | custom-call | flops 1000 | bytes 1000 | tf_op jit(solution)/shard_map/pack_operators/pallas_call | solution.py:299
  8.6 0.6 %collective-permute-start.2 = (bf16[1568,128]{1,0:T(8,128)(2,1)S(1)}, bf16[1568,128]{1,0:T(8,128)(2,1)S(1)}, u32[]{:S(2)}, u32[]{:S(2)}) collective-permute-start(bf16[1568,128]{1,0:T(8,128)(2,1)S(1)} %pack_operators.1.refs_1_.refs_4_), channel_id=1, source_target_pairs={{0,2},{2,0},{1,3},{3,1},{4,6},{6,4},{5,7},{7,5},{8,10},{10,8},{9,1... | collective-permute-start | bytes 1204232 | tf_op jit(solution)/shard_map/ppermute | solution.py:321
  9.2 1.4 %own_terms_own.1 = (bf16[4,256,256]{2,1,0:T(8,128)(2,1)S(1)}, f32[8,256,256]{2,1,0:T(8,128)S(1)}) custom-call(s32[1,128]{1,0:T(1,128)S(1)} %slice_convert_fusion.1.live_ref.refs_0_, s32[1,128]{1,0:T(1,128)S(1)} %slice_convert_fusion.1.live_ref.refs_0_, bf16[1568,128]{1,0:T(8,128)(2,1)S(1)} %pack_operators.1.refs_1_.refs_4_, ...), custom_call_target="tpu_custom_call" | custom-call | flops 1000 | bytes 1000 | tf_op jit(solution)/shard_map/own_terms_own/pallas_call | solution.py:335
  10.5 2.1 %collective-permute-done.refs_3_.refs_4_.refs_10_ = bf16[512,256]{1,0:T(8,128)(2,1)S(1)} collective-permute-done((bf16[512,256]{1,0:T(8,128)(2,1)S(1)}, bf16[512,256]{1,0:T(8,128)(2,1)S(1)}, u32[]{:S(2)}, u32[]{:S(2)}) %collective-permute-start) | collective-permute-done | bytes 262176 | tf_op jit(solution)/shard_map/ppermute | solution.py:319
  12.6 6.4 %collective-permute-start.5 = (bf16[512,256]{1,0:T(8,128)(2,1)S(1)}, bf16[512,256]{1,0:T(8,128)(2,1)S(1)}, u32[]{:S(2)}, u32[]{:S(2)}) collective-permute-start(bf16[512,256]{1,0:T(8,128)(2,1)S(1)} %collective-permute-done.refs_3_.refs_4_.refs_10_), channel_id=1, source_target_pairs={{4,0},{8,12},{5,1},{9,13},{6,2},{10,14},{7,3},{11,15},{20,16},{24,... | collective-permute-start | bytes 786440 | tf_op jit(solution)/shard_map/ppermute | solution.py:347
  19.0 0.1 collective-permute-start.3
  19.1 1.9 %collective-permute-start.6 = (bf16[512,256]{1,0:T(8,128)(2,1)S(1)}, bf16[512,256]{1,0:T(8,128)(2,1)S(1)}, u32[]{:S(2)}, u32[]{:S(2)}) collective-permute-start(bf16[512,256]{1,0:T(8,128)(2,1)S(1)} %own_states.1.refs_2_.refs_8_), channel_id=1, source_target_pairs={{4,8},{8,4},{5,9},{9,5},{6,10},{10,6},{7,11},{11,7},{20,24},{24,20... | collective-permute-start | bytes 786440 | tf_op jit(solution)/shard_map/ppermute | solution.py:349
  21.0 0.0 collective-permute-done.1.refs_2_.refs_3_.refs_9_
  21.0 1.5 %own_terms.1.refs_5_ = f32[8,256,256]{2,1,0:T(8,128)S(1)} custom-call(s32[1,128]{1,0:T(1,128)S(1)} %slice_convert_fusion.1.live_ref.refs_0_, s32[1,128]{1,0:T(1,128)S(1)} %slice_convert_fusion.1.live_ref.refs_0_, bf16[1568,128]{1,0:T(8,128)(2,1)S(1)} %pack_operators.1.refs_1_.refs_4_, bf16[512,256]{1,0:T(8,128)(2,1)S(1)} %collective-permute-done.1.refs_2_.refs_3_.refs_9_, ...), custom_call_target="tpu_custom_call" | custom-call | flops 8000000000 | bytes 1000 | tf_op jit(solution)/shard_map/own_terms/pallas_call | solution.py:335
  22.5 0.0 collective-permute-done.2.refs_2_.refs_6_
  22.5 0.0 collective-permute-done.3.refs_1_.refs_5_
  22.5 0.6 %collective-permute-start.4 = (bf16[1568,128]{1,0:T(8,128)(2,1)S(1)}, bf16[1568,128]{1,0:T(8,128)(2,1)S(1)}, u32[]{:S(2)}, u32[]{:S(2)}) collective-permute-start(bf16[1568,128]{1,0:T(8,128)(2,1)S(1)} %collective-permute-done.2.refs_2_.refs_6_), channel_id=1, source_target_pairs={{0,1},{1,0},{2,3},{3,2},{4,5},{5,4},{6,7},{7,6},{8,9},{9,8},{10,11... | collective-permute-start | bytes 1204232 | tf_op jit(solution)/shard_map/ppermute | solution.py:297
  23.1 1.8 %core_terms.1 = (bf16[4,256,256]{2,1,0:T(8,128)(2,1)S(1)}, f32[8,256,256]{2,1,0:T(8,128)S(1)}) custom-call(s32[1,128]{1,0:T(1,128)S(1)} %slice_convert_fusion.1.live_ref.refs_0_, s32[1,128]{1,0:T(1,128)S(1)} %get-tuple-element.48.refs_0_.refs_1_, bf16[1568,128]{1,0:T(8,128)(2,1)S(1)} %collective-permute-done.3.refs_1_.refs_5_, ...), custom_call_target="tpu_custom_call" | custom-call | flops 3000000000 | bytes 1000 | tf_op jit(solution)/shard_map/core_terms/pallas_call | solution.py:335
  24.9 0.0 collective-permute-done.4.refs_3_.refs_7_
  24.9 2.8 %beside_terms.1 = (bf16[8,256,256]{2,1,0:T(8,128)(2,1)S(1)}, bf16[256,256]{1,0:T(8,128)(2,1)S(1)}, f32[8,256,256]{2,1,0:T(8,128)S(1)}) custom-call(s32[1,128]{1,0:T(1,128)S(1)} %slice_convert_fusion.1.live_ref.refs_0_, s32[1,128]{1,0:T(1,128)S(1)} %get-tuple-element.47.refs_0_.refs_2_, s32[1,128]{1,0:T(1,128)S(1)} %slice_convert_fusion.refs_1_.refs_3_, ...), custom_call_target="tpu_custom_call" | custom-call | flops 1000 | bytes 1000 | tf_op jit(solution)/shard_map/beside_terms/pallas_call | solution.py:335
  27.7 0.0 collective-permute-done.5.refs_14_
  27.7 2.0 %collective-permute-done.6.refs_13_ = bf16[512,256]{1,0:T(8,128)(2,1)S(1)} collective-permute-done((bf16[512,256]{1,0:T(8,128)(2,1)S(1)}, bf16[512,256]{1,0:T(8,128)(2,1)S(1)}, u32[]{:S(2)}, u32[]{:S(2)}) %collective-permute-start.6) | collective-permute-done | bytes 262176 | tf_op jit(solution)/shard_map/ppermute | solution.py:349
  29.6 1.8 %last_shard.1 = (bf16[128,1024]{1,0:T(8,128)(2,1)S(1)}, bf16[128,1024]{1,0:T(8,128)(2,1)S(1)}, f32[128,1024]{1,0:T(8,128)S(1)}, f32[128,1024]{1,0:T(8,128)S(1)}) custom-call(s32[1,128]{1,0:T(1,128)S(1)} %slice_convert_fusion.1.live_ref.refs_0_, s32[1,128]{1,0:T(1,128)S(1)} %get-tuple-element.48.refs_0_.refs_1_, ...), custom_call_target="tpu_custom_call" | custom-call | flops 1000 | bytes 1000 | tf_op jit(solution)/shard_map/last_shard/pallas_call | solution.py:367
  31.4 0.1 collective-permute-start.8
  31.5 0.5 %collective-permute-start.7 = (bf16[128,1024]{1,0:T(8,128)(2,1)S(1)}, bf16[128,1024]{1,0:T(8,128)(2,1)S(1)}, u32[]{:S(2)}, u32[]{:S(2)}) collective-permute-start(bf16[128,1024]{1,0:T(8,128)(2,1)S(1)} %get-tuple-element.44), channel_id=1, source_target_pairs={{0,1},{1,0},{2,3},{3,2},{4,5},{5,4},{6,7},{7,6},{8,9},{9,8},{10,11... | collective-permute-start | bytes 786440 | tf_op jit(solution)/shard_map/ppermute | solution.py:297
  32.0 1.0 %collective-permute-done.8 = bf16[128,1024]{1,0:T(8,128)(2,1)S(1)} collective-permute-done((bf16[128,1024]{1,0:T(8,128)(2,1)S(1)}, bf16[128,1024]{1,0:T(8,128)(2,1)S(1)}, u32[]{:S(2)}, u32[]{:S(2)}) %collective-permute-start.8) | collective-permute-done | bytes 262176 | tf_op jit(solution)/shard_map/ppermute | solution.py:297
  33.0 0.1 add_convert_fusion.1
  33.1 0.6 %collective-permute-start.9 = (bf16[128,1024]{1,0:T(8,128)(2,1)S(1)}, bf16[128,1024]{1,0:T(8,128)(2,1)S(1)}, u32[]{:S(2)}, u32[]{:S(2)}) collective-permute-start(bf16[128,1024]{1,0:T(8,128)(2,1)S(1)} %add_convert_fusion.1), channel_id=1, source_target_pairs={{0,2},{2,0},{1,3},{3,1},{4,6},{6,4},{5,7},{7,5},{8,10},{10,8},{9,1... | collective-permute-start | bytes 786440 | tf_op jit(solution)/shard_map/ppermute | solution.py:377
  33.7 0.0 collective-permute-done.7
  33.7 7.8 %collective-permute-done.9 = bf16[128,1024]{1,0:T(8,128)(2,1)S(1)} collective-permute-done((bf16[128,1024]{1,0:T(8,128)(2,1)S(1)}, bf16[128,1024]{1,0:T(8,128)(2,1)S(1)}, u32[]{:S(2)}, u32[]{:S(2)}) %collective-permute-start.9) | collective-permute-done | bytes 262176 | tf_op jit(solution)/shard_map/ppermute | solution.py:377
  41.5 0.8 %add_convert_fusion = bf16[128,1024]{1,0:T(8,128)(2,1)} fusion(bf16[128,1024]{1,0:T(8,128)(2,1)S(1)} %collective-permute-done.9, f32[128,1024]{1,0:T(8,128)S(1)} %get-tuple-element.43, bf16[128,1024]{1,0:T(8,128)(2,1)S(1)} %collective-permute-done.7), kind=kLoop, calls=%fused_computation | loop fusion | flops 655360 | bytes 1310720 | tf_op jit(solution)/shard_map/convert_element_type | solution.py:378
  (3 shorter events, 0.0 us)
Async XLA Ops:
  1.0 11.6 %collective-permute-start = (bf16[512,256]{1,0:T(8,128)(2,1)S(1)}, bf16[512,256]{1,0:T(8,128)(2,1)S(1)}, u32[]{:S(2)}, u32[]{:S(2)}) collective-permute-start(bf16[512,256]{1,0:T(8,128)(2,1)S(1)} %own_states.1.refs_2_.refs_8_), channel_id=1, source_target_pairs={{0,8},{8,0},{4,12},{12,4},{1,9},{9,1},{5,13},{13,5},{2,10},{10,2},... | collective-permute-start | bytes 786440 | tf_op jit(solution)/shard_map/ppermute | solution.py:319
  1.4 19.6 %collective-permute-start.1 = (bf16[512,256]{1,0:T(8,128)(2,1)S(1)}, bf16[512,256]{1,0:T(8,128)(2,1)S(1)}, u32[]{:S(2)}, u32[]{:S(2)}) collective-permute-start(bf16[512,256]{1,0:T(8,128)(2,1)S(1)} %own_states.1.refs_2_.refs_8_), channel_id=1, source_target_pairs={{0,4},{4,0},{8,12},{12,8},{1,5},{5,1},{9,13},{13,9},{2,6},{6,2},{1... | collective-permute-start | bytes 786440 | tf_op jit(solution)/shard_map/ppermute | solution.py:320
  2.9 0.9 %copy-start = (bf16[4,2,128,128]{3,2,1,0:T(8,128)(2,1)S(1)}, bf16[4,2,128,128]{3,2,1,0:T(8,128)(2,1)}, u32[]{:S(2)}) copy-start(bf16[4,2,128,128]{3,2,1,0:T(8,128)(2,1)} %right_hbm.1) | copy-start | bytes 786436
  3.9 0.9 %copy-start.1 = (bf16[4,1,128,128]{3,2,1,0:T(8,128)(2,1)S(1)}, bf16[4,1,128,128]{3,2,1,0:T(8,128)(2,1)}, u32[]{:S(2)}) copy-start(bf16[4,1,128,128]{3,2,1,0:T(8,128)(2,1)} %left_hbm.1) | copy-start | bytes 393220
  4.8 0.7 %copy-start.2 = (bf16[4,16,16]{2,1,0:T(8,128)(2,1)S(1)}, bf16[4,16,16]{2,1,0:T(8,128)(2,1)}, u32[]{:S(2)}) copy-start(bf16[4,16,16]{2,1,0:T(8,128)(2,1)} %site_hbm.1) | copy-start | bytes 6148
  5.5 0.7 %copy-start.3 = (s32[4,4]{1,0:T(4,128)S(1)}, s32[4,4]{1,0:T(4,128)}, u32[]{:S(2)}) copy-start(s32[4,4]{1,0:T(4,128)} %sources_hbm.1) | copy-start | bytes 196
  6.2 0.7 %copy-start.4 = (s32[4,2]{0,1:T(2,128)S(1)}, s32[4,2]{0,1:T(2,128)}, u32[]{:S(2)}) copy-start(s32[4,2]{0,1:T(2,128)} %param.12) | copy-start | bytes 100
  6.9 0.7 %copy-start.5 = (s32[4,2]{0,1:T(2,128)S(1)}, s32[4,2]{0,1:T(2,128)}, u32[]{:S(2)}) copy-start(s32[4,2]{0,1:T(2,128)} %param.13) | copy-start | bytes 100
  8.6 13.9 %collective-permute-start.2 = (bf16[1568,128]{1,0:T(8,128)(2,1)S(1)}, bf16[1568,128]{1,0:T(8,128)(2,1)S(1)}, u32[]{:S(2)}, u32[]{:S(2)}) collective-permute-start(bf16[1568,128]{1,0:T(8,128)(2,1)S(1)} %pack_operators.1.refs_1_.refs_4_), channel_id=1, source_target_pairs={{0,2},{2,0},{1,3},{3,1},{4,6},{6,4},{5,7},{7,5},{8,10},{10,8},{9,1... | collective-permute-start | bytes 1204232 | tf_op jit(solution)/shard_map/ppermute | solution.py:321
  12.6 15.1 %collective-permute-start.5 = (bf16[512,256]{1,0:T(8,128)(2,1)S(1)}, bf16[512,256]{1,0:T(8,128)(2,1)S(1)}, u32[]{:S(2)}, u32[]{:S(2)}) collective-permute-start(bf16[512,256]{1,0:T(8,128)(2,1)S(1)} %collective-permute-done.refs_3_.refs_4_.refs_10_), channel_id=1, source_target_pairs={{4,0},{8,12},{5,1},{9,13},{6,2},{10,14},{7,3},{11,15},{20,16},{24,... | collective-permute-start | bytes 786440 | tf_op jit(solution)/shard_map/ppermute | solution.py:347
  19.0 3.5 %collective-permute-start.3 = (bf16[1568,128]{1,0:T(8,128)(2,1)S(1)}, bf16[1568,128]{1,0:T(8,128)(2,1)S(1)}, u32[]{:S(2)}, u32[]{:S(2)}) collective-permute-start(bf16[1568,128]{1,0:T(8,128)(2,1)S(1)} %pack_operators.1.refs_1_.refs_4_), channel_id=1, source_target_pairs={{0,1},{1,0},{2,3},{3,2},{4,5},{5,4},{6,7},{7,6},{8,9},{9,8},{10,11... | collective-permute-start | bytes 1204232 | tf_op jit(solution)/shard_map/ppermute | solution.py:297
  19.1 10.6 %collective-permute-start.6 = (bf16[512,256]{1,0:T(8,128)(2,1)S(1)}, bf16[512,256]{1,0:T(8,128)(2,1)S(1)}, u32[]{:S(2)}, u32[]{:S(2)}) collective-permute-start(bf16[512,256]{1,0:T(8,128)(2,1)S(1)} %own_states.1.refs_2_.refs_8_), channel_id=1, source_target_pairs={{4,8},{8,4},{5,9},{9,5},{6,10},{10,6},{7,11},{11,7},{20,24},{24,20... | collective-permute-start | bytes 786440 | tf_op jit(solution)/shard_map/ppermute | solution.py:349
  22.5 2.3 %collective-permute-start.4 = (bf16[1568,128]{1,0:T(8,128)(2,1)S(1)}, bf16[1568,128]{1,0:T(8,128)(2,1)S(1)}, u32[]{:S(2)}, u32[]{:S(2)}) collective-permute-start(bf16[1568,128]{1,0:T(8,128)(2,1)S(1)} %collective-permute-done.2.refs_2_.refs_6_), channel_id=1, source_target_pairs={{0,1},{1,0},{2,3},{3,2},{4,5},{5,4},{6,7},{7,6},{8,9},{9,8},{10,11... | collective-permute-start | bytes 1204232 | tf_op jit(solution)/shard_map/ppermute | solution.py:297
  31.4 1.6 %collective-permute-start.8 = (bf16[128,1024]{1,0:T(8,128)(2,1)S(1)}, bf16[128,1024]{1,0:T(8,128)(2,1)S(1)}, u32[]{:S(2)}, u32[]{:S(2)}) collective-permute-start(bf16[128,1024]{1,0:T(8,128)(2,1)S(1)} %get-tuple-element.46), channel_id=1, source_target_pairs={{0,1},{1,0},{2,3},{3,2},{4,5},{5,4},{6,7},{7,6},{8,9},{9,8},{10,11... | collective-permute-start | bytes 786440 | tf_op jit(solution)/shard_map/ppermute | solution.py:297
  31.5 2.2 %collective-permute-start.7 = (bf16[128,1024]{1,0:T(8,128)(2,1)S(1)}, bf16[128,1024]{1,0:T(8,128)(2,1)S(1)}, u32[]{:S(2)}, u32[]{:S(2)}) collective-permute-start(bf16[128,1024]{1,0:T(8,128)(2,1)S(1)} %get-tuple-element.44), channel_id=1, source_target_pairs={{0,1},{1,0},{2,3},{3,2},{4,5},{5,4},{6,7},{7,6},{8,9},{9,8},{10,11... | collective-permute-start | bytes 786440 | tf_op jit(solution)/shard_map/ppermute | solution.py:297
  33.1 8.4 %collective-permute-start.9 = (bf16[128,1024]{1,0:T(8,128)(2,1)S(1)}, bf16[128,1024]{1,0:T(8,128)(2,1)S(1)}, u32[]{:S(2)}, u32[]{:S(2)}) collective-permute-start(bf16[128,1024]{1,0:T(8,128)(2,1)S(1)} %add_convert_fusion.1), channel_id=1, source_target_pairs={{0,2},{2,0},{1,3},{3,1},{4,6},{6,4},{5,7},{7,5},{8,10},{10,8},{9,1... | collective-permute-start | bytes 786440 | tf_op jit(solution)/shard_map/ppermute | solution.py:377

commit v3 on v2

--- a/solution.py
+++ b/solution.py
@@ -10,14 +10,14 @@
 F32 = jnp.float32
 BF16 = jnp.bfloat16
 VMEM_BYTES = 32 * 1024 * 1024
-SLICE_BYTES = 53 * 1024 * 1024
-PACK_BYTES = 53 * 1024 * 1024
+SLICE_BYTES = 32 * 1024 * 1024
+PACK_BYTES = 32 * 1024 * 1024
+OWN_FLOPS = 1000
 CHIP_FLOPS = int(8e9)
+OTHER_FLOPS = 1000
 CORE_FLOPS = int(3e9)
 NEAR = ((0, 1), (1, 0), (2, 3), (3, 2))
 FAR = ((0, 2), (2, 0), (1, 3), (3, 1))
-MIDDLE = ((1, 2), (2, 1))
-OUTWARD = ((1, 0), (2, 3))
 CORE = ((0, 1), (1, 0), (2, 3), (3, 2))
 ACROSS = ((0, 2), (2, 0), (1, 3), (3, 1))
 SUB = 16
@@ -136,22 +136,21 @@
         copy.wait()
 
 
-def right_matrices(terms, rights, numbers, alive, packs, w_ref):
-    block = packs[0].shape[-1]
-    for k in range(len(packs)):
-        for w in range(terms):
-            for b in range(rights):
-                start = (terms + w * rights + b) * block
-                turned = packs[k][start : start + block, :]
-                source = numbers[k, terms + w * rights + b]
-                for r in range(rights):
-                    keep = jnp.logical_and(source == r, alive[b] != 0)
-                    w_ref[k * terms + w, r * block : (r + 1) * block, b * block : (b + 1) * block] = (
-                        jnp.where(keep, turned, jnp.zeros_like(turned))
-                    )
-
-
-def spread_site(terms, rights, phys, packs, first, kron_ref):
+def right_matrices(terms, rights, numbers, alive, pack, w_ref):
+    block = pack.shape[-1]
+    for w in range(terms):
+        for b in range(rights):
+            start = (terms + w * rights + b) * block
+            turned = pack[start : start + block, :]
+            source = numbers[0, terms + w * rights + b]
+            for r in range(rights):
+                keep = jnp.logical_and(source == r, alive[b] != 0)
+                w_ref[w, r * block : (r + 1) * block, b * block : (b + 1) * block] = jnp.where(
+                    keep, turned, jnp.zeros_like(turned)
+                )
+
+
+def spread_site(terms, rights, phys, packs, chunks, kron_ref):
     block = packs[0].shape[-1]
     me, own_blk = lax.axis_index("mpo"), lax.axis_index("blk")
     site_at = (1 + rights) * terms * block
@@ -165,14 +164,14 @@
     pick_s = jnp.where(
         lax.broadcasted_iota(jnp.int32, (rows, phys), 1) == swant, 1.0, 0.0
     ).astype(BF16)
-    column = lax.broadcasted_iota(jnp.int32, (here, depth), 1)
-    slot = column >> 4
-    shard, pack, term = slot // (terms * len(packs)), (slot // terms) % len(packs), slot % terms
-    state = lax.bitwise_xor(own_blk, shard + first) * quarter + me
+    slot = lax.broadcasted_iota(jnp.int32, (1, depth), 1) >> 4
+    want = jnp.zeros((1, depth), jnp.int32)
+    for n, (shard, pack) in enumerate(chunks):
+        state = lax.bitwise_xor(own_blk, shard) * quarter + me
+        spot = pack * block + (slot - n * terms) * phys + state
+        want = jnp.where(jnp.logical_and(slot >= n * terms, slot < (n + 1) * terms), spot, want)
     pick_t = jnp.where(
-        lax.broadcasted_iota(jnp.int32, (here, depth), 0) == pack * block + term * phys + state,
-        1.0,
-        0.0,
+        lax.broadcasted_iota(jnp.int32, (here, depth), 0) == want, 1.0, 0.0
     ).astype(BF16)
     spread = matmul(pick_s, matmul(site, pick_t).astype(BF16))
     diagonal = (lax.broadcasted_iota(jnp.int32, (rows, depth), 0) & 15) == (
@@ -181,76 +180,70 @@
     kron_ref[...] = jnp.where(diagonal, spread, 0.0).astype(BF16)
 
 
-def turn_shard(terms, numbers, packs, w_ref, shard, y_ref, at):
-    block = packs[0].shape[-1]
+def turn_shard(terms, numbers, pack, w_ref, shard, y_ref, at):
+    block = pack.shape[-1]
     tiles = y_ref.shape[0]
-    for k in range(len(packs)):
-        for w in range(terms):
-            row = pl.multiple_of(numbers[k, w] * block, block)
-            left = packs[k][w * block : (w + 1) * block, :]
-            carried = matmul(left, shard[pl.ds(row, block), :]).astype(BF16)
-            y = matmul(carried, w_ref[k * terms + w]).astype(BF16)
-            y_ref[:, at : at + SUB, :] = y.reshape(tiles, SUB, y.shape[-1])
-            at += SUB
-    return at
-
-
-class Numbers:
-    def __init__(self, refs):
-        self.refs = refs
-
-    def __getitem__(self, at):
-        return self.refs[at[0]][0, at[1]]
+    for w in range(terms):
+        row = pl.multiple_of(numbers[0, w] * block, block)
+        left = pack[w * block : (w + 1) * block, :]
+        carried = matmul(left, shard[pl.ds(row, block), :]).astype(BF16)
+        y = matmul(carried, w_ref[w]).astype(BF16)
+        y_ref[:, at + w * SUB : at + (w + 1) * SUB, :] = y.reshape(tiles, SUB, y.shape[-1])
+
+
+class Plan:
+    def __init__(self, packs, chunks, made=(), before=True, prepare_last=False, last=False):
+        self.packs, self.chunks, self.made = packs, chunks, made
+        self.before, self.prepare_last, self.last = before, prepare_last, last
+        self.used = sorted({k for _, k in chunks})
+        self.given = [k for k in self.used if k not in made]
+        self.shards = sorted({q for q, _ in chunks})
 
 
 def terms_body(terms, rights, phys, plan, live_ref, *refs):
-    packs_n, shards_n, first, make, before, all_n = plan
-    number_refs, refs = refs[:packs_n], refs[packs_n:]
-    packs, refs = refs[:packs_n], refs[packs_n:]
-    others, refs = refs[:all_n], refs[all_n:]
-    shards, refs = refs[:shards_n], refs[shards_n:]
-    if not make:
-        w_ref, refs = refs[0], refs[1:]
-    acc_in, refs = (refs[0], refs[1:]) if before else (None, refs)
-    numbers = Numbers(number_refs)
-    if make:
-        w_ref, refs = refs[0], refs[1:]
-        alive = [live_ref[0, terms * (1 + rights) + b] for b in range(rights)]
-        right_matrices(terms, rights, numbers, alive, packs, w_ref)
-    if all_n:
-        spread_site(terms, rights, phys, others, 3, refs[0])
-        refs = refs[1:]
-    acc_ref, kron_ref, y_ref = refs
-    spread_site(terms, rights, phys, packs, first, kron_ref)
-    at = 0
-    for shard in shards:
-        at = turn_shard(terms, numbers, packs, w_ref, shard, y_ref, at)
+    refs = list(refs)
+
+    def take(count):
+        taken, refs[:] = refs[:count], refs[count:]
+        return taken
+
+    numbers, packs = take(plan.packs), take(plan.packs)
+    w_refs = dict(zip(plan.given, take(len(plan.given))))
+    shards = dict(zip(plan.shards, take(len(plan.shards))))
+    acc_in = take(1)[0] if plan.before else None
+    kron_ref = take(1)[0] if plan.last else None
+    w_refs.update(zip(plan.made, take(len(plan.made))))
+    if plan.prepare_last:
+        spread_site(terms, rights, phys, packs, [(3, k) for k in range(plan.packs)], take(1)[0])
+    targets = take(4 if plan.last else 1)
+    y_ref = take(1)[0]
+    if not plan.last:
+        kron_ref = take(1)[0]
+        spread_site(terms, rights, phys, packs, plan.chunks, kron_ref)
+    alive = [live_ref[0, terms * (1 + rights) + b] for b in range(rights)]
+    for k in plan.made:
+        right_matrices(terms, rights, numbers[k], alive, packs[k], w_refs[k])
+    for n, (q, k) in enumerate(plan.chunks):
+        turn_shard(terms, numbers[k], packs[k], w_refs[k], shards[q], y_ref, n * terms * SUB)
     for i in range(y_ref.shape[0]):
         total = matmul(kron_ref[...], y_ref[i])
-        acc_ref[i] = total if acc_in is None else total + acc_in[i]
-
-
-def last_body(terms, *refs):
-    number_refs, packs, (w_own, w_core, w_far, kron_ref, acc_in) = refs[:4], refs[4:8], refs[8:13]
-    inner, outer = refs[13:15]
-    quarters, (y_ref, shard_ref) = refs[15:19], refs[19:]
-    own_blk = lax.axis_index("blk")
-    at_end = jnp.logical_or(own_blk == 0, own_blk == 3)
-    shard_ref[...] = jnp.where(at_end, outer[...], inner[...])
-    at = 0
-    for here, w_ref in (((0,), w_own), ((1,), w_core), ((2, 3), w_far)):
-        numbers = Numbers([number_refs[k] for k in here])
-        at = turn_shard(terms, numbers, [packs[k] for k in here], w_ref, shard_ref, y_ref, at)
-    width = w_own.shape[-1]
-    for i in range(y_ref.shape[0]):
-        total = matmul(kron_ref[...], y_ref[i]) + acc_in[i]
+        if plan.before:
+            total = total + acc_in[i]
+        if not plan.last:
+            targets[0][i] = total
+            continue
+        width = total.shape[1]
         count = total.shape[0] // SUB // 4
-        for n, target in enumerate(quarters):
+        for n, target in enumerate(targets):
             for m in range(count):
                 start = (n * count + m) * SUB
                 target[i * SUB : (i + 1) * SUB, m * width : (m + 1) * width] = total[
                     start : start + SUB, :
                 ].astype(target.dtype)
+
+
+def in_hbm(x):
+    return pltpu.with_memory_space_constraint(x, pltpu.HBM)
 
 
 def call(body, out_shape, in_specs, scratch=(), out_specs=None, name=None, vmem=VMEM_BYTES, flops=1000):
@@ -291,7 +284,7 @@
         out_specs=vmem,
         name="own_states",
         vmem=SLICE_BYTES,
-    )(wavefunction)
+    )(in_hbm(wavefunction))
 
     def swap(x):
         return lax.ppermute(x, "mpo", CORE)
@@ -311,67 +304,101 @@
         out_specs=vmem,
         name="pack_operators",
         vmem=PACK_BYTES,
-    )(left_blocks, right_blocks, site_terms, left_source, right_source.T, live_pairs.T)
+    )(
+        *[
+            in_hbm(x)
+            for x in (
+                left_blocks, right_blocks, site_terms, left_source, right_source.T, live_pairs.T
+            )
+        ]
+    )
 
     def numbers_of(p):
         return p[pack_rows - SUB : pack_rows - SUB + 1, :].astype(jnp.int32)
 
-    far = lax.ppermute(mine, "blk", FAR)
-    near = lax.ppermute(mine, "blk", NEAR)
-    pack_x = lax.ppermute(pack, "mpo", ACROSS)
-    acc_shape = jax.ShapeDtypeStruct((tiles, rows, width), F32)
     one_pack = terms * SUB
-
-    def run(name, packs, numbers, shards, first, acc, w=None, every=(), flops=1000):
-        plan = (len(packs), len(shards), first, w is None, acc is not None, len(every))
-        depth = len(packs) * len(shards) * one_pack
-        shapes = [acc_shape]
-        if every:
-            shapes.insert(0, jax.ShapeDtypeStruct((rows, len(every) * one_pack), BF16))
-        if w is None:
-            shapes.insert(0, jax.ShapeDtypeStruct((len(packs) * terms, width, width), BF16))
-        arrays = [*packs, *every, *shards]
-        arrays += [a for a in (w, acc) if a is not None]
+    quarter = (block, phys // slots * width)
+
+    def run(name, plan, packs, numbers, shards, acc=None, w=(), kron=None, flops=1000):
+        depth = len(plan.chunks) * one_pack
+        shapes = [jax.ShapeDtypeStruct((terms, width, width), BF16) for _ in plan.made]
+        if plan.prepare_last:
+            shapes.append(jax.ShapeDtypeStruct((rows, len(packs) * one_pack), BF16))
+        if plan.last:
+            shapes += [jax.ShapeDtypeStruct(quarter, t) for t in (BF16, BF16, F32, F32)]
+        else:
+            shapes.append(jax.ShapeDtypeStruct((tiles, rows, width), F32))
+        arrays = [*packs, *w, *shards] + [a for a in (acc, kron) if a is not None]
+        scratch = [pltpu.VMEM((tiles, depth, width), BF16)]
+        if not plan.last:
+            scratch.append(pltpu.VMEM((rows, depth), BF16))
         return call(
             functools.partial(terms_body, terms, rights, phys, plan),
             tuple(shapes),
             [smem] * (1 + len(numbers)) + [vmem] * len(arrays),
-            [pltpu.VMEM((rows, depth), BF16), pltpu.VMEM((tiles, depth, width), BF16)],
+            scratch,
             name=name,
             flops=flops,
-        )(own_number, *numbers, *arrays)
-
-    own_number = numbers_of(pack)
-    w_own, acc = run("own_terms_own", (pack,), (own_number,), (mine,), 0, None)
-    far, acc = lax.optimization_barrier((far, acc))
-    outer = lax.ppermute(far, "blk", OUTWARD)
-    far, later, pack_own = lax.optimization_barrier((far, mine, pack))
-    inner = lax.ppermute(later, "blk", MIDDLE)
-    pack_c = swap(pack_own)
+        )(numbers[0], *numbers, *arrays)
+
+    far = lax.ppermute(mine, "blk", FAR)
+    near = lax.ppermute(mine, "blk", NEAR)
+    pack_x = lax.ppermute(pack, "mpo", ACROSS)
+    number = numbers_of(pack)
+    w_own, acc = run(
+        "own_pack_own_shard",
+        Plan(1, [(0, 0)], made=(0,), before=False),
+        (pack,),
+        (number,),
+        (mine,),
+        flops=OWN_FLOPS,
+    )
+    far, acc, pack, mine = lax.optimization_barrier((far, acc, pack, mine))
+    farthest = lax.ppermute(far, "blk", NEAR)
+    pack_c = swap(pack)
     (acc,) = run(
-        "own_terms", (pack_own,), (own_number,), (near, far), 1, acc, w=w_own, flops=CHIP_FLOPS
+        "own_pack_near_far",
+        Plan(1, [(1, 0), (2, 0)]),
+        (pack,),
+        (number,),
+        (near, far),
+        acc,
+        (w_own,),
+        flops=CHIP_FLOPS,
     )
     acc, pack_x, pack_c = lax.optimization_barrier((acc, pack_x, pack_c))
-    core_number = numbers_of(pack_c)
+    number_c = numbers_of(pack_c)
     x_packs = (pack_x, swap(pack_x))
     x_numbers = [numbers_of(p) for p in x_packs]
     w_core, acc = run(
-        "core_terms", (pack_c,), (core_number,), (later, near, far), 0, acc, flops=CORE_FLOPS
-    )
-    packs = (pack_own, pack_c, *x_packs)
-    w_far, kron, acc = run(
-        "beside_terms", x_packs, x_numbers, (later, near, far), 0, acc, every=packs
-    )
-    outer, acc = lax.optimization_barrier((outer, acc))
-    quarter = (block, phys // slots * width)
-    give_far, give_core, keep_x, keep = call(
-        functools.partial(last_body, terms),
-        tuple(jax.ShapeDtypeStruct(quarter, t) for t in (BF16, BF16, F32, F32)),
-        [smem] * 4 + [vmem] * 11,
-        [pltpu.VMEM((tiles, slots * one_pack, width), BF16), pltpu.VMEM((all_rows, width), BF16)],
-        name="last_shard",
-    )(
-        own_number, core_number, *x_numbers, *packs, w_own, w_core, w_far, kron, acc, inner, outer
+        "core_pack",
+        Plan(1, [(0, 0), (1, 0), (2, 0)], made=(0,)),
+        (pack_c,),
+        (number_c,),
+        (mine, near, far),
+        acc,
+        flops=CORE_FLOPS,
+    )
+    packs, numbers = (pack, pack_c, *x_packs), (number, number_c, *x_numbers)
+    w_x, w_xc, kron, acc = run(
+        "other_packs",
+        Plan(4, [(q, k) for q in (0, 1, 2) for k in (2, 3)], made=(2, 3), prepare_last=True),
+        packs,
+        numbers,
+        (mine, near, far),
+        acc,
+        flops=OTHER_FLOPS,
+    )
+    farthest, acc = lax.optimization_barrier((farthest, acc))
+    give_far, give_core, keep_x, keep = run(
+        "third_shard",
+        Plan(4, [(3, k) for k in range(4)], last=True),
+        packs,
+        numbers,
+        (farthest,),
+        acc,
+        (w_own, w_core, w_x, w_xc),
+        kron,
     )
     give = (keep_x + swap(give_far).astype(F32)).astype(BF16)
     taken = lax.ppermute(give, "mpo", ACROSS)

time: 42.6 us -> 38.6 us (0.906)
  the two profiles are of different devices: /device:TPU:18 before, /device:TPU:0 now
where the time goes in v3:
time: 38.6 us; the launch traced here: 38.5 us
  waiting for transfers between devices  15.8 us (41%)
  Pallas kernels  11.4 us (30%)
  starting transfers between devices  10.3 us (27%)
  other arithmetic  0.88 us (2%)
    pallas_call x5, Pallas kernels, run(): call(functools.partial(terms_body, terms, rights, phys, plan), tuple(shap...  9.21 us
    ppermute x1, waiting for transfers between devices, by_states(): taken = lax.ppermute(give, 'mpo', ACROSS)  6.8 us
    ppermute x1, waiting for transfers between devices, by_states(): far = lax.ppermute(mine, 'blk', FAR)  6.29 us
    ppermute x1, starting transfers between devices, by_states(): far = lax.ppermute(mine, 'blk', FAR)  4.1 us
    ppermute x1, waiting for transfers between devices, by_states(): farthest = lax.ppermute(far, 'blk', NEAR)  1.68 us
    ppermute x1, starting transfers between devices, by_states(): taken = lax.ppermute(give, 'mpo', ACROSS)  1.61 us
    ppermute x1, starting transfers between devices, by_states(): near = lax.ppermute(mine, 'blk', NEAR)  1.58 us
    ppermute x1, starting transfers between devices, by_states(): pack_x = lax.ppermute(pack, 'mpo', ACROSS)  1.56 us
  transfers between devices with their start and end apart: 9, of which 4 were waited for; matrix products, arithmetic and copies ran while one was open for 0% of the time, Pallas kernels for 22%

profile of v3, /device:TPU:0, one launch (start us, length us, event | category | flops | bytes accessed | tf_op | source)
XLA Modules:
  0.0 38.5 jit_solution(13394191402647070697)
XLA Ops:
  0.0 1.0 %own_states.1.refs_2_.refs_8_ = bf16[512,256]{1,0:T(8,128)(2,1)S(1)} custom-call(bf16[512,1024]{1,0:T(8,128)(2,1)} %wave_ref.1), custom_call_target="tpu_custom_call" | custom-call | flops 1000 | bytes 1000 | tf_op jit(solution)/shard_map/own_states/pallas_call | solution.py:279
  1.0 4.1 %collective-permute-start = (bf16[512,256]{1,0:T(8,128)(2,1)S(1)}, bf16[512,256]{1,0:T(8,128)(2,1)S(1)}, u32[]{:S(2)}, u32[]{:S(2)}) collective-permute-start(bf16[512,256]{1,0:T(8,128)(2,1)S(1)} %own_states.1.refs_2_.refs_8_), channel_id=1, source_target_pairs={{0,8},{8,0},{4,12},{12,4},{1,9},{9,1},{5,13},{13,5},{2,10},{10,2},... | collective-permute-start | bytes 786440 | tf_op jit(solution)/shard_map/ppermute | solution.py:344
  5.1 1.6 %collective-permute-start.1 = (bf16[512,256]{1,0:T(8,128)(2,1)S(1)}, bf16[512,256]{1,0:T(8,128)(2,1)S(1)}, u32[]{:S(2)}, u32[]{:S(2)}) collective-permute-start(bf16[512,256]{1,0:T(8,128)(2,1)S(1)} %own_states.1.refs_2_.refs_8_), channel_id=1, source_target_pairs={{0,4},{4,0},{8,12},{12,8},{1,5},{5,1},{9,13},{13,9},{2,6},{6,2},{1... | collective-permute-start | bytes 786440 | tf_op jit(solution)/shard_map/ppermute | solution.py:345
  6.6 1.2 %pack_operators.1.refs_1_.refs_4_ = bf16[1568,128]{1,0:T(8,128)(2,1)S(1)} custom-call(bf16[4,1,128,128]{3,2,1,0:T(8,128)(2,1)} %left_hbm.1, bf16[4,2,128,128]{3,2,1,0:T(8,128)(2,1)} %right_hbm.1, bf16[4,16,16]{2,1,0:T(8,128)(2,1)} %site_hbm.1, s32[4,4]{1,0:T(4,128)} %sources_hbm.1, s32[2,4]{1,0:T(2,128)} %bitcast.2, s32[2,4]{1,0:T(2,128)} %bitcast.3), custom_call_target="tpu_custom_call" | custom-call | flops 1000 | bytes 1000 | tf_op jit(solution)/shard_map/pack_operators/pallas_call | solution.py:292
  7.9 1.6 %collective-permute-start.2 = (bf16[1568,128]{1,0:T(8,128)(2,1)S(1)}, bf16[1568,128]{1,0:T(8,128)(2,1)S(1)}, u32[]{:S(2)}, u32[]{:S(2)}) collective-permute-start(bf16[1568,128]{1,0:T(8,128)(2,1)S(1)} %pack_operators.1.refs_1_.refs_4_), channel_id=1, source_target_pairs={{0,2},{2,0},{1,3},{3,1},{4,6},{6,4},{5,7},{7,5},{8,10},{10,8},{9,1... | collective-permute-start | bytes 1204232 | tf_op jit(solution)/shard_map/ppermute | solution.py:346
  9.4 1.4 %own_pack_own_shard.1 = (bf16[4,256,256]{2,1,0:T(8,128)(2,1)S(1)}, f32[8,256,256]{2,1,0:T(8,128)S(1)}) custom-call(s32[1,128]{1,0:T(1,128)S(1)} %slice_convert_fusion.1.live_ref.refs_0_, s32[1,128]{1,0:T(1,128)S(1)} %slice_convert_fusion.1.live_ref.refs_0_, bf16[1568,128]{1,0:T(8,128)(2,1)S(1)} %pack_operators.1.refs_1_.refs_4_, ...), custom_call_target="tpu_custom_call" | custom-call | flops 1000 | bytes 1000 | tf_op jit(solution)/shard_map/own_pack_own_shard/pallas_call | solution.py:335
  10.8 6.3 %collective-permute-done.refs_4_.refs_10_ = bf16[512,256]{1,0:T(8,128)(2,1)S(1)} collective-permute-done((bf16[512,256]{1,0:T(8,128)(2,1)S(1)}, bf16[512,256]{1,0:T(8,128)(2,1)S(1)}, u32[]{:S(2)}, u32[]{:S(2)}) %collective-permute-start) | collective-permute-done | bytes 262176 | tf_op jit(solution)/shard_map/ppermute | solution.py:344
  17.1 0.0 collective-permute-start.3
  17.1 0.6 %collective-permute-start.5 = (bf16[512,256]{1,0:T(8,128)(2,1)S(1)}, bf16[512,256]{1,0:T(8,128)(2,1)S(1)}, u32[]{:S(2)}, u32[]{:S(2)}) collective-permute-start(bf16[512,256]{1,0:T(8,128)(2,1)S(1)} %collective-permute-done.refs_4_.refs_10_), channel_id=1, source_target_pairs={{0,4},{4,0},{8,12},{12,8},{1,5},{5,1},{9,13},{13,9},{2,6},{6,2},{1... | collective-permute-start | bytes 786440 | tf_op jit(solution)/shard_map/ppermute | solution.py:357
  17.7 0.0 collective-permute-done.1.refs_3_.refs_9_
  17.7 1.5 %own_pack_near_far.1.refs_5_ = f32[8,256,256]{2,1,0:T(8,128)S(1)} custom-call(s32[1,128]{1,0:T(1,128)S(1)} %slice_convert_fusion.1.live_ref.refs_0_, s32[1,128]{1,0:T(1,128)S(1)} %slice_convert_fusion.1.live_ref.refs_0_, bf16[1568,128]{1,0:T(8,128)(2,1)S(1)} %pack_operators.1.refs_1_.refs_4_, bf16[4,256,256]{2,1,0:T(8,128)(2,1)S(1)} %get-tuple-element.28.refs_2_.refs_8_, ...), custom_call_target="tpu_custom_call" | custom-call | flops 8000000000 | bytes 1000 | tf_op jit(solution)/shard_map/own_pack_near_far/pallas_call | solution.py:335
  19.2 0.0 collective-permute-done.2.refs_6_
  19.2 0.0 collective-permute-done.3.refs_1_.refs_5_
  19.3 0.3 collective-permute-start.4
  19.5 1.8 %core_pack.1 = (bf16[4,256,256]{2,1,0:T(8,128)(2,1)S(1)}, f32[8,256,256]{2,1,0:T(8,128)S(1)}) custom-call(s32[1,128]{1,0:T(1,128)S(1)} %get-tuple-element.48.live_ref.refs_0_.refs_1_, s32[1,128]{1,0:T(1,128)S(1)} %get-tuple-element.48.live_ref.refs_0_.refs_1_, bf16[1568,128]{1,0:T(8,128)(2,1)S(1)} %collective-permute-done.3.refs_1_.refs_5_, ...), custom_call_target="tpu_custom_call" | custom-call | flops 3000000000 | bytes 1000 | tf_op jit(solution)/shard_map/core_pack/pallas_call | solution.py:335
  21.3 0.0 collective-permute-done.4.refs_7_
  21.4 2.8 %other_packs.1 = (bf16[4,256,256]{2,1,0:T(8,128)(2,1)S(1)}, bf16[4,256,256]{2,1,0:T(8,128)(2,1)S(1)}, bf16[256,256]{1,0:T(8,128)(2,1)S(1)}, f32[8,256,256]{2,1,0:T(8,128)S(1)}) custom-call(s32[1,128]{1,0:T(1,128)S(1)} %slice_convert_fusion.1.live_ref.refs_0_, s32[1,128]{1,0:T(1,128)S(1)} %slice_convert_fusion.1.live_ref.refs_0_, ...), custom_call_target="tpu_custom_call" | custom-call | flops 1000 | bytes 1000 | tf_op jit(solution)/shard_map/other_packs/pallas_call | solution.py:335
  24.1 1.7 %collective-permute-done.5.refs_12_ = bf16[512,256]{1,0:T(8,128)(2,1)S(1)} collective-permute-done((bf16[512,256]{1,0:T(8,128)(2,1)S(1)}, bf16[512,256]{1,0:T(8,128)(2,1)S(1)}, u32[]{:S(2)}, u32[]{:S(2)}) %collective-permute-start.5) | collective-permute-done | bytes 262176 | tf_op jit(solution)/shard_map/ppermute | solution.py:357
  25.8 1.8 %third_shard.1 = (bf16[128,1024]{1,0:T(8,128)(2,1)S(1)}, bf16[128,1024]{1,0:T(8,128)(2,1)S(1)}, f32[128,1024]{1,0:T(8,128)S(1)}, f32[128,1024]{1,0:T(8,128)S(1)}) custom-call(s32[1,128]{1,0:T(1,128)S(1)} %slice_convert_fusion.1.live_ref.refs_0_, s32[1,128]{1,0:T(1,128)S(1)} %slice_convert_fusion.1.live_ref.refs_0_, ...), custom_call_target="tpu_custom_call" | custom-call | flops 1000 | bytes 1000 | tf_op jit(solution)/shard_map/third_shard/pallas_call | solution.py:335
  27.6 0.1 collective-permute-start.7
  27.7 0.5 %collective-permute-start.6 = (bf16[128,1024]{1,0:T(8,128)(2,1)S(1)}, bf16[128,1024]{1,0:T(8,128)(2,1)S(1)}, u32[]{:S(2)}, u32[]{:S(2)}) collective-permute-start(bf16[128,1024]{1,0:T(8,128)(2,1)S(1)} %get-tuple-element.44), channel_id=1, source_target_pairs={{0,1},{1,0},{2,3},{3,2},{4,5},{5,4},{6,7},{7,6},{8,9},{9,8},{10,11... | collective-permute-start | bytes 786440 | tf_op jit(solution)/shard_map/ppermute | solution.py:290
  28.2 1.0 %collective-permute-done.7 = bf16[128,1024]{1,0:T(8,128)(2,1)S(1)} collective-permute-done((bf16[128,1024]{1,0:T(8,128)(2,1)S(1)}, bf16[128,1024]{1,0:T(8,128)(2,1)S(1)}, u32[]{:S(2)}, u32[]{:S(2)}) %collective-permute-start.7) | collective-permute-done | bytes 262176 | tf_op jit(solution)/shard_map/ppermute | solution.py:290
  29.2 0.1 add_convert_fusion.1
  29.3 1.6 %collective-permute-start.8 = (bf16[128,1024]{1,0:T(8,128)(2,1)S(1)}, bf16[128,1024]{1,0:T(8,128)(2,1)S(1)}, u32[]{:S(2)}, u32[]{:S(2)}) collective-permute-start(bf16[128,1024]{1,0:T(8,128)(2,1)S(1)} %add_convert_fusion.1), channel_id=1, source_target_pairs={{0,2},{2,0},{1,3},{3,1},{4,6},{6,4},{5,7},{7,5},{8,10},{10,8},{9,1... | collective-permute-start | bytes 786440 | tf_op jit(solution)/shard_map/ppermute | solution.py:404
  30.9 0.0 collective-permute-done.6
  30.9 6.8 %collective-permute-done.8 = bf16[128,1024]{1,0:T(8,128)(2,1)S(1)} collective-permute-done((bf16[128,1024]{1,0:T(8,128)(2,1)S(1)}, bf16[128,1024]{1,0:T(8,128)(2,1)S(1)}, u32[]{:S(2)}, u32[]{:S(2)}) %collective-permute-start.8) | collective-permute-done | bytes 262176 | tf_op jit(solution)/shard_map/ppermute | solution.py:404
  37.7 0.8 %add_convert_fusion = bf16[128,1024]{1,0:T(8,128)(2,1)} fusion(bf16[128,1024]{1,0:T(8,128)(2,1)S(1)} %collective-permute-done.8, f32[128,1024]{1,0:T(8,128)S(1)} %get-tuple-element.43, bf16[128,1024]{1,0:T(8,128)(2,1)S(1)} %collective-permute-done.6), kind=kLoop, calls=%fused_computation | loop fusion | flops 655360 | bytes 1310720 | tf_op jit(solution)/shard_map/convert_element_type | solution.py:405
  (3 shorter events, 0.0 us)
Async XLA Ops:
  1.0 16.1 %collective-permute-start = (bf16[512,256]{1,0:T(8,128)(2,1)S(1)}, bf16[512,256]{1,0:T(8,128)(2,1)S(1)}, u32[]{:S(2)}, u32[]{:S(2)}) collective-permute-start(bf16[512,256]{1,0:T(8,128)(2,1)S(1)} %own_states.1.refs_2_.refs_8_), channel_id=1, source_target_pairs={{0,8},{8,0},{4,12},{12,4},{1,9},{9,1},{5,13},{13,5},{2,10},{10,2},... | collective-permute-start | bytes 786440 | tf_op jit(solution)/shard_map/ppermute | solution.py:344
  5.1 12.7 %collective-permute-start.1 = (bf16[512,256]{1,0:T(8,128)(2,1)S(1)}, bf16[512,256]{1,0:T(8,128)(2,1)S(1)}, u32[]{:S(2)}, u32[]{:S(2)}) collective-permute-start(bf16[512,256]{1,0:T(8,128)(2,1)S(1)} %own_states.1.refs_2_.refs_8_), channel_id=1, source_target_pairs={{0,4},{4,0},{8,12},{12,8},{1,5},{5,1},{9,13},{13,9},{2,6},{6,2},{1... | collective-permute-start | bytes 786440 | tf_op jit(solution)/shard_map/ppermute | solution.py:345
  7.9 11.4 %collective-permute-start.2 = (bf16[1568,128]{1,0:T(8,128)(2,1)S(1)}, bf16[1568,128]{1,0:T(8,128)(2,1)S(1)}, u32[]{:S(2)}, u32[]{:S(2)}) collective-permute-start(bf16[1568,128]{1,0:T(8,128)(2,1)S(1)} %pack_operators.1.refs_1_.refs_4_), channel_id=1, source_target_pairs={{0,2},{2,0},{1,3},{3,1},{4,6},{6,4},{5,7},{7,5},{8,10},{10,8},{9,1... | collective-permute-start | bytes 1204232 | tf_op jit(solution)/shard_map/ppermute | solution.py:346
  17.1 2.2 %collective-permute-start.3 = (bf16[1568,128]{1,0:T(8,128)(2,1)S(1)}, bf16[1568,128]{1,0:T(8,128)(2,1)S(1)}, u32[]{:S(2)}, u32[]{:S(2)}) collective-permute-start(bf16[1568,128]{1,0:T(8,128)(2,1)S(1)} %pack_operators.1.refs_1_.refs_4_), channel_id=1, source_target_pairs={{0,1},{1,0},{2,3},{3,2},{4,5},{5,4},{6,7},{7,6},{8,9},{9,8},{10,11... | collective-permute-start | bytes 1204232 | tf_op jit(solution)/shard_map/ppermute | solution.py:290
  17.1 8.7 %collective-permute-start.5 = (bf16[512,256]{1,0:T(8,128)(2,1)S(1)}, bf16[512,256]{1,0:T(8,128)(2,1)S(1)}, u32[]{:S(2)}, u32[]{:S(2)}) collective-permute-start(bf16[512,256]{1,0:T(8,128)(2,1)S(1)} %collective-permute-done.refs_4_.refs_10_), channel_id=1, source_target_pairs={{0,4},{4,0},{8,12},{12,8},{1,5},{5,1},{9,13},{13,9},{2,6},{6,2},{1... | collective-permute-start | bytes 786440 | tf_op jit(solution)/shard_map/ppermute | solution.py:357
  19.3 2.1 %collective-permute-start.4 = (bf16[1568,128]{1,0:T(8,128)(2,1)S(1)}, bf16[1568,128]{1,0:T(8,128)(2,1)S(1)}, u32[]{:S(2)}, u32[]{:S(2)}) collective-permute-start(bf16[1568,128]{1,0:T(8,128)(2,1)S(1)} %collective-permute-done.2.refs_6_), channel_id=1, source_target_pairs={{0,1},{1,0},{2,3},{3,2},{4,5},{5,4},{6,7},{7,6},{8,9},{9,8},{10,11... | collective-permute-start | bytes 1204232 | tf_op jit(solution)/shard_map/ppermute | solution.py:290
  27.6 1.6 %collective-permute-start.7 = (bf16[128,1024]{1,0:T(8,128)(2,1)S(1)}, bf16[128,1024]{1,0:T(8,128)(2,1)S(1)}, u32[]{:S(2)}, u32[]{:S(2)}) collective-permute-start(bf16[128,1024]{1,0:T(8,128)(2,1)S(1)} %get-tuple-element.46), channel_id=1, source_target_pairs={{0,1},{1,0},{2,3},{3,2},{4,5},{5,4},{6,7},{7,6},{8,9},{9,8},{10,11... | collective-permute-start | bytes 786440 | tf_op jit(solution)/shard_map/ppermute | solution.py:290
  27.7 3.2 %collective-permute-start.6 = (bf16[128,1024]{1,0:T(8,128)(2,1)S(1)}, bf16[128,1024]{1,0:T(8,128)(2,1)S(1)}, u32[]{:S(2)}, u32[]{:S(2)}) collective-permute-start(bf16[128,1024]{1,0:T(8,128)(2,1)S(1)} %get-tuple-element.44), channel_id=1, source_target_pairs={{0,1},{1,0},{2,3},{3,2},{4,5},{5,4},{6,7},{7,6},{8,9},{9,8},{10,11... | collective-permute-start | bytes 786440 | tf_op jit(solution)/shard_map/ppermute | solution.py:290
  29.3 8.4 %collective-permute-start.8 = (bf16[128,1024]{1,0:T(8,128)(2,1)S(1)}, bf16[128,1024]{1,0:T(8,128)(2,1)S(1)}, u32[]{:S(2)}, u32[]{:S(2)}) collective-permute-start(bf16[128,1024]{1,0:T(8,128)(2,1)S(1)} %add_convert_fusion.1), channel_id=1, source_target_pairs={{0,2},{2,0},{1,3},{3,1},{4,6},{6,4},{5,7},{7,5},{8,10},{10,8},{9,1... | collective-permute-start | bytes 786440 | tf_op jit(solution)/shard_map/ppermute | solution.py:404

commit v4 on v3

--- a/solution.py
+++ b/solution.py
@@ -180,15 +180,22 @@
     kron_ref[...] = jnp.where(diagonal, spread, 0.0).astype(BF16)
 
 
-def turn_shard(terms, numbers, pack, w_ref, shard, y_ref, at):
+def left_products(terms, numbers, pack, shards, c_ref, starts):
     block = pack.shape[-1]
-    tiles = y_ref.shape[0]
     for w in range(terms):
         row = pl.multiple_of(numbers[0, w] * block, block)
         left = pack[w * block : (w + 1) * block, :]
-        carried = matmul(left, shard[pl.ds(row, block), :]).astype(BF16)
-        y = matmul(carried, w_ref[w]).astype(BF16)
-        y_ref[:, at + w * SUB : at + (w + 1) * SUB, :] = y.reshape(tiles, SUB, y.shape[-1])
+        for start, shard in zip(starts, shards):
+            c_ref[start + w] = matmul(left, shard[pl.ds(row, block), :]).astype(BF16)
+
+
+def right_products(terms, w_ref, c_ref, y_ref, starts):
+    tiles = y_ref.shape[0]
+    for w in range(terms):
+        for start in starts:
+            y = matmul(c_ref[start + w], w_ref[w]).astype(BF16)
+            at = (start + w) * SUB
+            y_ref[:, at : at + SUB, :] = y.reshape(tiles, SUB, y.shape[-1])
 
 
 class Plan:
@@ -216,15 +223,19 @@
     if plan.prepare_last:
         spread_site(terms, rights, phys, packs, [(3, k) for k in range(plan.packs)], take(1)[0])
     targets = take(4 if plan.last else 1)
-    y_ref = take(1)[0]
+    c_ref, y_ref = take(2)
     if not plan.last:
         kron_ref = take(1)[0]
         spread_site(terms, rights, phys, packs, plan.chunks, kron_ref)
     alive = [live_ref[0, terms * (1 + rights) + b] for b in range(rights)]
     for k in plan.made:
         right_matrices(terms, rights, numbers[k], alive, packs[k], w_refs[k])
-    for n, (q, k) in enumerate(plan.chunks):
-        turn_shard(terms, numbers[k], packs[k], w_refs[k], shards[q], y_ref, n * terms * SUB)
+    starts = {k: [n * terms for n, (_, pack) in enumerate(plan.chunks) if pack == k] for k in plan.used}
+    for k in plan.used:
+        sources = [shards[q] for q, pack in plan.chunks if pack == k]
+        left_products(terms, numbers[k], packs[k], sources, c_ref, starts[k])
+    for k in plan.used:
+        right_products(terms, w_refs[k], c_ref, y_ref, starts[k])
     for i in range(y_ref.shape[0]):
         total = matmul(kron_ref[...], y_ref[i])
         if plan.before:
@@ -329,7 +340,10 @@
         else:
             shapes.append(jax.ShapeDtypeStruct((tiles, rows, width), F32))
         arrays = [*packs, *w, *shards] + [a for a in (acc, kron) if a is not None]
-        scratch = [pltpu.VMEM((tiles, depth, width), BF16)]
+        scratch = [
+            pltpu.VMEM((len(plan.chunks) * terms, block, width), BF16),
+            pltpu.VMEM((tiles, depth, width), BF16),
+        ]
         if not plan.last:
             scratch.append(pltpu.VMEM((rows, depth), BF16))
         return call(
@@ -353,9 +367,9 @@
         (mine,),
         flops=OWN_FLOPS,
     )
-    far, acc, pack, mine = lax.optimization_barrier((far, acc, pack, mine))
+    pack_c = swap(pack)
+    far, acc, mine = lax.optimization_barrier((far, acc, mine))
     farthest = lax.ppermute(far, "blk", NEAR)
-    pack_c = swap(pack)
     (acc,) = run(
         "own_pack_near_far",
         Plan(1, [(1, 0), (2, 0)]),

time: 38.6 us -> 37.3 us (0.966)
  waiting for transfers between devices: 15.8 us -> 15.1 us
  starting transfers between devices: 10.3 us -> 9.8 us
    ppermute x1, waiting for transfers between devices: 1.68 us -> 0.75 us  [by_states(): farthest = lax.ppermute(far, 'blk', NEAR)]
  transfers between devices with their start and end apart: 9 -> 9, of which waited for: 4 -> 4; matrix products, arithmetic and copies ran while one was open for 0% -> 0% of each run, Pallas kernels for 22% -> 23%
where the time goes in v4:
time: 37.3 us; the launch traced here: 37.1 us
  waiting for transfers between devices  15.1 us (40%)
  Pallas kernels  11.2 us (30%)
  starting transfers between devices  9.8 us (26%)
  other arithmetic  0.88 us (2%)
    pallas_call x5, Pallas kernels, run(): call(functools.partial(terms_body, terms, rights, phys, plan), tuple(shap...  9.01 us
    ppermute x1, waiting for transfers between devices, by_states(): taken = lax.ppermute(give, 'mpo', ACROSS)  7.1 us
    ppermute x1, waiting for transfers between devices, by_states(): far = lax.ppermute(mine, 'blk', FAR)  6.22 us
    ppermute x1, starting transfers between devices, by_states(): far = lax.ppermute(mine, 'blk', FAR)  4.1 us
    ppermute x1, starting transfers between devices, by_states(): near = lax.ppermute(mine, 'blk', NEAR)  1.58 us
    ppermute x1, starting transfers between devices, by_states(): pack_x = lax.ppermute(pack, 'mpo', ACROSS)  1.56 us
    ppermute x1, starting transfers between devices, by_states(): taken = lax.ppermute(give, 'mpo', ACROSS)  1.31 us
    pallas_call x1, Pallas kernels, by_states(): call(functools.partial(pack_body, terms, rights, phys), jax.ShapeDtypeStr...  1.23 us
  transfers between devices with their start and end apart: 9, of which 4 were waited for; matrix products, arithmetic and copies ran while one was open for 0% of the time, Pallas kernels for 23%

profile of v4, /device:TPU:0, one launch (start us, length us, event | category | flops | bytes accessed | tf_op | source)
XLA Modules:
  0.0 37.1 jit_solution(5220141602886042581)
XLA Ops:
  0.0 1.0 %own_states.1.refs_2_.refs_8_ = bf16[512,256]{1,0:T(8,128)(2,1)S(1)} custom-call(bf16[512,1024]{1,0:T(8,128)(2,1)} %wave_ref.1), custom_call_target="tpu_custom_call" | custom-call | flops 1000 | bytes 1000 | tf_op jit(solution)/shard_map/own_states/pallas_call | solution.py:290
  1.0 4.1 %collective-permute-start.1 = (bf16[512,256]{1,0:T(8,128)(2,1)S(1)}, bf16[512,256]{1,0:T(8,128)(2,1)S(1)}, u32[]{:S(2)}, u32[]{:S(2)}) collective-permute-start(bf16[512,256]{1,0:T(8,128)(2,1)S(1)} %own_states.1.refs_2_.refs_8_), channel_id=1, source_target_pairs={{0,8},{8,0},{4,12},{12,4},{1,9},{9,1},{5,13},{13,5},{2,10},{10,2},... | collective-permute-start | bytes 786440 | tf_op jit(solution)/shard_map/ppermute | solution.py:358
  5.1 1.6 %collective-permute-start = (bf16[512,256]{1,0:T(8,128)(2,1)S(1)}, bf16[512,256]{1,0:T(8,128)(2,1)S(1)}, u32[]{:S(2)}, u32[]{:S(2)}) collective-permute-start(bf16[512,256]{1,0:T(8,128)(2,1)S(1)} %own_states.1.refs_2_.refs_8_), channel_id=1, source_target_pairs={{0,4},{4,0},{8,12},{12,8},{1,5},{5,1},{9,13},{13,9},{2,6},{6,2},{1... | collective-permute-start | bytes 786440 | tf_op jit(solution)/shard_map/ppermute | solution.py:359
  6.6 1.2 %pack_operators.1.refs_1_.refs_4_ = bf16[1568,128]{1,0:T(8,128)(2,1)S(1)} custom-call(bf16[4,1,128,128]{3,2,1,0:T(8,128)(2,1)} %left_hbm.1, bf16[4,2,128,128]{3,2,1,0:T(8,128)(2,1)} %right_hbm.1, bf16[4,16,16]{2,1,0:T(8,128)(2,1)} %site_hbm.1, s32[4,4]{1,0:T(4,128)} %sources_hbm.1, s32[2,4]{1,0:T(2,128)} %bitcast.2, s32[2,4]{1,0:T(2,128)} %bitcast.3), custom_call_target="tpu_custom_call" | custom-call | flops 1000 | bytes 1000 | tf_op jit(solution)/shard_map/pack_operators/pallas_call | solution.py:303
  7.9 1.6 %collective-permute-start.2 = (bf16[1568,128]{1,0:T(8,128)(2,1)S(1)}, bf16[1568,128]{1,0:T(8,128)(2,1)S(1)}, u32[]{:S(2)}, u32[]{:S(2)}) collective-permute-start(bf16[1568,128]{1,0:T(8,128)(2,1)S(1)} %pack_operators.1.refs_1_.refs_4_), channel_id=1, source_target_pairs={{0,2},{2,0},{1,3},{3,1},{4,6},{6,4},{5,7},{7,5},{8,10},{10,8},{9,1... | collective-permute-start | bytes 1204232 | tf_op jit(solution)/shard_map/ppermute | solution.py:360
  9.4 0.0 collective-permute-start.3
  9.4 1.4 %own_pack_own_shard.1 = (bf16[4,256,256]{2,1,0:T(8,128)(2,1)S(1)}, f32[8,256,256]{2,1,0:T(8,128)S(1)}) custom-call(s32[1,128]{1,0:T(1,128)S(1)} %slice_convert_fusion.1.live_ref.refs_0_, s32[1,128]{1,0:T(1,128)S(1)} %slice_convert_fusion.1.live_ref.refs_0_, bf16[1568,128]{1,0:T(8,128)(2,1)S(1)} %pack_operators.1.refs_1_.refs_4_, ...), custom_call_target="tpu_custom_call" | custom-call | flops 1000 | bytes 1000 | tf_op jit(solution)/shard_map/own_pack_own_shard/pallas_call | solution.py:349
  10.9 6.2 %collective-permute-done.1.refs_4_.refs_10_ = bf16[512,256]{1,0:T(8,128)(2,1)S(1)} collective-permute-done((bf16[512,256]{1,0:T(8,128)(2,1)S(1)}, bf16[512,256]{1,0:T(8,128)(2,1)S(1)}, u32[]{:S(2)}, u32[]{:S(2)}) %collective-permute-start.1) | collective-permute-done | bytes 262176 | tf_op jit(solution)/shard_map/ppermute | solution.py:358
  17.1 0.6 %collective-permute-start.5 = (bf16[512,256]{1,0:T(8,128)(2,1)S(1)}, bf16[512,256]{1,0:T(8,128)(2,1)S(1)}, u32[]{:S(2)}, u32[]{:S(2)}) collective-permute-start(bf16[512,256]{1,0:T(8,128)(2,1)S(1)} %collective-permute-done.1.refs_4_.refs_10_), channel_id=1, source_target_pairs={{0,4},{4,0},{8,12},{12,8},{1,5},{5,1},{9,13},{13,9},{2,6},{6,2},{1... | collective-permute-start | bytes 786440 | tf_op jit(solution)/shard_map/ppermute | solution.py:372
  17.7 0.0 collective-permute-done.refs_3_.refs_9_
  17.7 1.5 %own_pack_near_far.1.refs_5_ = f32[8,256,256]{2,1,0:T(8,128)S(1)} custom-call(s32[1,128]{1,0:T(1,128)S(1)} %slice_convert_fusion.1.live_ref.refs_0_, s32[1,128]{1,0:T(1,128)S(1)} %slice_convert_fusion.1.live_ref.refs_0_, bf16[1568,128]{1,0:T(8,128)(2,1)S(1)} %pack_operators.1.refs_1_.refs_4_, bf16[4,256,256]{2,1,0:T(8,128)(2,1)S(1)} %get-tuple-element.25.refs_2_.refs_8_, ...), custom_call_target="tpu_custom_call" | custom-call | flops 8000000000 | bytes 1000 | tf_op jit(solution)/shard_map/own_pack_near_far/pallas_call | solution.py:349
  19.2 0.0 collective-permute-done.2.refs_6_
  19.2 0.0 collective-permute-done.3.refs_1_.refs_5_
  19.2 0.1 collective-permute-start.4
  19.3 1.7 %core_pack.1 = (bf16[4,256,256]{2,1,0:T(8,128)(2,1)S(1)}, f32[8,256,256]{2,1,0:T(8,128)S(1)}) custom-call(s32[1,128]{1,0:T(1,128)S(1)} %get-tuple-element.46.live_ref.refs_0_.refs_1_, s32[1,128]{1,0:T(1,128)S(1)} %get-tuple-element.46.live_ref.refs_0_.refs_1_, bf16[1568,128]{1,0:T(8,128)(2,1)S(1)} %collective-permute-done.3.refs_1_.refs_5_, ...), custom_call_target="tpu_custom_call" | custom-call | flops 3000000000 | bytes 1000 | tf_op jit(solution)/shard_map/core_pack/pallas_call | solution.py:349
  21.0 0.0 collective-permute-done.4.refs_7_
  21.1 2.7 %other_packs.1 = (bf16[4,256,256]{2,1,0:T(8,128)(2,1)S(1)}, bf16[4,256,256]{2,1,0:T(8,128)(2,1)S(1)}, bf16[256,256]{1,0:T(8,128)(2,1)S(1)}, f32[8,256,256]{2,1,0:T(8,128)S(1)}) custom-call(s32[1,128]{1,0:T(1,128)S(1)} %slice_convert_fusion.1.live_ref.refs_0_, s32[1,128]{1,0:T(1,128)S(1)} %slice_convert_fusion.1.live_ref.refs_0_, ...), custom_call_target="tpu_custom_call" | custom-call | flops 1000 | bytes 1000 | tf_op jit(solution)/shard_map/other_packs/pallas_call | solution.py:349
  23.8 0.7 %collective-permute-done.5.refs_12_ = bf16[512,256]{1,0:T(8,128)(2,1)S(1)} collective-permute-done((bf16[512,256]{1,0:T(8,128)(2,1)S(1)}, bf16[512,256]{1,0:T(8,128)(2,1)S(1)}, u32[]{:S(2)}, u32[]{:S(2)}) %collective-permute-start.5) | collective-permute-done | bytes 262176 | tf_op jit(solution)/shard_map/ppermute | solution.py:372
  24.5 1.7 %third_shard.1 = (bf16[128,1024]{1,0:T(8,128)(2,1)S(1)}, bf16[128,1024]{1,0:T(8,128)(2,1)S(1)}, f32[128,1024]{1,0:T(8,128)S(1)}, f32[128,1024]{1,0:T(8,128)S(1)}) custom-call(s32[1,128]{1,0:T(1,128)S(1)} %slice_convert_fusion.1.live_ref.refs_0_, s32[1,128]{1,0:T(1,128)S(1)} %slice_convert_fusion.1.live_ref.refs_0_, ...), custom_call_target="tpu_custom_call" | custom-call | flops 1000 | bytes 1000 | tf_op jit(solution)/shard_map/third_shard/pallas_call | solution.py:349
  26.2 0.1 collective-permute-start.7
  26.3 0.5 %collective-permute-start.6 = (bf16[128,1024]{1,0:T(8,128)(2,1)S(1)}, bf16[128,1024]{1,0:T(8,128)(2,1)S(1)}, u32[]{:S(2)}, u32[]{:S(2)}) collective-permute-start(bf16[128,1024]{1,0:T(8,128)(2,1)S(1)} %get-tuple-element.42), channel_id=1, source_target_pairs={{0,1},{1,0},{2,3},{3,2},{4,5},{5,4},{6,7},{7,6},{8,9},{9,8},{10,11... | collective-permute-start | bytes 786440 | tf_op jit(solution)/shard_map/ppermute | solution.py:301
  26.8 1.0 %collective-permute-done.7 = bf16[128,1024]{1,0:T(8,128)(2,1)S(1)} collective-permute-done((bf16[128,1024]{1,0:T(8,128)(2,1)S(1)}, bf16[128,1024]{1,0:T(8,128)(2,1)S(1)}, u32[]{:S(2)}, u32[]{:S(2)}) %collective-permute-start.7) | collective-permute-done | bytes 262176 | tf_op jit(solution)/shard_map/ppermute | solution.py:301
  27.8 0.1 add_convert_fusion.1
  27.9 1.3 %collective-permute-start.8 = (bf16[128,1024]{1,0:T(8,128)(2,1)S(1)}, bf16[128,1024]{1,0:T(8,128)(2,1)S(1)}, u32[]{:S(2)}, u32[]{:S(2)}) collective-permute-start(bf16[128,1024]{1,0:T(8,128)(2,1)S(1)} %add_convert_fusion.1), channel_id=1, source_target_pairs={{0,2},{2,0},{1,3},{3,1},{4,6},{6,4},{5,7},{7,5},{8,10},{10,8},{9,1... | collective-permute-start | bytes 786440 | tf_op jit(solution)/shard_map/ppermute | solution.py:418
  29.2 0.0 collective-permute-done.6
  29.2 7.1 %collective-permute-done.8 = bf16[128,1024]{1,0:T(8,128)(2,1)S(1)} collective-permute-done((bf16[128,1024]{1,0:T(8,128)(2,1)S(1)}, bf16[128,1024]{1,0:T(8,128)(2,1)S(1)}, u32[]{:S(2)}, u32[]{:S(2)}) %collective-permute-start.8) | collective-permute-done | bytes 262176 | tf_op jit(solution)/shard_map/ppermute | solution.py:418
  36.3 0.8 %add_convert_fusion = bf16[128,1024]{1,0:T(8,128)(2,1)} fusion(bf16[128,1024]{1,0:T(8,128)(2,1)S(1)} %collective-permute-done.8, f32[128,1024]{1,0:T(8,128)S(1)} %get-tuple-element.41, bf16[128,1024]{1,0:T(8,128)(2,1)S(1)} %collective-permute-done.6), kind=kLoop, calls=%fused_computation | loop fusion | flops 655360 | bytes 1310720 | tf_op jit(solution)/shard_map/convert_element_type | solution.py:419
  (3 shorter events, 0.0 us)
Async XLA Ops:
  1.0 16.1 %collective-permute-start.1 = (bf16[512,256]{1,0:T(8,128)(2,1)S(1)}, bf16[512,256]{1,0:T(8,128)(2,1)S(1)}, u32[]{:S(2)}, u32[]{:S(2)}) collective-permute-start(bf16[512,256]{1,0:T(8,128)(2,1)S(1)} %own_states.1.refs_2_.refs_8_), channel_id=1, source_target_pairs={{0,8},{8,0},{4,12},{12,4},{1,9},{9,1},{5,13},{13,5},{2,10},{10,2},... | collective-permute-start | bytes 786440 | tf_op jit(solution)/shard_map/ppermute | solution.py:358
  5.1 12.6 %collective-permute-start = (bf16[512,256]{1,0:T(8,128)(2,1)S(1)}, bf16[512,256]{1,0:T(8,128)(2,1)S(1)}, u32[]{:S(2)}, u32[]{:S(2)}) collective-permute-start(bf16[512,256]{1,0:T(8,128)(2,1)S(1)} %own_states.1.refs_2_.refs_8_), channel_id=1, source_target_pairs={{0,4},{4,0},{8,12},{12,8},{1,5},{5,1},{9,13},{13,9},{2,6},{6,2},{1... | collective-permute-start | bytes 786440 | tf_op jit(solution)/shard_map/ppermute | solution.py:359
  7.9 11.3 %collective-permute-start.2 = (bf16[1568,128]{1,0:T(8,128)(2,1)S(1)}, bf16[1568,128]{1,0:T(8,128)(2,1)S(1)}, u32[]{:S(2)}, u32[]{:S(2)}) collective-permute-start(bf16[1568,128]{1,0:T(8,128)(2,1)S(1)} %pack_operators.1.refs_1_.refs_4_), channel_id=1, source_target_pairs={{0,2},{2,0},{1,3},{3,1},{4,6},{6,4},{5,7},{7,5},{8,10},{10,8},{9,1... | collective-permute-start | bytes 1204232 | tf_op jit(solution)/shard_map/ppermute | solution.py:360
  9.4 9.8 %collective-permute-start.3 = (bf16[1568,128]{1,0:T(8,128)(2,1)S(1)}, bf16[1568,128]{1,0:T(8,128)(2,1)S(1)}, u32[]{:S(2)}, u32[]{:S(2)}) collective-permute-start(bf16[1568,128]{1,0:T(8,128)(2,1)S(1)} %pack_operators.1.refs_1_.refs_4_), channel_id=1, source_target_pairs={{0,1},{1,0},{2,3},{3,2},{4,5},{5,4},{6,7},{7,6},{8,9},{9,8},{10,11... | collective-permute-start | bytes 1204232 | tf_op jit(solution)/shard_map/ppermute | solution.py:301
  17.1 7.4 %collective-permute-start.5 = (bf16[512,256]{1,0:T(8,128)(2,1)S(1)}, bf16[512,256]{1,0:T(8,128)(2,1)S(1)}, u32[]{:S(2)}, u32[]{:S(2)}) collective-permute-start(bf16[512,256]{1,0:T(8,128)(2,1)S(1)} %collective-permute-done.1.refs_4_.refs_10_), channel_id=1, source_target_pairs={{0,4},{4,0},{8,12},{12,8},{1,5},{5,1},{9,13},{13,9},{2,6},{6,2},{1... | collective-permute-start | bytes 786440 | tf_op jit(solution)/shard_map/ppermute | solution.py:372
  19.2 1.8 %collective-permute-start.4 = (bf16[1568,128]{1,0:T(8,128)(2,1)S(1)}, bf16[1568,128]{1,0:T(8,128)(2,1)S(1)}, u32[]{:S(2)}, u32[]{:S(2)}) collective-permute-start(bf16[1568,128]{1,0:T(8,128)(2,1)S(1)} %collective-permute-done.2.refs_6_), channel_id=1, source_target_pairs={{0,1},{1,0},{2,3},{3,2},{4,5},{5,4},{6,7},{7,6},{8,9},{9,8},{10,11... | collective-permute-start | bytes 1204232 | tf_op jit(solution)/shard_map/ppermute | solution.py:301
  26.2 1.6 %collective-permute-start.7 = (bf16[128,1024]{1,0:T(8,128)(2,1)S(1)}, bf16[128,1024]{1,0:T(8,128)(2,1)S(1)}, u32[]{:S(2)}, u32[]{:S(2)}) collective-permute-start(bf16[128,1024]{1,0:T(8,128)(2,1)S(1)} %get-tuple-element.44), channel_id=1, source_target_pairs={{0,1},{1,0},{2,3},{3,2},{4,5},{5,4},{6,7},{7,6},{8,9},{9,8},{10,11... | collective-permute-start | bytes 786440 | tf_op jit(solution)/shard_map/ppermute | solution.py:301
  26.3 2.9 %collective-permute-start.6 = (bf16[128,1024]{1,0:T(8,128)(2,1)S(1)}, bf16[128,1024]{1,0:T(8,128)(2,1)S(1)}, u32[]{:S(2)}, u32[]{:S(2)}) collective-permute-start(bf16[128,1024]{1,0:T(8,128)(2,1)S(1)} %get-tuple-element.42), channel_id=1, source_target_pairs={{0,1},{1,0},{2,3},{3,2},{4,5},{5,4},{6,7},{7,6},{8,9},{9,8},{10,11... | collective-permute-start | bytes 786440 | tf_op jit(solution)/shard_map/ppermute | solution.py:301
  27.9 8.4 %collective-permute-start.8 = (bf16[128,1024]{1,0:T(8,128)(2,1)S(1)}, bf16[128,1024]{1,0:T(8,128)(2,1)S(1)}, u32[]{:S(2)}, u32[]{:S(2)}) collective-permute-start(bf16[128,1024]{1,0:T(8,128)(2,1)S(1)} %add_convert_fusion.1), channel_id=1, source_target_pairs={{0,2},{2,0},{1,3},{3,1},{4,6},{6,4},{5,7},{7,5},{8,10},{10,8},{9,1... | collective-permute-start | bytes 786440 | tf_op jit(solution)/shard_map/ppermute | solution.py:418

commit v5 on v4

--- a/solution.py
+++ b/solution.py
@@ -14,12 +14,12 @@
 PACK_BYTES = 32 * 1024 * 1024
 OWN_FLOPS = 1000
 CHIP_FLOPS = int(8e9)
-OTHER_FLOPS = 1000
 CORE_FLOPS = int(3e9)
 NEAR = ((0, 1), (1, 0), (2, 3), (3, 2))
 FAR = ((0, 2), (2, 0), (1, 3), (3, 1))
 CORE = ((0, 1), (1, 0), (2, 3), (3, 2))
 ACROSS = ((0, 2), (2, 0), (1, 3), (3, 1))
+PARTS = 2
 SUB = 16
 
 
@@ -136,17 +136,23 @@
         copy.wait()
 
 
-def right_matrices(terms, rights, numbers, alive, pack, w_ref):
+def block_matrices(terms, rights, numbers, pack, left_ref, right_ref):
     block = pack.shape[-1]
-    for w in range(terms):
+    sectors = left_ref.shape[-1] // block
+    for w in range(terms):
+        left = pack[w * block : (w + 1) * block, :]
+        for r in range(sectors):
+            left_ref[w, :, r * block : (r + 1) * block] = jnp.where(
+                numbers[0, w] == r, left, jnp.zeros_like(left)
+            )
         for b in range(rights):
             start = (terms + w * rights + b) * block
             turned = pack[start : start + block, :]
             source = numbers[0, terms + w * rights + b]
+            alive = numbers[0, terms * (1 + rights) + b] != 0
             for r in range(rights):
-                keep = jnp.logical_and(source == r, alive[b] != 0)
-                w_ref[w, r * block : (r + 1) * block, b * block : (b + 1) * block] = jnp.where(
-                    keep, turned, jnp.zeros_like(turned)
+                right_ref[w, r * block : (r + 1) * block, b * block : (b + 1) * block] = jnp.where(
+                    jnp.logical_and(source == r, alive), turned, jnp.zeros_like(turned)
                 )
 
 
@@ -180,13 +186,14 @@
     kron_ref[...] = jnp.where(diagonal, spread, 0.0).astype(BF16)
 
 
-def left_products(terms, numbers, pack, shards, c_ref, starts):
-    block = pack.shape[-1]
-    for w in range(terms):
-        row = pl.multiple_of(numbers[0, w] * block, block)
-        left = pack[w * block : (w + 1) * block, :]
-        for start, shard in zip(starts, shards):
-            c_ref[start + w] = matmul(left, shard[pl.ds(row, block), :]).astype(BF16)
+def left_products(left_ref, shards, c_ref, starts, first):
+    terms, _, depth = left_ref.shape
+    count = c_ref.shape[1]
+    left = left_ref[:, first : first + count, :].reshape(terms * count, depth)
+    for start, shard in zip(starts, shards):
+        c_ref[start : start + terms] = (
+            matmul(left, shard[...]).astype(BF16).reshape(terms, count, c_ref.shape[2])
+        )
 
 
 def right_products(terms, w_ref, c_ref, y_ref, starts):
@@ -199,7 +206,7 @@
 
 
 class Plan:
-    def __init__(self, packs, chunks, made=(), before=True, prepare_last=False, last=False):
+    def __init__(self, packs, chunks, made=(), before=True, prepare_last=False, last=None):
         self.packs, self.chunks, self.made = packs, chunks, made
         self.before, self.prepare_last, self.last = before, prepare_last, last
         self.used = sorted({k for _, k in chunks})
@@ -207,48 +214,54 @@
         self.shards = sorted({q for q, _ in chunks})
 
 
-def terms_body(terms, rights, phys, plan, live_ref, *refs):
+def terms_body(terms, rights, phys, plan, *refs):
     refs = list(refs)
 
     def take(count):
         taken, refs[:] = refs[:count], refs[count:]
         return taken
 
-    numbers, packs = take(plan.packs), take(plan.packs)
-    w_refs = dict(zip(plan.given, take(len(plan.given))))
+    last = plan.last is not None
+    numbers = dict(zip(plan.made, take(len(plan.made))))
+    packs = take(0 if last else plan.packs)
+    lefts = dict(zip(plan.given, take(len(plan.given))))
+    rights_of = dict(zip(plan.given, take(len(plan.given))))
     shards = dict(zip(plan.shards, take(len(plan.shards))))
     acc_in = take(1)[0] if plan.before else None
-    kron_ref = take(1)[0] if plan.last else None
-    w_refs.update(zip(plan.made, take(len(plan.made))))
+    kron_ref = take(1)[0] if last else None
+    lefts.update(zip(plan.made, take(len(plan.made))))
+    rights_of.update(zip(plan.made, take(len(plan.made))))
     if plan.prepare_last:
         spread_site(terms, rights, phys, packs, [(3, k) for k in range(plan.packs)], take(1)[0])
-    targets = take(4 if plan.last else 1)
+    targets = take(3 if last else 1)
     c_ref, y_ref = take(2)
-    if not plan.last:
+    if not last:
         kron_ref = take(1)[0]
         spread_site(terms, rights, phys, packs, plan.chunks, kron_ref)
-    alive = [live_ref[0, terms * (1 + rights) + b] for b in range(rights)]
     for k in plan.made:
-        right_matrices(terms, rights, numbers[k], alive, packs[k], w_refs[k])
+        block_matrices(terms, rights, numbers[k], packs[k], lefts[k], rights_of[k])
     starts = {k: [n * terms for n, (_, pack) in enumerate(plan.chunks) if pack == k] for k in plan.used}
+    first = plan.last * c_ref.shape[1] if last else 0
     for k in plan.used:
         sources = [shards[q] for q, pack in plan.chunks if pack == k]
-        left_products(terms, numbers[k], packs[k], sources, c_ref, starts[k])
+        left_products(lefts[k], sources, c_ref, starts[k], first)
     for k in plan.used:
-        right_products(terms, w_refs[k], c_ref, y_ref, starts[k])
+        right_products(terms, rights_of[k], c_ref, y_ref, starts[k])
     for i in range(y_ref.shape[0]):
         total = matmul(kron_ref[...], y_ref[i])
         if plan.before:
-            total = total + acc_in[i]
-        if not plan.last:
+            total = total + acc_in[first // SUB + i]
+        if not last:
             targets[0][i] = total
             continue
         width = total.shape[1]
         count = total.shape[0] // SUB // 4
-        for n, target in enumerate(targets):
+        for n, (target, place) in enumerate(
+            ((targets[0], 0), (targets[0], 1), (targets[1], 0), (targets[2], 0))
+        ):
             for m in range(count):
-                start = (n * count + m) * SUB
-                target[i * SUB : (i + 1) * SUB, m * width : (m + 1) * width] = total[
+                start, column = (n * count + m) * SUB, (place * count + m) * width
+                target[i * SUB : (i + 1) * SUB, column : column + width] = total[
                     start : start + SUB, :
                 ].astype(target.dtype)
 
@@ -328,42 +341,49 @@
         return p[pack_rows - SUB : pack_rows - SUB + 1, :].astype(jnp.int32)
 
     one_pack = terms * SUB
-    quarter = (block, phys // slots * width)
-
-    def run(name, plan, packs, numbers, shards, acc=None, w=(), kron=None, flops=1000):
+
+    def run(name, plan, packs, numbers, shards, acc=None, given=(), kron=None, flops=1000):
         depth = len(plan.chunks) * one_pack
-        shapes = [jax.ShapeDtypeStruct((terms, width, width), BF16) for _ in plan.made]
+        last = plan.last is not None
+        part = PARTS if last else 1
+        shapes = [jax.ShapeDtypeStruct((terms, block, all_rows), BF16) for _ in plan.made]
+        shapes += [jax.ShapeDtypeStruct((terms, width, width), BF16) for _ in plan.made]
         if plan.prepare_last:
             shapes.append(jax.ShapeDtypeStruct((rows, len(packs) * one_pack), BF16))
-        if plan.last:
-            shapes += [jax.ShapeDtypeStruct(quarter, t) for t in (BF16, BF16, F32, F32)]
+        if last:
+            size, columns = block // part, phys // slots * width
+            shapes.append(jax.ShapeDtypeStruct((size, 2 * columns), BF16))
+            shapes += [jax.ShapeDtypeStruct((size, columns), F32)] * 2
         else:
             shapes.append(jax.ShapeDtypeStruct((tiles, rows, width), F32))
-        arrays = [*packs, *w, *shards] + [a for a in (acc, kron) if a is not None]
+        lefts, rights_of = [g[0] for g in given], [g[1] for g in given]
+        arrays = [*packs, *lefts, *rights_of, *shards]
+        arrays += [a for a in (acc, kron) if a is not None]
         scratch = [
-            pltpu.VMEM((len(plan.chunks) * terms, block, width), BF16),
-            pltpu.VMEM((tiles, depth, width), BF16),
+            pltpu.VMEM((len(plan.chunks) * terms, block // part, width), BF16),
+            pltpu.VMEM((tiles // part, depth, width), BF16),
         ]
-        if not plan.last:
+        if not last:
             scratch.append(pltpu.VMEM((rows, depth), BF16))
-        return call(
+        outs = call(
             functools.partial(terms_body, terms, rights, phys, plan),
             tuple(shapes),
-            [smem] * (1 + len(numbers)) + [vmem] * len(arrays),
+            [smem] * len(numbers) + [vmem] * len(arrays),
             scratch,
             name=name,
             flops=flops,
-        )(numbers[0], *numbers, *arrays)
+        )(*numbers, *arrays)
+        made = len(plan.made)
+        return tuple(zip(outs[:made], outs[made : 2 * made])) + tuple(outs[2 * made :])
 
     far = lax.ppermute(mine, "blk", FAR)
     near = lax.ppermute(mine, "blk", NEAR)
     pack_x = lax.ppermute(pack, "mpo", ACROSS)
-    number = numbers_of(pack)
-    w_own, acc = run(
+    own, acc = run(
         "own_pack_own_shard",
         Plan(1, [(0, 0)], made=(0,), before=False),
         (pack,),
-        (number,),
+        (numbers_of(pack),),
         (mine,),
         flops=OWN_FLOPS,
     )
@@ -374,49 +394,50 @@
         "own_pack_near_far",
         Plan(1, [(1, 0), (2, 0)]),
         (pack,),
-        (number,),
+        (),
         (near, far),
         acc,
-        (w_own,),
+        (own,),
         flops=CHIP_FLOPS,
     )
     acc, pack_x, pack_c = lax.optimization_barrier((acc, pack_x, pack_c))
-    number_c = numbers_of(pack_c)
     x_packs = (pack_x, swap(pack_x))
-    x_numbers = [numbers_of(p) for p in x_packs]
-    w_core, acc = run(
+    core, acc = run(
         "core_pack",
         Plan(1, [(0, 0), (1, 0), (2, 0)], made=(0,)),
         (pack_c,),
-        (number_c,),
+        (numbers_of(pack_c),),
         (mine, near, far),
         acc,
         flops=CORE_FLOPS,
     )
-    packs, numbers = (pack, pack_c, *x_packs), (number, number_c, *x_numbers)
-    w_x, w_xc, kron, acc = run(
+    across, beyond, kron, acc = run(
         "other_packs",
         Plan(4, [(q, k) for q in (0, 1, 2) for k in (2, 3)], made=(2, 3), prepare_last=True),
-        packs,
-        numbers,
+        (pack, pack_c, *x_packs),
+        [numbers_of(p) for p in x_packs],
         (mine, near, far),
         acc,
-        flops=OTHER_FLOPS,
     )
     farthest, acc = lax.optimization_barrier((farthest, acc))
-    give_far, give_core, keep_x, keep = run(
-        "third_shard",
-        Plan(4, [(3, k) for k in range(4)], last=True),
-        packs,
-        numbers,
-        (farthest,),
-        acc,
-        (w_own, w_core, w_x, w_xc),
-        kron,
-    )
-    give = (keep_x + swap(give_far).astype(F32)).astype(BF16)
-    taken = lax.ppermute(give, "mpo", ACROSS)
-    return (keep + swap(give_core).astype(F32) + taken.astype(F32)).astype(BF16)
+    outs = []
+    for part in range(PARTS):
+        give, keep_x, keep = run(
+            "third_shard",
+            Plan(4, [(3, k) for k in range(4)], last=part),
+            (),
+            (),
+            (farthest,),
+            acc,
+            (own, core, across, beyond),
+            kron,
+        )
+        columns = keep.shape[1]
+        back = swap(give)
+        send = (keep_x + back[:, :columns].astype(F32)).astype(BF16)
+        taken = lax.ppermute(send, "mpo", ACROSS)
+        outs.append((keep + back[:, columns:].astype(F32) + taken.astype(F32)).astype(BF16))
+    return jnp.concatenate(outs, axis=0) if PARTS > 1 else outs[0]
 
 
 def solution(mesh):

time: 37.3 us -> 36.7 us (0.984)
  waiting for transfers between devices: 15.1 us -> 12 us
  starting transfers between devices: 9.8 us -> 11.3 us
  Pallas kernels: 11.2 us -> 12.2 us
    ppermute x1 -> x2, waiting for transfers between devices: 7.1 us -> 5.66 us  [by_states(): taken = lax.ppermute(send, 'mpo', ACROSS)]
    ppermute x1 -> x2, starting transfers between devices: 1.31 us -> 2.69 us  [by_states(): taken = lax.ppermute(send, 'mpo', ACROSS)]
    pallas_call x5 -> x6, Pallas kernels: 9.01 us -> 10.1 us  [run(): call(functools.partial(terms_body, terms, rights, phys, plan), tuple(shap...]
    ppermute x4, waiting for transfers between devices: 1.03 us -> 0.01 us  [swap(): return lax.ppermute(x, 'mpo', CORE)]
    concatenate x0 -> x1, other arithmetic: none -> 0.72 us  [by_states(): return jnp.concatenate(outs, axis=0) if PARTS > 1 else outs[0]]
    convert_element_type x2 -> x4, other arithmetic: 0.86 us -> 0.15 us  [the longest x2 0.1 us: by_states(): (keep + back[:, columns:].astype(F32) + taken.astype(F32)).astype(BF16)]
    ppermute x1, waiting for transfers between devices: 0.75 us -> 0.34 us  [by_states(): farthest = lax.ppermute(far, 'blk', NEAR)]
  transfers between devices with their start and end apart: 9 -> 10, of which waited for: 4 -> 4; matrix products, arithmetic and copies ran while one was open for 0% -> 0% of each run, Pallas kernels for 23% -> 28%
where the time goes in v5:
time: 36.7 us; the launch traced here: 36.5 us
  Pallas kernels  12.2 us (33%)
  waiting for transfers between devices  12 us (33%)
  starting transfers between devices  11.3 us (31%)
  other arithmetic  0.89 us (2%)
    pallas_call x6, Pallas kernels, run(): call(functools.partial(terms_body, terms, rights, phys, plan), tuple(shap...  10.1 us
    ppermute x1, waiting for transfers between devices, by_states(): far = lax.ppermute(mine, 'blk', FAR)  5.97 us
    ppermute x2, waiting for transfers between devices, by_states(): taken = lax.ppermute(send, 'mpo', ACROSS)  5.66 us
    ppermute x1, starting transfers between devices, by_states(): far = lax.ppermute(mine, 'blk', FAR)  4.1 us
    ppermute x2, starting transfers between devices, by_states(): taken = lax.ppermute(send, 'mpo', ACROSS)  2.69 us
    ppermute x1, starting transfers between devices, by_states(): near = lax.ppermute(mine, 'blk', NEAR)  1.58 us
    ppermute x1, starting transfers between devices, by_states(): pack_x = lax.ppermute(pack, 'mpo', ACROSS)  1.56 us
    pallas_call x1, Pallas kernels, by_states(): call(functools.partial(pack_body, terms, rights, phys), jax.ShapeDtypeStr...  1.23 us
  transfers between devices with their start and end apart: 10, of which 4 were waited for; matrix products, arithmetic and copies ran while one was open for 0% of the time, Pallas kernels for 28%

profile of v5, /device:TPU:0, one launch (start us, length us, event | category | flops | bytes accessed | tf_op | source)
XLA Modules:
  0.0 36.5 jit_solution(11543406672866217088)
XLA Ops:
  0.0 1.0 %own_states.1.refs_2_.refs_6_ = bf16[512,256]{1,0:T(8,128)(2,1)S(1)} custom-call(bf16[512,1024]{1,0:T(8,128)(2,1)} %wave_ref.1), custom_call_target="tpu_custom_call" | custom-call | flops 1000 | bytes 1000 | tf_op jit(solution)/shard_map/own_states/pallas_call | solution.py:303
  1.0 4.1 %collective-permute-start.1 = (bf16[512,256]{1,0:T(8,128)(2,1)S(1)}, bf16[512,256]{1,0:T(8,128)(2,1)S(1)}, u32[]{:S(2)}, u32[]{:S(2)}) collective-permute-start(bf16[512,256]{1,0:T(8,128)(2,1)S(1)} %own_states.1.refs_2_.refs_6_), channel_id=1, source_target_pairs={{0,8},{8,0},{4,12},{12,4},{1,9},{9,1},{5,13},{13,5},{2,10},{10,2},... | collective-permute-start | bytes 786440 | tf_op jit(solution)/shard_map/ppermute | solution.py:379
  5.1 1.6 %collective-permute-start = (bf16[512,256]{1,0:T(8,128)(2,1)S(1)}, bf16[512,256]{1,0:T(8,128)(2,1)S(1)}, u32[]{:S(2)}, u32[]{:S(2)}) collective-permute-start(bf16[512,256]{1,0:T(8,128)(2,1)S(1)} %own_states.1.refs_2_.refs_6_), channel_id=1, source_target_pairs={{0,4},{4,0},{8,12},{12,8},{1,5},{5,1},{9,13},{13,9},{2,6},{6,2},{1... | collective-permute-start | bytes 786440 | tf_op jit(solution)/shard_map/ppermute | solution.py:380
  6.6 1.2 %pack_operators.1.refs_1_.refs_0_.refs_2_ = bf16[1568,128]{1,0:T(8,128)(2,1)S(1)} custom-call(bf16[4,1,128,128]{3,2,1,0:T(8,128)(2,1)} %left_hbm.1, bf16[4,2,128,128]{3,2,1,0:T(8,128)(2,1)} %right_hbm.1, bf16[4,16,16]{2,1,0:T(8,128)(2,1)} %site_hbm.1, s32[4,4]{1,0:T(4,128)} %sources_hbm.1, s32[2,4]{1,0:T(2,128)} %bitcast.2, s32[2,4]{1,0:T(2,128)} %bitcast.3), custom_call_target="tpu_custom_call" | custom-call | flops 1000 | bytes 1000 | tf_op jit(solution)/shard_map/pack_operators/pallas_call | solution.py:316
  7.9 1.6 %collective-permute-start.2 = (bf16[1568,128]{1,0:T(8,128)(2,1)S(1)}, bf16[1568,128]{1,0:T(8,128)(2,1)S(1)}, u32[]{:S(2)}, u32[]{:S(2)}) collective-permute-start(bf16[1568,128]{1,0:T(8,128)(2,1)S(1)} %pack_operators.1.refs_1_.refs_0_.refs_2_), channel_id=1, source_target_pairs={{0,2},{2,0},{1,3},{3,1},{4,6},{6,4},{5,7},{7,5},{8,10},{10,8},{9,1... | collective-permute-start | bytes 1204232 | tf_op jit(solution)/shard_map/ppermute | solution.py:381
  9.4 0.0 collective-permute-start.3
  9.4 1.7 %own_pack_own_shard.1 = (bf16[4,128,512]{2,1,0:T(8,128)(2,1)S(1)}, bf16[4,256,256]{2,1,0:T(8,128)(2,1)S(1)}, f32[8,256,256]{2,1,0:T(8,128)S(1)}) custom-call(s32[1,128]{1,0:T(1,128)S(1)} %slice_convert_fusion.1.refs_0_, bf16[1568,128]{1,0:T(8,128)(2,1)S(1)} %pack_operators.1.refs_1_.refs_0_.refs_2_, bf16[512,256]{1,0:T(8,128)(2,1)S(1)} %own_states.1.refs_2_.refs_6_), custom_call_target="tpu_custom_call" | custom-call | flops 1000 | bytes 1000 | tf_op jit(solution)/shard_map/own_pack_own_shard/pallas_call | solution.py:368
  11.1 6.0 %collective-permute-done.1.refs_4_.refs_8_ = bf16[512,256]{1,0:T(8,128)(2,1)S(1)} collective-permute-done((bf16[512,256]{1,0:T(8,128)(2,1)S(1)}, bf16[512,256]{1,0:T(8,128)(2,1)S(1)}, u32[]{:S(2)}, u32[]{:S(2)}) %collective-permute-start.1) | collective-permute-done | bytes 262176 | tf_op jit(solution)/shard_map/ppermute | solution.py:379
  17.1 0.6 %collective-permute-start.5 = (bf16[512,256]{1,0:T(8,128)(2,1)S(1)}, bf16[512,256]{1,0:T(8,128)(2,1)S(1)}, u32[]{:S(2)}, u32[]{:S(2)}) collective-permute-start(bf16[512,256]{1,0:T(8,128)(2,1)S(1)} %collective-permute-done.1.refs_4_.refs_8_), channel_id=1, source_target_pairs={{0,4},{4,0},{8,12},{12,8},{1,5},{5,1},{9,13},{13,9},{2,6},{6,2},{1... | collective-permute-start | bytes 786440 | tf_op jit(solution)/shard_map/ppermute | solution.py:392
  17.7 0.0 collective-permute-done.refs_3_.refs_7_
  17.7 1.1 %own_pack_near_far.1.refs_5_ = f32[8,256,256]{2,1,0:T(8,128)S(1)} custom-call(bf16[1568,128]{1,0:T(8,128)(2,1)S(1)} %pack_operators.1.refs_1_.refs_0_.refs_2_, bf16[4,128,512]{2,1,0:T(8,128)(2,1)S(1)} %get-tuple-element.31.refs_1_.refs_0_, bf16[4,256,256]{2,1,0:T(8,128)(2,1)S(1)} %get-tuple-element.32.refs_2_.refs_4_, ...), custom_call_target="tpu_custom_call" | custom-call | flops 8000000000 | bytes 1000 | tf_op jit(solution)/shard_map/own_pack_near_far/pallas_call | solution.py:368
  18.8 0.0 collective-permute-done.2.refs_4_
  18.8 0.0 collective-permute-done.3.refs_1_.refs_3_
  18.8 0.1 collective-permute-start.4
  18.9 2.1 %core_pack.1 = (bf16[4,128,512]{2,1,0:T(8,128)(2,1)S(1)}, bf16[4,256,256]{2,1,0:T(8,128)(2,1)S(1)}, f32[8,256,256]{2,1,0:T(8,128)S(1)}) custom-call(s32[1,128]{1,0:T(1,128)S(1)} %get-tuple-element.58.refs_0_, bf16[1568,128]{1,0:T(8,128)(2,1)S(1)} %collective-permute-done.3.refs_1_.refs_3_, bf16[512,256]{1,0:T(8,128)(2,1)S(1)} %own_states.1.refs_2_.refs_6_, ...), custom_call_target="tpu_custom_call" | custom-call | flops 3000000000 | bytes 1000 | tf_op jit(solution)/shard_map/core_pack/pallas_call | solution.py:368
  21.0 0.0 collective-permute-done.4.refs_5_
  21.0 3.1 %other_packs.1 = (bf16[4,128,512]{2,1,0:T(8,128)(2,1)S(1)}, bf16[4,128,512]{2,1,0:T(8,128)(2,1)S(1)}, bf16[4,256,256]{2,1,0:T(8,128)(2,1)S(1)}, bf16[4,256,256]{...) custom-call(s32[1,128]{1,0:T(1,128)S(1)} %get-tuple-element.57.refs_0_, ...), custom_call_target="tpu_custom_call" | custom-call | flops 1000 | bytes 1000 | tf_op jit(solution)/shard_map/other_packs/pallas_call | solution.py:368
  24.2 0.3 collective-permute-done.5.refs_8_
  24.5 1.0 %third_shard.2 = (bf16[64,2048]{1,0:T(8,128)(2,1)S(1)}, f32[64,1024]{1,0:T(8,128)S(1)}, f32[64,1024]{1,0:T(8,128)S(1)}) custom-call(bf16[4,128,512]{2,1,0:T(8,128)(2,1)S(1)} %get-tuple-element.31.refs_1_.refs_0_, bf16[4,128,512]{2,1,0:T(8,128)(2,1)S(1)} %get-tuple-element.39.refs_1_, bf16[4,128,512]{2,1,0:T(8,128)(2,1)S(1)} %get-tuple-element.42.refs_2_, ...), custom_call_target="tpu_custom_call" | custom-call | flops 1000 | bytes 1000 | tf_op jit(solution)/shard_map/third_shard/pallas_call | solution.py:368
  25.6 0.2 collective-permute-start.6
  25.8 1.0 %third_shard.3 = (bf16[64,2048]{1,0:T(8,128)(2,1)S(1)}, f32[64,1024]{1,0:T(8,128)S(1)}, f32[64,1024]{1,0:T(8,128)S(1)}) custom-call(bf16[4,128,512]{2,1,0:T(8,128)(2,1)S(1)} %get-tuple-element.31.refs_1_.refs_0_, bf16[4,128,512]{2,1,0:T(8,128)(2,1)S(1)} %get-tuple-element.39.refs_1_, bf16[4,128,512]{2,1,0:T(8,128)(2,1)S(1)} %get-tuple-element.42.refs_2_, ...), custom_call_target="tpu_custom_call" | custom-call | flops 1000 | bytes 1000 | tf_op jit(solution)/shard_map/third_shard/pallas_call | solution.py:368
  26.8 0.4 %collective-permute-start.8 = (bf16[64,2048]{1,0:T(8,128)(2,1)S(1)}, bf16[64,2048]{1,0:T(8,128)(2,1)S(1)}, u32[]{:S(2)}, u32[]{:S(2)}) collective-permute-start(bf16[64,2048]{1,0:T(8,128)(2,1)S(1)} %get-tuple-element.55), channel_id=1, source_target_pairs={{0,1},{1,0},{2,3},{3,2},{4,5},{5,4},{6,7},{7,6},{8,9},{9,8},{10,11... | collective-permute-start | bytes 786440 | tf_op jit(solution)/shard_map/ppermute | solution.py:314
  27.2 0.0 collective-permute-done.6
  27.3 1.3 %collective-permute-start.7 = (bf16[64,1024]{1,0:T(8,128)(2,1)S(1)}, bf16[64,1024]{1,0:T(8,128)(2,1)S(1)}, u32[]{:S(2)}, u32[]{:S(2)}) collective-permute-start(bf16[64,1024]{1,0:T(8,128)(2,1)S(1)} %add_convert_fusion.3), channel_id=1, source_target_pairs={{0,2},{2,0},{1,3},{3,1},{4,6},{6,4},{5,7},{7,5},{8,10},{10,8},{9,1... | collective-permute-start | bytes 393224 | tf_op jit(solution)/shard_map/ppermute | solution.py:438
  28.6 0.0 collective-permute-done.8
  28.6 1.4 %collective-permute-start.9 = (bf16[64,1024]{1,0:T(8,128)(2,1)S(1)}, bf16[64,1024]{1,0:T(8,128)(2,1)S(1)}, u32[]{:S(2)}, u32[]{:S(2)}) collective-permute-start(bf16[64,1024]{1,0:T(8,128)(2,1)S(1)} %add_convert_fusion.1), channel_id=1, source_target_pairs={{0,2},{2,0},{1,3},{3,1},{4,6},{6,4},{5,7},{7,5},{8,10},{10,8},{9,1... | collective-permute-start | bytes 393224 | tf_op jit(solution)/shard_map/ppermute | solution.py:438
  30.0 3.7 %collective-permute-done.7 = bf16[64,1024]{1,0:T(8,128)(2,1)S(1)} collective-permute-done((bf16[64,1024]{1,0:T(8,128)(2,1)S(1)}, bf16[64,1024]{1,0:T(8,128)(2,1)S(1)}, u32[]{:S(2)}, u32[]{:S(2)}) %collective-permute-start.7) | collective-permute-done | bytes 131104 | tf_op jit(solution)/shard_map/ppermute | solution.py:438
  33.7 2.0 %collective-permute-done.9 = bf16[64,1024]{1,0:T(8,128)(2,1)S(1)} collective-permute-done((bf16[64,1024]{1,0:T(8,128)(2,1)S(1)}, bf16[64,1024]{1,0:T(8,128)(2,1)S(1)}, u32[]{:S(2)}, u32[]{:S(2)}) %collective-permute-start.9) | collective-permute-done | bytes 131104 | tf_op jit(solution)/shard_map/ppermute | solution.py:438
  35.8 0.7 %pad_maximum_fusion = bf16[128,1024]{1,0:T(8,128)(2,1)} fusion(bf16[64,1024]{1,0:T(8,128)(2,1)S(1)} %add_convert_fusion, bf16[64,1024]{1,0:T(8,128)(2,1)S(1)} %add_convert_fusion.2), kind=kLoop, calls=%fused_computation | loop fusion | flops 524288 | bytes 524288 | tf_op jit(solution)/shard_map/concatenate | solution.py:440
  (7 shorter events, 0.2 us)
Async XLA Ops:
  1.0 16.1 %collective-permute-start.1 = (bf16[512,256]{1,0:T(8,128)(2,1)S(1)}, bf16[512,256]{1,0:T(8,128)(2,1)S(1)}, u32[]{:S(2)}, u32[]{:S(2)}) collective-permute-start(bf16[512,256]{1,0:T(8,128)(2,1)S(1)} %own_states.1.refs_2_.refs_6_), channel_id=1, source_target_pairs={{0,8},{8,0},{4,12},{12,4},{1,9},{9,1},{5,13},{13,5},{2,10},{10,2},... | collective-permute-start | bytes 786440 | tf_op jit(solution)/shard_map/ppermute | solution.py:379
  5.1 12.6 %collective-permute-start = (bf16[512,256]{1,0:T(8,128)(2,1)S(1)}, bf16[512,256]{1,0:T(8,128)(2,1)S(1)}, u32[]{:S(2)}, u32[]{:S(2)}) collective-permute-start(bf16[512,256]{1,0:T(8,128)(2,1)S(1)} %own_states.1.refs_2_.refs_6_), channel_id=1, source_target_pairs={{0,4},{4,0},{8,12},{12,8},{1,5},{5,1},{9,13},{13,9},{2,6},{6,2},{1... | collective-permute-start | bytes 786440 | tf_op jit(solution)/shard_map/ppermute | solution.py:380
  7.9 10.9 %collective-permute-start.2 = (bf16[1568,128]{1,0:T(8,128)(2,1)S(1)}, bf16[1568,128]{1,0:T(8,128)(2,1)S(1)}, u32[]{:S(2)}, u32[]{:S(2)}) collective-permute-start(bf16[1568,128]{1,0:T(8,128)(2,1)S(1)} %pack_operators.1.refs_1_.refs_0_.refs_2_), channel_id=1, source_target_pairs={{0,2},{2,0},{1,3},{3,1},{4,6},{6,4},{5,7},{7,5},{8,10},{10,8},{9,1... | collective-permute-start | bytes 1204232 | tf_op jit(solution)/shard_map/ppermute | solution.py:381
  9.4 9.4 %collective-permute-start.3 = (bf16[1568,128]{1,0:T(8,128)(2,1)S(1)}, bf16[1568,128]{1,0:T(8,128)(2,1)S(1)}, u32[]{:S(2)}, u32[]{:S(2)}) collective-permute-start(bf16[1568,128]{1,0:T(8,128)(2,1)S(1)} %pack_operators.1.refs_1_.refs_0_.refs_2_), channel_id=1, source_target_pairs={{0,1},{1,0},{2,3},{3,2},{4,5},{5,4},{6,7},{7,6},{8,9},{9,8},{10,11... | collective-permute-start | bytes 1204232 | tf_op jit(solution)/shard_map/ppermute | solution.py:314
  17.1 7.4 %collective-permute-start.5 = (bf16[512,256]{1,0:T(8,128)(2,1)S(1)}, bf16[512,256]{1,0:T(8,128)(2,1)S(1)}, u32[]{:S(2)}, u32[]{:S(2)}) collective-permute-start(bf16[512,256]{1,0:T(8,128)(2,1)S(1)} %collective-permute-done.1.refs_4_.refs_8_), channel_id=1, source_target_pairs={{0,4},{4,0},{8,12},{12,8},{1,5},{5,1},{9,13},{13,9},{2,6},{6,2},{1... | collective-permute-start | bytes 786440 | tf_op jit(solution)/shard_map/ppermute | solution.py:392
  18.8 2.2 %collective-permute-start.4 = (bf16[1568,128]{1,0:T(8,128)(2,1)S(1)}, bf16[1568,128]{1,0:T(8,128)(2,1)S(1)}, u32[]{:S(2)}, u32[]{:S(2)}) collective-permute-start(bf16[1568,128]{1,0:T(8,128)(2,1)S(1)} %collective-permute-done.2.refs_4_), channel_id=1, source_target_pairs={{0,1},{1,0},{2,3},{3,2},{4,5},{5,4},{6,7},{7,6},{8,9},{9,8},{10,11... | collective-permute-start | bytes 1204232 | tf_op jit(solution)/shard_map/ppermute | solution.py:314
  25.6 1.7 %collective-permute-start.6 = (bf16[64,2048]{1,0:T(8,128)(2,1)S(1)}, bf16[64,2048]{1,0:T(8,128)(2,1)S(1)}, u32[]{:S(2)}, u32[]{:S(2)}) collective-permute-start(bf16[64,2048]{1,0:T(8,128)(2,1)S(1)} %get-tuple-element.52), channel_id=1, source_target_pairs={{0,1},{1,0},{2,3},{3,2},{4,5},{5,4},{6,7},{7,6},{8,9},{9,8},{10,11... | collective-permute-start | bytes 786440 | tf_op jit(solution)/shard_map/ppermute | solution.py:314
  26.8 1.8 %collective-permute-start.8 = (bf16[64,2048]{1,0:T(8,128)(2,1)S(1)}, bf16[64,2048]{1,0:T(8,128)(2,1)S(1)}, u32[]{:S(2)}, u32[]{:S(2)}) collective-permute-start(bf16[64,2048]{1,0:T(8,128)(2,1)S(1)} %get-tuple-element.55), channel_id=1, source_target_pairs={{0,1},{1,0},{2,3},{3,2},{4,5},{5,4},{6,7},{7,6},{8,9},{9,8},{10,11... | collective-permute-start | bytes 786440 | tf_op jit(solution)/shard_map/ppermute | solution.py:314
  27.3 6.4 %collective-permute-start.7 = (bf16[64,1024]{1,0:T(8,128)(2,1)S(1)}, bf16[64,1024]{1,0:T(8,128)(2,1)S(1)}, u32[]{:S(2)}, u32[]{:S(2)}) collective-permute-start(bf16[64,1024]{1,0:T(8,128)(2,1)S(1)} %add_convert_fusion.3), channel_id=1, source_target_pairs={{0,2},{2,0},{1,3},{3,1},{4,6},{6,4},{5,7},{7,5},{8,10},{10,8},{9,1... | collective-permute-start | bytes 393224 | tf_op jit(solution)/shard_map/ppermute | solution.py:438
  28.6 7.1 %collective-permute-start.9 = (bf16[64,1024]{1,0:T(8,128)(2,1)S(1)}, bf16[64,1024]{1,0:T(8,128)(2,1)S(1)}, u32[]{:S(2)}, u32[]{:S(2)}) collective-permute-start(bf16[64,1024]{1,0:T(8,128)(2,1)S(1)} %add_convert_fusion.1), channel_id=1, source_target_pairs={{0,2},{2,0},{1,3},{3,1},{4,6},{6,4},{5,7},{7,5},{8,10},{10,8},{9,1... | collective-permute-start | bytes 393224 | tf_op jit(solution)/shard_map/ppermute | solution.py:438

commit v6 on v5

--- a/solution.py
+++ b/solution.py
@@ -196,6 +196,15 @@
         )
 
 
+def chosen_products(terms, numbers, pack, shards, c_ref, starts):
+    block = pack.shape[-1]
+    for w in range(terms):
+        row = pl.multiple_of(numbers[0, w] * block, block)
+        left = pack[w * block : (w + 1) * block, :]
+        for start, shard in zip(starts, shards):
+            c_ref[start + w] = matmul(left, shard[pl.ds(row, block), :]).astype(BF16)
+
+
 def right_products(terms, w_ref, c_ref, y_ref, starts):
     tiles = y_ref.shape[0]
     for w in range(terms):
@@ -244,7 +253,10 @@
     first = plan.last * c_ref.shape[1] if last else 0
     for k in plan.used:
         sources = [shards[q] for q, pack in plan.chunks if pack == k]
-        left_products(lefts[k], sources, c_ref, starts[k], first)
+        if k in plan.made:
+            chosen_products(terms, numbers[k], packs[k], sources, c_ref, starts[k])
+        else:
+            left_products(lefts[k], sources, c_ref, starts[k], first)
     for k in plan.used:
         right_products(terms, rights_of[k], c_ref, y_ref, starts[k])
     for i in range(y_ref.shape[0]):

time: 36.7 us -> 36.5 us (level)
  waiting for transfers between devices: 12 us -> 13.1 us
  Pallas kernels: 12.2 us -> 11.3 us
    pallas_call x6, Pallas kernels: 10.1 us -> 9.09 us  [run(): call(functools.partial(terms_body, terms, rights, phys, plan), tuple(shap...]
    ppermute x1, waiting for transfers between devices: 0.34 us -> 1.06 us  [by_states(): farthest = lax.ppermute(far, 'blk', NEAR)]
  transfers between devices with their start and end apart: 10 -> 10, of which waited for: 4 -> 4; matrix products, arithmetic and copies ran while one was open for 0% -> 0% of each run, Pallas kernels for 28% -> 25%
where the time goes in v6:
time: 36.5 us; the launch traced here: 36.4 us
  waiting for transfers between devices  13.1 us (36%)
  Pallas kernels  11.3 us (31%)
  starting transfers between devices  11 us (30%)
  other arithmetic  0.89 us (2%)
    pallas_call x6, Pallas kernels, run(): call(functools.partial(terms_body, terms, rights, phys, plan), tuple(shap...  9.09 us
    ppermute x1, waiting for transfers between devices, by_states(): far = lax.ppermute(mine, 'blk', FAR)  6.22 us
    ppermute x2, waiting for transfers between devices, by_states(): taken = lax.ppermute(send, 'mpo', ACROSS)  5.8 us
    ppermute x1, starting transfers between devices, by_states(): far = lax.ppermute(mine, 'blk', FAR)  4.1 us
    ppermute x2, starting transfers between devices, by_states(): taken = lax.ppermute(send, 'mpo', ACROSS)  2.44 us
    ppermute x1, starting transfers between devices, by_states(): near = lax.ppermute(mine, 'blk', NEAR)  1.58 us
    ppermute x1, starting transfers between devices, by_states(): pack_x = lax.ppermute(pack, 'mpo', ACROSS)  1.56 us
    pallas_call x1, Pallas kernels, by_states(): call(functools.partial(pack_body, terms, rights, phys), jax.ShapeDtypeStr...  1.23 us
  transfers between devices with their start and end apart: 10, of which 4 were waited for; matrix products, arithmetic and copies ran while one was open for 0% of the time, Pallas kernels for 25%

profile of v6, /device:TPU:0, one launch (start us, length us, event | category | flops | bytes accessed | tf_op | source)
XLA Modules:
  0.0 36.4 jit_solution(2298663270814276417)
XLA Ops:
  0.0 1.0 %own_states.1.refs_2_.refs_6_ = bf16[512,256]{1,0:T(8,128)(2,1)S(1)} custom-call(bf16[512,1024]{1,0:T(8,128)(2,1)} %wave_ref.1), custom_call_target="tpu_custom_call" | custom-call | flops 1000 | bytes 1000 | tf_op jit(solution)/shard_map/own_states/pallas_call | solution.py:315
  1.0 4.1 %collective-permute-start.1 = (bf16[512,256]{1,0:T(8,128)(2,1)S(1)}, bf16[512,256]{1,0:T(8,128)(2,1)S(1)}, u32[]{:S(2)}, u32[]{:S(2)}) collective-permute-start(bf16[512,256]{1,0:T(8,128)(2,1)S(1)} %own_states.1.refs_2_.refs_6_), channel_id=1, source_target_pairs={{0,8},{8,0},{4,12},{12,4},{1,9},{9,1},{5,13},{13,5},{2,10},{10,2},... | collective-permute-start | bytes 786440 | tf_op jit(solution)/shard_map/ppermute | solution.py:391
  5.1 1.6 %collective-permute-start = (bf16[512,256]{1,0:T(8,128)(2,1)S(1)}, bf16[512,256]{1,0:T(8,128)(2,1)S(1)}, u32[]{:S(2)}, u32[]{:S(2)}) collective-permute-start(bf16[512,256]{1,0:T(8,128)(2,1)S(1)} %own_states.1.refs_2_.refs_6_), channel_id=1, source_target_pairs={{0,4},{4,0},{8,12},{12,8},{1,5},{5,1},{9,13},{13,9},{2,6},{6,2},{1... | collective-permute-start | bytes 786440 | tf_op jit(solution)/shard_map/ppermute | solution.py:392
  6.6 1.2 %pack_operators.1.refs_1_.refs_0_.refs_2_ = bf16[1568,128]{1,0:T(8,128)(2,1)S(1)} custom-call(bf16[4,1,128,128]{3,2,1,0:T(8,128)(2,1)} %left_hbm.1, bf16[4,2,128,128]{3,2,1,0:T(8,128)(2,1)} %right_hbm.1, bf16[4,16,16]{2,1,0:T(8,128)(2,1)} %site_hbm.1, s32[4,4]{1,0:T(4,128)} %sources_hbm.1, s32[2,4]{1,0:T(2,128)} %bitcast.2, s32[2,4]{1,0:T(2,128)} %bitcast.3), custom_call_target="tpu_custom_call" | custom-call | flops 1000 | bytes 1000 | tf_op jit(solution)/shard_map/pack_operators/pallas_call | solution.py:328
  7.9 1.6 %collective-permute-start.2 = (bf16[1568,128]{1,0:T(8,128)(2,1)S(1)}, bf16[1568,128]{1,0:T(8,128)(2,1)S(1)}, u32[]{:S(2)}, u32[]{:S(2)}) collective-permute-start(bf16[1568,128]{1,0:T(8,128)(2,1)S(1)} %pack_operators.1.refs_1_.refs_0_.refs_2_), channel_id=1, source_target_pairs={{0,2},{2,0},{1,3},{3,1},{4,6},{6,4},{5,7},{7,5},{8,10},{10,8},{9,1... | collective-permute-start | bytes 1204232 | tf_op jit(solution)/shard_map/ppermute | solution.py:393
  9.4 0.0 collective-permute-start.3
  9.4 1.4 %own_pack_own_shard.1 = (bf16[4,128,512]{2,1,0:T(8,128)(2,1)S(1)}, bf16[4,256,256]{2,1,0:T(8,128)(2,1)S(1)}, f32[8,256,256]{2,1,0:T(8,128)S(1)}) custom-call(s32[1,128]{1,0:T(1,128)S(1)} %slice_convert_fusion.1.refs_0_, bf16[1568,128]{1,0:T(8,128)(2,1)S(1)} %pack_operators.1.refs_1_.refs_0_.refs_2_, bf16[512,256]{1,0:T(8,128)(2,1)S(1)} %own_states.1.refs_2_.refs_6_), custom_call_target="tpu_custom_call" | custom-call | flops 1000 | bytes 1000 | tf_op jit(solution)/shard_map/own_pack_own_shard/pallas_call | solution.py:380
  10.9 6.2 %collective-permute-done.1.refs_4_.refs_8_ = bf16[512,256]{1,0:T(8,128)(2,1)S(1)} collective-permute-done((bf16[512,256]{1,0:T(8,128)(2,1)S(1)}, bf16[512,256]{1,0:T(8,128)(2,1)S(1)}, u32[]{:S(2)}, u32[]{:S(2)}) %collective-permute-start.1) | collective-permute-done | bytes 262176 | tf_op jit(solution)/shard_map/ppermute | solution.py:391
  17.1 0.6 %collective-permute-start.5 = (bf16[512,256]{1,0:T(8,128)(2,1)S(1)}, bf16[512,256]{1,0:T(8,128)(2,1)S(1)}, u32[]{:S(2)}, u32[]{:S(2)}) collective-permute-start(bf16[512,256]{1,0:T(8,128)(2,1)S(1)} %collective-permute-done.1.refs_4_.refs_8_), channel_id=1, source_target_pairs={{0,4},{4,0},{8,12},{12,8},{1,5},{5,1},{9,13},{13,9},{2,6},{6,2},{1... | collective-permute-start | bytes 786440 | tf_op jit(solution)/shard_map/ppermute | solution.py:404
  17.7 0.0 collective-permute-done.refs_3_.refs_7_
  17.7 1.1 %own_pack_near_far.1.refs_5_ = f32[8,256,256]{2,1,0:T(8,128)S(1)} custom-call(bf16[1568,128]{1,0:T(8,128)(2,1)S(1)} %pack_operators.1.refs_1_.refs_0_.refs_2_, bf16[4,128,512]{2,1,0:T(8,128)(2,1)S(1)} %get-tuple-element.31.refs_1_.refs_0_, bf16[4,256,256]{2,1,0:T(8,128)(2,1)S(1)} %get-tuple-element.32.refs_2_.refs_4_, ...), custom_call_target="tpu_custom_call" | custom-call | flops 8000000000 | bytes 1000 | tf_op jit(solution)/shard_map/own_pack_near_far/pallas_call | solution.py:380
  18.8 0.0 collective-permute-done.2.refs_4_
  18.8 0.0 collective-permute-done.3.refs_1_.refs_3_
  18.8 0.1 collective-permute-start.4
  18.9 1.7 %core_pack.1 = (bf16[4,128,512]{2,1,0:T(8,128)(2,1)S(1)}, bf16[4,256,256]{2,1,0:T(8,128)(2,1)S(1)}, f32[8,256,256]{2,1,0:T(8,128)S(1)}) custom-call(s32[1,128]{1,0:T(1,128)S(1)} %get-tuple-element.58.refs_0_, bf16[1568,128]{1,0:T(8,128)(2,1)S(1)} %collective-permute-done.3.refs_1_.refs_3_, bf16[512,256]{1,0:T(8,128)(2,1)S(1)} %own_states.1.refs_2_.refs_6_, ...), custom_call_target="tpu_custom_call" | custom-call | flops 3000000000 | bytes 1000 | tf_op jit(solution)/shard_map/core_pack/pallas_call | solution.py:380
  20.7 0.0 collective-permute-done.4.refs_5_
  20.7 2.8 %other_packs.1 = (bf16[4,128,512]{2,1,0:T(8,128)(2,1)S(1)}, bf16[4,128,512]{2,1,0:T(8,128)(2,1)S(1)}, bf16[4,256,256]{2,1,0:T(8,128)(2,1)S(1)}, bf16[4,256,256]{...) custom-call(s32[1,128]{1,0:T(1,128)S(1)} %get-tuple-element.57.refs_0_, ...), custom_call_target="tpu_custom_call" | custom-call | flops 1000 | bytes 1000 | tf_op jit(solution)/shard_map/other_packs/pallas_call | solution.py:380
  23.5 1.1 %collective-permute-done.5.refs_8_ = bf16[512,256]{1,0:T(8,128)(2,1)S(1)} collective-permute-done((bf16[512,256]{1,0:T(8,128)(2,1)S(1)}, bf16[512,256]{1,0:T(8,128)(2,1)S(1)}, u32[]{:S(2)}, u32[]{:S(2)}) %collective-permute-start.5) | collective-permute-done | bytes 262176 | tf_op jit(solution)/shard_map/ppermute | solution.py:404
  24.5 1.0 %third_shard.2 = (bf16[64,2048]{1,0:T(8,128)(2,1)S(1)}, f32[64,1024]{1,0:T(8,128)S(1)}, f32[64,1024]{1,0:T(8,128)S(1)}) custom-call(bf16[4,128,512]{2,1,0:T(8,128)(2,1)S(1)} %get-tuple-element.31.refs_1_.refs_0_, bf16[4,128,512]{2,1,0:T(8,128)(2,1)S(1)} %get-tuple-element.39.refs_1_, bf16[4,128,512]{2,1,0:T(8,128)(2,1)S(1)} %get-tuple-element.42.refs_2_, ...), custom_call_target="tpu_custom_call" | custom-call | flops 1000 | bytes 1000 | tf_op jit(solution)/shard_map/third_shard/pallas_call | solution.py:380
  25.6 0.1 collective-permute-start.6
  25.6 1.0 %third_shard.3 = (bf16[64,2048]{1,0:T(8,128)(2,1)S(1)}, f32[64,1024]{1,0:T(8,128)S(1)}, f32[64,1024]{1,0:T(8,128)S(1)}) custom-call(bf16[4,128,512]{2,1,0:T(8,128)(2,1)S(1)} %get-tuple-element.31.refs_1_.refs_0_, bf16[4,128,512]{2,1,0:T(8,128)(2,1)S(1)} %get-tuple-element.39.refs_1_, bf16[4,128,512]{2,1,0:T(8,128)(2,1)S(1)} %get-tuple-element.42.refs_2_, ...), custom_call_target="tpu_custom_call" | custom-call | flops 1000 | bytes 1000 | tf_op jit(solution)/shard_map/third_shard/pallas_call | solution.py:380
  26.7 0.6 %collective-permute-start.8 = (bf16[64,2048]{1,0:T(8,128)(2,1)S(1)}, bf16[64,2048]{1,0:T(8,128)(2,1)S(1)}, u32[]{:S(2)}, u32[]{:S(2)}) collective-permute-start(bf16[64,2048]{1,0:T(8,128)(2,1)S(1)} %get-tuple-element.55), channel_id=1, source_target_pairs={{0,1},{1,0},{2,3},{3,2},{4,5},{5,4},{6,7},{7,6},{8,9},{9,8},{10,11... | collective-permute-start | bytes 786440 | tf_op jit(solution)/shard_map/ppermute | solution.py:326
  27.2 0.0 collective-permute-done.6
  27.3 1.3 %collective-permute-start.7 = (bf16[64,1024]{1,0:T(8,128)(2,1)S(1)}, bf16[64,1024]{1,0:T(8,128)(2,1)S(1)}, u32[]{:S(2)}, u32[]{:S(2)}) collective-permute-start(bf16[64,1024]{1,0:T(8,128)(2,1)S(1)} %add_convert_fusion.3), channel_id=1, source_target_pairs={{0,2},{2,0},{1,3},{3,1},{4,6},{6,4},{5,7},{7,5},{8,10},{10,8},{9,1... | collective-permute-start | bytes 393224 | tf_op jit(solution)/shard_map/ppermute | solution.py:450
  28.6 0.0 collective-permute-done.8
  28.6 1.1 %collective-permute-start.9 = (bf16[64,1024]{1,0:T(8,128)(2,1)S(1)}, bf16[64,1024]{1,0:T(8,128)(2,1)S(1)}, u32[]{:S(2)}, u32[]{:S(2)}) collective-permute-start(bf16[64,1024]{1,0:T(8,128)(2,1)S(1)} %add_convert_fusion.1), channel_id=1, source_target_pairs={{0,2},{2,0},{1,3},{3,1},{4,6},{6,4},{5,7},{7,5},{8,10},{10,8},{9,1... | collective-permute-start | bytes 393224 | tf_op jit(solution)/shard_map/ppermute | solution.py:450
  29.8 3.9 %collective-permute-done.7 = bf16[64,1024]{1,0:T(8,128)(2,1)S(1)} collective-permute-done((bf16[64,1024]{1,0:T(8,128)(2,1)S(1)}, bf16[64,1024]{1,0:T(8,128)(2,1)S(1)}, u32[]{:S(2)}, u32[]{:S(2)}) %collective-permute-start.7) | collective-permute-done | bytes 131104 | tf_op jit(solution)/shard_map/ppermute | solution.py:450
  33.8 1.9 %collective-permute-done.9 = bf16[64,1024]{1,0:T(8,128)(2,1)S(1)} collective-permute-done((bf16[64,1024]{1,0:T(8,128)(2,1)S(1)}, bf16[64,1024]{1,0:T(8,128)(2,1)S(1)}, u32[]{:S(2)}, u32[]{:S(2)}) %collective-permute-start.9) | collective-permute-done | bytes 131104 | tf_op jit(solution)/shard_map/ppermute | solution.py:450
  35.7 0.7 %pad_maximum_fusion = bf16[128,1024]{1,0:T(8,128)(2,1)} fusion(bf16[64,1024]{1,0:T(8,128)(2,1)S(1)} %add_convert_fusion, bf16[64,1024]{1,0:T(8,128)(2,1)S(1)} %add_convert_fusion.2), kind=kLoop, calls=%fused_computation | loop fusion | flops 524288 | bytes 524288 | tf_op jit(solution)/shard_map/concatenate | solution.py:452
  (7 shorter events, 0.2 us)
Async XLA Ops:
  1.0 16.1 %collective-permute-start.1 = (bf16[512,256]{1,0:T(8,128)(2,1)S(1)}, bf16[512,256]{1,0:T(8,128)(2,1)S(1)}, u32[]{:S(2)}, u32[]{:S(2)}) collective-permute-start(bf16[512,256]{1,0:T(8,128)(2,1)S(1)} %own_states.1.refs_2_.refs_6_), channel_id=1, source_target_pairs={{0,8},{8,0},{4,12},{12,4},{1,9},{9,1},{5,13},{13,5},{2,10},{10,2},... | collective-permute-start | bytes 786440 | tf_op jit(solution)/shard_map/ppermute | solution.py:391
  5.1 12.6 %collective-permute-start = (bf16[512,256]{1,0:T(8,128)(2,1)S(1)}, bf16[512,256]{1,0:T(8,128)(2,1)S(1)}, u32[]{:S(2)}, u32[]{:S(2)}) collective-permute-start(bf16[512,256]{1,0:T(8,128)(2,1)S(1)} %own_states.1.refs_2_.refs_6_), channel_id=1, source_target_pairs={{0,4},{4,0},{8,12},{12,8},{1,5},{5,1},{9,13},{13,9},{2,6},{6,2},{1... | collective-permute-start | bytes 786440 | tf_op jit(solution)/shard_map/ppermute | solution.py:392
  7.9 10.9 %collective-permute-start.2 = (bf16[1568,128]{1,0:T(8,128)(2,1)S(1)}, bf16[1568,128]{1,0:T(8,128)(2,1)S(1)}, u32[]{:S(2)}, u32[]{:S(2)}) collective-permute-start(bf16[1568,128]{1,0:T(8,128)(2,1)S(1)} %pack_operators.1.refs_1_.refs_0_.refs_2_), channel_id=1, source_target_pairs={{0,2},{2,0},{1,3},{3,1},{4,6},{6,4},{5,7},{7,5},{8,10},{10,8},{9,1... | collective-permute-start | bytes 1204232 | tf_op jit(solution)/shard_map/ppermute | solution.py:393
  9.4 9.4 %collective-permute-start.3 = (bf16[1568,128]{1,0:T(8,128)(2,1)S(1)}, bf16[1568,128]{1,0:T(8,128)(2,1)S(1)}, u32[]{:S(2)}, u32[]{:S(2)}) collective-permute-start(bf16[1568,128]{1,0:T(8,128)(2,1)S(1)} %pack_operators.1.refs_1_.refs_0_.refs_2_), channel_id=1, source_target_pairs={{0,1},{1,0},{2,3},{3,2},{4,5},{5,4},{6,7},{7,6},{8,9},{9,8},{10,11... | collective-permute-start | bytes 1204232 | tf_op jit(solution)/shard_map/ppermute | solution.py:326
  17.1 7.4 %collective-permute-start.5 = (bf16[512,256]{1,0:T(8,128)(2,1)S(1)}, bf16[512,256]{1,0:T(8,128)(2,1)S(1)}, u32[]{:S(2)}, u32[]{:S(2)}) collective-permute-start(bf16[512,256]{1,0:T(8,128)(2,1)S(1)} %collective-permute-done.1.refs_4_.refs_8_), channel_id=1, source_target_pairs={{0,4},{4,0},{8,12},{12,8},{1,5},{5,1},{9,13},{13,9},{2,6},{6,2},{1... | collective-permute-start | bytes 786440 | tf_op jit(solution)/shard_map/ppermute | solution.py:404
  18.8 1.8 %collective-permute-start.4 = (bf16[1568,128]{1,0:T(8,128)(2,1)S(1)}, bf16[1568,128]{1,0:T(8,128)(2,1)S(1)}, u32[]{:S(2)}, u32[]{:S(2)}) collective-permute-start(bf16[1568,128]{1,0:T(8,128)(2,1)S(1)} %collective-permute-done.2.refs_4_), channel_id=1, source_target_pairs={{0,1},{1,0},{2,3},{3,2},{4,5},{5,4},{6,7},{7,6},{8,9},{9,8},{10,11... | collective-permute-start | bytes 1204232 | tf_op jit(solution)/shard_map/ppermute | solution.py:326
  25.6 1.7 %collective-permute-start.6 = (bf16[64,2048]{1,0:T(8,128)(2,1)S(1)}, bf16[64,2048]{1,0:T(8,128)(2,1)S(1)}, u32[]{:S(2)}, u32[]{:S(2)}) collective-permute-start(bf16[64,2048]{1,0:T(8,128)(2,1)S(1)} %get-tuple-element.52), channel_id=1, source_target_pairs={{0,1},{1,0},{2,3},{3,2},{4,5},{5,4},{6,7},{7,6},{8,9},{9,8},{10,11... | collective-permute-start | bytes 786440 | tf_op jit(solution)/shard_map/ppermute | solution.py:326
  26.7 1.9 %collective-permute-start.8 = (bf16[64,2048]{1,0:T(8,128)(2,1)S(1)}, bf16[64,2048]{1,0:T(8,128)(2,1)S(1)}, u32[]{:S(2)}, u32[]{:S(2)}) collective-permute-start(bf16[64,2048]{1,0:T(8,128)(2,1)S(1)} %get-tuple-element.55), channel_id=1, source_target_pairs={{0,1},{1,0},{2,3},{3,2},{4,5},{5,4},{6,7},{7,6},{8,9},{9,8},{10,11... | collective-permute-start | bytes 786440 | tf_op jit(solution)/shard_map/ppermute | solution.py:326
  27.3 6.4 %collective-permute-start.7 = (bf16[64,1024]{1,0:T(8,128)(2,1)S(1)}, bf16[64,1024]{1,0:T(8,128)(2,1)S(1)}, u32[]{:S(2)}, u32[]{:S(2)}) collective-permute-start(bf16[64,1024]{1,0:T(8,128)(2,1)S(1)} %add_convert_fusion.3), channel_id=1, source_target_pairs={{0,2},{2,0},{1,3},{3,1},{4,6},{6,4},{5,7},{7,5},{8,10},{10,8},{9,1... | collective-permute-start | bytes 393224 | tf_op jit(solution)/shard_map/ppermute | solution.py:450
  28.6 7.0 %collective-permute-start.9 = (bf16[64,1024]{1,0:T(8,128)(2,1)S(1)}, bf16[64,1024]{1,0:T(8,128)(2,1)S(1)}, u32[]{:S(2)}, u32[]{:S(2)}) collective-permute-start(bf16[64,1024]{1,0:T(8,128)(2,1)S(1)} %add_convert_fusion.1), channel_id=1, source_target_pairs={{0,2},{2,0},{1,3},{3,1},{4,6},{6,4},{5,7},{7,5},{8,10},{10,8},{9,1... | collective-permute-start | bytes 393224 | tf_op jit(solution)/shard_map/ppermute | solution.py:450

commit v7 on v6

--- a/solution.py
+++ b/solution.py
@@ -278,6 +278,40 @@
                 ].astype(target.dtype)
 
 
+def third_body(terms, packs, *refs):
+    lefts, rights_of, (shard, acc_in, kron_ref) = refs[:packs], refs[packs : 2 * packs], refs[2 * packs : 2 * packs + 3]
+    (*gives, y_ref), c_ref = refs[2 * packs + 3 : -1], refs[-1]
+    for k in range(packs):
+        left_products(lefts[k], [shard], c_ref, [k * terms], 0)
+    for k in range(packs):
+        right_products(terms, rights_of[k], c_ref, y_ref, [k * terms])
+    quarter = kron_ref.shape[0] // 4
+    tiles = y_ref.shape[0]
+    for i in range(tiles):
+        total = matmul(kron_ref[0:quarter, :], y_ref[i]) + acc_in[i, 0:quarter, :]
+        put_tile(gives, i, tiles, total)
+
+
+def put_tile(targets, tile, tiles, total):
+    each = tiles // len(targets)
+    target, first = targets[tile // each], tile % each * SUB
+    width = total.shape[1]
+    for m in range(total.shape[0] // SUB):
+        target[first : first + SUB, m * width : (m + 1) * width] = total[
+            m * SUB : (m + 1) * SUB, :
+        ].astype(target.dtype)
+
+
+def sums_body(y_ref, acc_in, kron_ref, core_ref, *refs):
+    keeps_x, keep_ref = refs[:-1], refs[-1]
+    quarter = kron_ref.shape[0] // 4
+    tiles = y_ref.shape[0]
+    for i in range(tiles):
+        total = matmul(kron_ref[quarter:, :], y_ref[i]) + acc_in[i, quarter:, :]
+        for n, targets in enumerate(((core_ref,), keeps_x, (keep_ref,))):
+            put_tile(targets, i, tiles, total[n * quarter : (n + 1) * quarter, :])
+
+
 def in_hbm(x):
     return pltpu.with_memory_space_constraint(x, pltpu.HBM)
 
@@ -432,24 +466,40 @@
         acc,
     )
     farthest, acc = lax.optimization_barrier((farthest, acc))
-    outs = []
-    for part in range(PARTS):
-        give, keep_x, keep = run(
-            "third_shard",
-            Plan(4, [(3, k) for k in range(4)], last=part),
-            (),
-            (),
-            (farthest,),
-            acc,
-            (own, core, across, beyond),
-            kron,
-        )
-        columns = keep.shape[1]
-        back = swap(give)
-        send = (keep_x + back[:, :columns].astype(F32)).astype(BF16)
-        taken = lax.ppermute(send, "mpo", ACROSS)
-        outs.append((keep + back[:, columns:].astype(F32) + taken.astype(F32)).astype(BF16))
-    return jnp.concatenate(outs, axis=0) if PARTS > 1 else outs[0]
+    given = (own, core, across, beyond)
+    columns = phys // slots * width
+    part_shape = (block // PARTS, columns)
+    *gives, y = call(
+        functools.partial(third_body, terms, len(given)),
+        (
+            *[jax.ShapeDtypeStruct(part_shape, BF16)] * PARTS,
+            jax.ShapeDtypeStruct((tiles, len(given) * one_pack, width), BF16),
+        ),
+        [vmem] * (2 * len(given) + 3),
+        [pltpu.VMEM((len(given) * terms, block, width), BF16)],
+        name="third_shard",
+    )(*[g[0] for g in given], *[g[1] for g in given], farthest, acc, kron)
+    core_sum, *keeps_x, keep = call(
+        sums_body,
+        (
+            jax.ShapeDtypeStruct((block, columns), BF16),
+            *[jax.ShapeDtypeStruct(part_shape, F32)] * PARTS,
+            jax.ShapeDtypeStruct((block, columns), F32),
+        ),
+        [vmem] * 3,
+        name="sums",
+    )(y, acc, kron)
+    taken = []
+    for give, keep_x in zip(gives, keeps_x):
+        send = (keep_x + swap(give).astype(F32)).astype(BF16)
+        taken.append(lax.ppermute(send, "mpo", ACROSS))
+    kept = keep + swap(core_sum).astype(F32)
+    size = block // PARTS
+    outs = [
+        (kept[n * size : (n + 1) * size] + part.astype(F32)).astype(BF16)
+        for n, part in enumerate(taken)
+    ]
+    return jnp.concatenate(outs, axis=0)
 
 
 def solution(mesh):

time: 36.5 us -> 36.6 us (level)
  waiting for transfers between devices: 13.1 us -> 13.8 us
  Pallas kernels: 11.3 us -> 10.9 us
    pallas_call x6 -> x4, Pallas kernels: 9.09 us -> 7.05 us  [run(): call(functools.partial(terms_body, terms, rights, phys, plan), tuple(shap...]
    pallas_call x0 -> x2, Pallas kernels: none -> 1.63 us  [the longest x1 1.26 us: by_states(): call(functools.partial(third_body, terms, len(given)), (*[jax.ShapeDtypeS...]
    ppermute x4 -> x5, starting transfers between devices: 0.7 us -> 0.78 us  [swap(): return lax.ppermute(x, 'mpo', CORE)]
  transfers between devices with their start and end apart: 10 -> 11, of which waited for: 4 -> 5; matrix products, arithmetic and copies ran while one was open for 0% -> 0% of each run, Pallas kernels for 25% -> 24%
where the time goes in v7:
time: 36.6 us; the launch traced here: 36.4 us
  waiting for transfers between devices  13.8 us (38%)
  Pallas kernels  10.9 us (30%)
  starting transfers between devices  10.8 us (30%)
  other arithmetic  0.91 us (2%)
    pallas_call x4, Pallas kernels, run(): call(functools.partial(terms_body, terms, rights, phys, plan), tuple(shap...  7.05 us
    ppermute x1, waiting for transfers between devices, by_states(): far = lax.ppermute(mine, 'blk', FAR)  6.22 us
    ppermute x2, waiting for transfers between devices, by_states(): taken.append(lax.ppermute(send, 'mpo', ACROSS))  6.17 us
    ppermute x1, starting transfers between devices, by_states(): far = lax.ppermute(mine, 'blk', FAR)  4.1 us
    ppermute x2, starting transfers between devices, by_states(): taken.append(lax.ppermute(send, 'mpo', ACROSS))  2.16 us
    ppermute x1, starting transfers between devices, by_states(): near = lax.ppermute(mine, 'blk', NEAR)  1.58 us
    ppermute x1, starting transfers between devices, by_states(): pack_x = lax.ppermute(pack, 'mpo', ACROSS)  1.56 us
    pallas_call x1, Pallas kernels, by_states(): call(functools.partial(third_body, terms, len(given)), (*[jax.ShapeDtypeS...  1.26 us
  transfers between devices with their start and end apart: 11, of which 5 were waited for; matrix products, arithmetic and copies ran while one was open for 0% of the time, Pallas kernels for 24%

profile of v7, /device:TPU:0, one launch (start us, length us, event | category | flops | bytes accessed | tf_op | source)
XLA Modules:
  0.0 36.4 jit_solution(17594762225794746622)
XLA Ops:
  0.0 1.0 %own_states.1.refs_2_.refs_6_ = bf16[512,256]{1,0:T(8,128)(2,1)S(1)} custom-call(bf16[512,1024]{1,0:T(8,128)(2,1)} %wave_ref.1), custom_call_target="tpu_custom_call" | custom-call | flops 1000 | bytes 1000 | tf_op jit(solution)/shard_map/own_states/pallas_call | solution.py:349
  1.0 4.1 %collective-permute-start.1 = (bf16[512,256]{1,0:T(8,128)(2,1)S(1)}, bf16[512,256]{1,0:T(8,128)(2,1)S(1)}, u32[]{:S(2)}, u32[]{:S(2)}) collective-permute-start(bf16[512,256]{1,0:T(8,128)(2,1)S(1)} %own_states.1.refs_2_.refs_6_), channel_id=1, source_target_pairs={{0,8},{8,0},{4,12},{12,4},{1,9},{9,1},{5,13},{13,5},{2,10},{10,2},... | collective-permute-start | bytes 786440 | tf_op jit(solution)/shard_map/ppermute | solution.py:425
  5.1 1.6 %collective-permute-start = (bf16[512,256]{1,0:T(8,128)(2,1)S(1)}, bf16[512,256]{1,0:T(8,128)(2,1)S(1)}, u32[]{:S(2)}, u32[]{:S(2)}) collective-permute-start(bf16[512,256]{1,0:T(8,128)(2,1)S(1)} %own_states.1.refs_2_.refs_6_), channel_id=1, source_target_pairs={{0,4},{4,0},{8,12},{12,8},{1,5},{5,1},{9,13},{13,9},{2,6},{6,2},{1... | collective-permute-start | bytes 786440 | tf_op jit(solution)/shard_map/ppermute | solution.py:426
  6.6 1.2 %pack_operators.1.refs_1_.refs_0_.refs_2_ = bf16[1568,128]{1,0:T(8,128)(2,1)S(1)} custom-call(bf16[4,1,128,128]{3,2,1,0:T(8,128)(2,1)} %left_hbm.1, bf16[4,2,128,128]{3,2,1,0:T(8,128)(2,1)} %right_hbm.1, bf16[4,16,16]{2,1,0:T(8,128)(2,1)} %site_hbm.1, s32[4,4]{1,0:T(4,128)} %sources_hbm.1, s32[2,4]{1,0:T(2,128)} %bitcast.2, s32[2,4]{1,0:T(2,128)} %bitcast.3), custom_call_target="tpu_custom_call" | custom-call | flops 1000 | bytes 1000 | tf_op jit(solution)/shard_map/pack_operators/pallas_call | solution.py:362
  7.9 1.6 %collective-permute-start.2 = (bf16[1568,128]{1,0:T(8,128)(2,1)S(1)}, bf16[1568,128]{1,0:T(8,128)(2,1)S(1)}, u32[]{:S(2)}, u32[]{:S(2)}) collective-permute-start(bf16[1568,128]{1,0:T(8,128)(2,1)S(1)} %pack_operators.1.refs_1_.refs_0_.refs_2_), channel_id=1, source_target_pairs={{0,2},{2,0},{1,3},{3,1},{4,6},{6,4},{5,7},{7,5},{8,10},{10,8},{9,1... | collective-permute-start | bytes 1204232 | tf_op jit(solution)/shard_map/ppermute | solution.py:427
  9.4 0.0 collective-permute-start.3
  9.4 1.4 %own_pack_own_shard.1 = (bf16[4,128,512]{2,1,0:T(8,128)(2,1)S(1)}, bf16[4,256,256]{2,1,0:T(8,128)(2,1)S(1)}, f32[8,256,256]{2,1,0:T(8,128)S(1)}) custom-call(s32[1,128]{1,0:T(1,128)S(1)} %slice_convert_fusion.1.refs_0_, bf16[1568,128]{1,0:T(8,128)(2,1)S(1)} %pack_operators.1.refs_1_.refs_0_.refs_2_, bf16[512,256]{1,0:T(8,128)(2,1)S(1)} %own_states.1.refs_2_.refs_6_), custom_call_target="tpu_custom_call" | custom-call | flops 1000 | bytes 1000 | tf_op jit(solution)/shard_map/own_pack_own_shard/pallas_call | solution.py:414
  10.9 6.2 %collective-permute-done.1.refs_4_.refs_8_ = bf16[512,256]{1,0:T(8,128)(2,1)S(1)} collective-permute-done((bf16[512,256]{1,0:T(8,128)(2,1)S(1)}, bf16[512,256]{1,0:T(8,128)(2,1)S(1)}, u32[]{:S(2)}, u32[]{:S(2)}) %collective-permute-start.1) | collective-permute-done | bytes 262176 | tf_op jit(solution)/shard_map/ppermute | solution.py:425
  17.1 0.6 %collective-permute-start.5 = (bf16[512,256]{1,0:T(8,128)(2,1)S(1)}, bf16[512,256]{1,0:T(8,128)(2,1)S(1)}, u32[]{:S(2)}, u32[]{:S(2)}) collective-permute-start(bf16[512,256]{1,0:T(8,128)(2,1)S(1)} %collective-permute-done.1.refs_4_.refs_8_), channel_id=1, source_target_pairs={{0,4},{4,0},{8,12},{12,8},{1,5},{5,1},{9,13},{13,9},{2,6},{6,2},{1... | collective-permute-start | bytes 786440 | tf_op jit(solution)/shard_map/ppermute | solution.py:438
  17.7 0.0 collective-permute-done.refs_3_.refs_7_
  17.7 1.1 %own_pack_near_far.1.refs_5_ = f32[8,256,256]{2,1,0:T(8,128)S(1)} custom-call(bf16[1568,128]{1,0:T(8,128)(2,1)S(1)} %pack_operators.1.refs_1_.refs_0_.refs_2_, bf16[4,128,512]{2,1,0:T(8,128)(2,1)S(1)} %get-tuple-element.32.refs_1_.refs_0_, bf16[4,256,256]{2,1,0:T(8,128)(2,1)S(1)} %get-tuple-element.33.refs_2_.refs_4_, ...), custom_call_target="tpu_custom_call" | custom-call | flops 8000000000 | bytes 1000 | tf_op jit(solution)/shard_map/own_pack_near_far/pallas_call | solution.py:414
  18.8 0.0 collective-permute-done.2.refs_4_
  18.8 0.0 collective-permute-done.3.refs_1_.refs_3_
  18.8 0.1 collective-permute-start.4
  18.9 1.8 %core_pack.1 = (bf16[4,128,512]{2,1,0:T(8,128)(2,1)S(1)}, bf16[4,256,256]{2,1,0:T(8,128)(2,1)S(1)}, f32[8,256,256]{2,1,0:T(8,128)S(1)}) custom-call(s32[1,128]{1,0:T(1,128)S(1)} %get-tuple-element.62.refs_0_, bf16[1568,128]{1,0:T(8,128)(2,1)S(1)} %collective-permute-done.3.refs_1_.refs_3_, bf16[512,256]{1,0:T(8,128)(2,1)S(1)} %own_states.1.refs_2_.refs_6_, ...), custom_call_target="tpu_custom_call" | custom-call | flops 3000000000 | bytes 1000 | tf_op jit(solution)/shard_map/core_pack/pallas_call | solution.py:414
  20.7 0.0 collective-permute-done.4.refs_5_
  20.7 2.8 %other_packs.1 = (bf16[4,128,512]{2,1,0:T(8,128)(2,1)S(1)}, bf16[4,128,512]{2,1,0:T(8,128)(2,1)S(1)}, bf16[4,256,256]{2,1,0:T(8,128)(2,1)S(1)}, bf16[4,256,256]{...) custom-call(s32[1,128]{1,0:T(1,128)S(1)} %get-tuple-element.61.refs_0_, ...), custom_call_target="tpu_custom_call" | custom-call | flops 1000 | bytes 1000 | tf_op jit(solution)/shard_map/other_packs/pallas_call | solution.py:414
  23.5 1.0 %collective-permute-done.5.refs_8_ = bf16[512,256]{1,0:T(8,128)(2,1)S(1)} collective-permute-done((bf16[512,256]{1,0:T(8,128)(2,1)S(1)}, bf16[512,256]{1,0:T(8,128)(2,1)S(1)}, u32[]{:S(2)}, u32[]{:S(2)}) %collective-permute-start.5) | collective-permute-done | bytes 262176 | tf_op jit(solution)/shard_map/ppermute | solution.py:438
  24.5 1.3 %third_shard.1 = (bf16[64,1024]{1,0:T(8,128)(2,1)S(1)}, bf16[64,1024]{1,0:T(8,128)(2,1)S(1)}, bf16[8,256,256]{2,1,0:T(8,128)(2,1)S(1)}) custom-call(bf16[4,128,512]{2,1,0:T(8,128)(2,1)S(1)} %get-tuple-element.32.refs_1_.refs_0_, bf16[4,128,512]{2,1,0:T(8,128)(2,1)S(1)} %get-tuple-element.40.refs_1_, bf16[4,128,512]{2,1,0:T(8,128)(2,1)S(1)} %get-tuple-element.43.refs_2_, ...), custom_call_target="tpu_custom_call" | custom-call | flops 1000 | bytes 1000 | tf_op jit(solution)/shard_map/third_shard/pallas_call | solution.py:472
  25.8 0.1 collective-permute-start.9
  25.9 0.4 %sums.1 = (bf16[128,1024]{1,0:T(8,128)(2,1)S(1)}, f32[64,1024]{1,0:T(8,128)S(1)}, f32[64,1024]{1,0:T(8,128)S(1)}, f32[128,1024]{1,0:T(8,128)S(1)}) custom-call(bf16[8,256,256]{2,1,0:T(8,128)(2,1)S(1)} %get-tuple-element.52.y_ref, f32[8,256,256]{2,1,0:T(8,128)S(1)} %get-tuple-element.50.refs_9_.acc_in, bf16[256,256]{1,0:T(8,128)(2,1)S(1)} %get-tuple-element.51.refs_10_.kron_ref), custom_call_target="tpu_custom_call" | custom-call | flops 1000 | bytes 1000 | tf_op jit(solution)/shard_map/sums/pallas_call | solution.py:482
  26.2 0.6 %collective-permute-start.7 = (bf16[64,1024]{1,0:T(8,128)(2,1)S(1)}, bf16[64,1024]{1,0:T(8,128)(2,1)S(1)}, u32[]{:S(2)}, u32[]{:S(2)}) collective-permute-start(bf16[64,1024]{1,0:T(8,128)(2,1)S(1)} %get-tuple-element.56), channel_id=1, source_target_pairs={{0,1},{1,0},{2,3},{3,2},{4,5},{5,4},{6,7},{7,6},{8,9},{9,8},{10,11... | collective-permute-start | bytes 393224 | tf_op jit(solution)/shard_map/ppermute | solution.py:360
  26.8 0.1 collective-permute-start.6
  26.9 0.3 collective-permute-done.9
  27.2 1.3 %collective-permute-start.10 = (bf16[64,1024]{1,0:T(8,128)(2,1)S(1)}, bf16[64,1024]{1,0:T(8,128)(2,1)S(1)}, u32[]{:S(2)}, u32[]{:S(2)}) collective-permute-start(bf16[64,1024]{1,0:T(8,128)(2,1)S(1)} %add_convert_fusion), channel_id=1, source_target_pairs={{0,2},{2,0},{1,3},{3,1},{4,6},{6,4},{5,7},{7,5},{8,10},{10,8},{9,1... | collective-permute-start | bytes 393224 | tf_op jit(solution)/shard_map/ppermute | solution.py:495
  28.5 0.0 collective-permute-done.7
  28.6 0.8 %collective-permute-start.8 = (bf16[64,1024]{1,0:T(8,128)(2,1)S(1)}, bf16[64,1024]{1,0:T(8,128)(2,1)S(1)}, u32[]{:S(2)}, u32[]{:S(2)}) collective-permute-start(bf16[64,1024]{1,0:T(8,128)(2,1)S(1)} %add_convert_fusion.1), channel_id=1, source_target_pairs={{0,2},{2,0},{1,3},{3,1},{4,6},{6,4},{5,7},{7,5},{8,10},{10,8},{9,1... | collective-permute-start | bytes 393224 | tf_op jit(solution)/shard_map/ppermute | solution.py:495
  29.4 0.0 collective-permute-done.6
  29.4 0.1 convert_add_fusion
  29.5 4.2 %collective-permute-done.10 = bf16[64,1024]{1,0:T(8,128)(2,1)S(1)} collective-permute-done((bf16[64,1024]{1,0:T(8,128)(2,1)S(1)}, bf16[64,1024]{1,0:T(8,128)(2,1)S(1)}, u32[]{:S(2)}, u32[]{:S(2)}) %collective-permute-start.10) | collective-permute-done | bytes 131104 | tf_op jit(solution)/shard_map/ppermute | solution.py:495
  33.6 2.0 %collective-permute-done.8 = bf16[64,1024]{1,0:T(8,128)(2,1)S(1)} collective-permute-done((bf16[64,1024]{1,0:T(8,128)(2,1)S(1)}, bf16[64,1024]{1,0:T(8,128)(2,1)S(1)}, u32[]{:S(2)}, u32[]{:S(2)}) %collective-permute-start.8) | collective-permute-done | bytes 131104 | tf_op jit(solution)/shard_map/ppermute | solution.py:495
  35.6 0.1 fusion.1
  35.7 0.7 %pad_maximum_fusion = bf16[128,1024]{1,0:T(8,128)(2,1)} fusion(bf16[64,1024]{1,0:T(8,128)(2,1)S(1)} %get-tuple-element.60, bf16[64,1024]{1,0:T(8,128)(2,1)S(1)} %get-tuple-element.59), kind=kLoop, calls=%fused_computation.5 | loop fusion | flops 524288 | bytes 524288 | tf_op jit(solution)/shard_map/concatenate | solution.py:502
  (5 shorter events, 0.1 us)
Async XLA Ops:
  1.0 16.1 %collective-permute-start.1 = (bf16[512,256]{1,0:T(8,128)(2,1)S(1)}, bf16[512,256]{1,0:T(8,128)(2,1)S(1)}, u32[]{:S(2)}, u32[]{:S(2)}) collective-permute-start(bf16[512,256]{1,0:T(8,128)(2,1)S(1)} %own_states.1.refs_2_.refs_6_), channel_id=1, source_target_pairs={{0,8},{8,0},{4,12},{12,4},{1,9},{9,1},{5,13},{13,5},{2,10},{10,2},... | collective-permute-start | bytes 786440 | tf_op jit(solution)/shard_map/ppermute | solution.py:425
  5.1 12.6 %collective-permute-start = (bf16[512,256]{1,0:T(8,128)(2,1)S(1)}, bf16[512,256]{1,0:T(8,128)(2,1)S(1)}, u32[]{:S(2)}, u32[]{:S(2)}) collective-permute-start(bf16[512,256]{1,0:T(8,128)(2,1)S(1)} %own_states.1.refs_2_.refs_6_), channel_id=1, source_target_pairs={{0,4},{4,0},{8,12},{12,8},{1,5},{5,1},{9,13},{13,9},{2,6},{6,2},{1... | collective-permute-start | bytes 786440 | tf_op jit(solution)/shard_map/ppermute | solution.py:426
  7.9 10.9 %collective-permute-start.2 = (bf16[1568,128]{1,0:T(8,128)(2,1)S(1)}, bf16[1568,128]{1,0:T(8,128)(2,1)S(1)}, u32[]{:S(2)}, u32[]{:S(2)}) collective-permute-start(bf16[1568,128]{1,0:T(8,128)(2,1)S(1)} %pack_operators.1.refs_1_.refs_0_.refs_2_), channel_id=1, source_target_pairs={{0,2},{2,0},{1,3},{3,1},{4,6},{6,4},{5,7},{7,5},{8,10},{10,8},{9,1... | collective-permute-start | bytes 1204232 | tf_op jit(solution)/shard_map/ppermute | solution.py:427
  9.4 9.4 %collective-permute-start.3 = (bf16[1568,128]{1,0:T(8,128)(2,1)S(1)}, bf16[1568,128]{1,0:T(8,128)(2,1)S(1)}, u32[]{:S(2)}, u32[]{:S(2)}) collective-permute-start(bf16[1568,128]{1,0:T(8,128)(2,1)S(1)} %pack_operators.1.refs_1_.refs_0_.refs_2_), channel_id=1, source_target_pairs={{0,1},{1,0},{2,3},{3,2},{4,5},{5,4},{6,7},{7,6},{8,9},{9,8},{10,11... | collective-permute-start | bytes 1204232 | tf_op jit(solution)/shard_map/ppermute | solution.py:360
  17.1 7.4 %collective-permute-start.5 = (bf16[512,256]{1,0:T(8,128)(2,1)S(1)}, bf16[512,256]{1,0:T(8,128)(2,1)S(1)}, u32[]{:S(2)}, u32[]{:S(2)}) collective-permute-start(bf16[512,256]{1,0:T(8,128)(2,1)S(1)} %collective-permute-done.1.refs_4_.refs_8_), channel_id=1, source_target_pairs={{0,4},{4,0},{8,12},{12,8},{1,5},{5,1},{9,13},{13,9},{2,6},{6,2},{1... | collective-permute-start | bytes 786440 | tf_op jit(solution)/shard_map/ppermute | solution.py:438
  18.8 1.9 %collective-permute-start.4 = (bf16[1568,128]{1,0:T(8,128)(2,1)S(1)}, bf16[1568,128]{1,0:T(8,128)(2,1)S(1)}, u32[]{:S(2)}, u32[]{:S(2)}) collective-permute-start(bf16[1568,128]{1,0:T(8,128)(2,1)S(1)} %collective-permute-done.2.refs_4_), channel_id=1, source_target_pairs={{0,1},{1,0},{2,3},{3,2},{4,5},{5,4},{6,7},{7,6},{8,9},{9,8},{10,11... | collective-permute-start | bytes 1204232 | tf_op jit(solution)/shard_map/ppermute | solution.py:360
  25.8 1.4 %collective-permute-start.9 = (bf16[64,1024]{1,0:T(8,128)(2,1)S(1)}, bf16[64,1024]{1,0:T(8,128)(2,1)S(1)}, u32[]{:S(2)}, u32[]{:S(2)}) collective-permute-start(bf16[64,1024]{1,0:T(8,128)(2,1)S(1)} %get-tuple-element.58), channel_id=1, source_target_pairs={{0,1},{1,0},{2,3},{3,2},{4,5},{5,4},{6,7},{7,6},{8,9},{9,8},{10,11... | collective-permute-start | bytes 393224 | tf_op jit(solution)/shard_map/ppermute | solution.py:360
  26.2 2.3 %collective-permute-start.7 = (bf16[64,1024]{1,0:T(8,128)(2,1)S(1)}, bf16[64,1024]{1,0:T(8,128)(2,1)S(1)}, u32[]{:S(2)}, u32[]{:S(2)}) collective-permute-start(bf16[64,1024]{1,0:T(8,128)(2,1)S(1)} %get-tuple-element.56), channel_id=1, source_target_pairs={{0,1},{1,0},{2,3},{3,2},{4,5},{5,4},{6,7},{7,6},{8,9},{9,8},{10,11... | collective-permute-start | bytes 393224 | tf_op jit(solution)/shard_map/ppermute | solution.py:360
  26.8 2.6 %collective-permute-start.6 = (bf16[128,1024]{1,0:T(8,128)(2,1)S(1)}, bf16[128,1024]{1,0:T(8,128)(2,1)S(1)}, u32[]{:S(2)}, u32[]{:S(2)}) collective-permute-start(bf16[128,1024]{1,0:T(8,128)(2,1)S(1)} %get-tuple-element.54), channel_id=1, source_target_pairs={{0,1},{1,0},{2,3},{3,2},{4,5},{5,4},{6,7},{7,6},{8,9},{9,8},{10,11... | collective-permute-start | bytes 786440 | tf_op jit(solution)/shard_map/ppermute | solution.py:360
  27.2 6.4 %collective-permute-start.10 = (bf16[64,1024]{1,0:T(8,128)(2,1)S(1)}, bf16[64,1024]{1,0:T(8,128)(2,1)S(1)}, u32[]{:S(2)}, u32[]{:S(2)}) collective-permute-start(bf16[64,1024]{1,0:T(8,128)(2,1)S(1)} %add_convert_fusion), channel_id=1, source_target_pairs={{0,2},{2,0},{1,3},{3,1},{4,6},{6,4},{5,7},{7,5},{8,10},{10,8},{9,1... | collective-permute-start | bytes 393224 | tf_op jit(solution)/shard_map/ppermute | solution.py:495
  28.6 7.1 %collective-permute-start.8 = (bf16[64,1024]{1,0:T(8,128)(2,1)S(1)}, bf16[64,1024]{1,0:T(8,128)(2,1)S(1)}, u32[]{:S(2)}, u32[]{:S(2)}) collective-permute-start(bf16[64,1024]{1,0:T(8,128)(2,1)S(1)} %add_convert_fusion.1), channel_id=1, source_target_pairs={{0,2},{2,0},{1,3},{3,1},{4,6},{6,4},{5,7},{7,5},{8,10},{10,8},{9,1... | collective-permute-start | bytes 393224 | tf_op jit(solution)/shard_map/ppermute | solution.py:495
